TPU v7x, 32 devices: a whole 2x2x4 slice. The times are simulated.
32 devices in a mesh: section: 8 (over z, core), expert: 4 (over y, x).
Axes of the slice: x: 2, y: 2, z: 4, core: 2. Of those that a mesh axis runs over, the one named last changes fastest.
Arguments:
- left_in: bfloat16 [8, 256, 2048], P('section', 'expert'), may hold values from -6 to 6
- left_new: bfloat16 [256, 2048], P('expert'), may hold values from -6 to 6
- left_saved: bfloat16 [8, 256, 2048], P('section', 'expert'), may hold values from -6 to 6
- left_cot: bfloat16 [8, 256, 2048], P('section', 'expert'), may hold values from -6 to 6
- right_in: bfloat16 [8, 256, 2048], P('section', 'expert'), may hold values from -6 to 6
- right_saved: bfloat16 [2, 8, 256, 2048], P(None, 'section', 'expert'), may hold values from -6 to 6
- right_cot: bfloat16 [8, 256, 2048], P('section', 'expert'), may hold values from -6 to 6
- right_cot_new: bfloat16 [256, 2048], P('expert'), may hold values from -6 to 6
- expert_ids: int32 [3, 2, 8, 256, 1], P(None, None, 'section', 'expert'), may hold values from 0 to 1; in each aligned block of 64 rows (0 to 63, 64 to 127, ..., all dimensions but the last counted through in order) at most 34 rows name the same one
- gate_values: float32 [3, 2, 8, 256, 1], P(None, None, 'section', 'expert'), may hold values from 0.25 to 1
- w_gate: bfloat16 [8, 4, 2048, 384], P('section', 'expert'), may hold values from -0.125 to 0.125
- w_up: bfloat16 [8, 4, 2048, 384], P('section', 'expert'), may hold values from -0.125 to 0.125
- w_down: bfloat16 [8, 4, 384, 2048], P('section', 'expert'), may hold values from -0.21875 to 0.21875
Outputs:
- left_out: bfloat16 [2, 8, 256, 2048], P(None, 'section', 'expert')
- right_out: bfloat16 [8, 256, 2048], P('section', 'expert')
- left_back: bfloat16 [8, 256, 2048], P('section', 'expert')
- right_back: bfloat16 [2, 8, 256, 2048], P(None, 'section', 'expert')
- grad_gate: bfloat16 [8, 4, 2048, 384], P('section', 'expert')
- grad_up: bfloat16 [8, 4, 2048, 384], P('section', 'expert')
- grad_down: bfloat16 [8, 4, 384, 2048], P('section', 'expert')
Inputs may be any that keep to these rules, and one draw needn't show every extreme that they name: `expert_ids`: each row names one expert. In each aligned block of 64 rows (one device's tokens in one pass) no expert is named by more than 34 rows, and in some blocks one expert is named by exactly 34 rows.
All inputs are finite; a program needn't handle non-finite values.
Results may differ from a plain program's by a relative error of at most 0.0064.
Values may be sent and summed in bfloat16 or wider, within the bound.
No kernel may reach another device: no remote copies, remote signals or barrier semaphores. Data moves between devices by JAX's collectives and lax.ppermute only.
A program may use at most 128 MiB of HBM per device.

v0:
```python
import jax
import jax.numpy as jnp
from jax import lax
from jax.sharding import PartitionSpec as P

HIGHEST = lax.Precision.HIGHEST


def swapped(block, axis, stride):
    count = lax.axis_size(axis)
    route = []
    for low in range(count):
        high = low | 1 << stride
        if high != low and high < count:
            route += [(low, high), (high, low)]
    return lax.ppermute(block, axis, route)


def passed_along(value, axis, by):
    peers = lax.axis_size(axis)
    pairs = [(i, i + by) for i in range(peers) if 0 <= i + by < peers]
    return lax.ppermute(value, axis, pairs)


def route_tables(ids_block, gates_block, experts, capacity):
    token_count = ids_block.shape[0]
    top_count = ids_block.shape[1]
    flat_ids = ids_block.reshape(-1)
    onehot = (flat_ids[:, None] == jnp.arange(experts, dtype=jnp.int32)[None, :]).astype(jnp.int32)
    before = jnp.cumsum(onehot, axis=0) - onehot
    position = jnp.sum(before * onehot, axis=1)
    target = (flat_ids * capacity + position).reshape(token_count, top_count)
    slot_ids = jnp.arange(experts * capacity, dtype=jnp.int32)
    matches = target[None, :, :] == slot_ids[:, None, None]
    placement = jnp.sum(matches.astype(jnp.float32), axis=2)
    weighting = jnp.sum(
        jnp.where(matches, gates_block[None, :, :], jnp.zeros_like(gates_block)[None]), axis=2
    )
    return (placement, weighting)


def expert_forward(expert_rows, gate_half, up_half, down_half):
    gate_act = jnp.dot(expert_rows, gate_half, preferred_element_type=jnp.float32)
    up_act = jnp.dot(expert_rows, up_half, preferred_element_type=jnp.float32)
    hidden = (gate_act * jax.nn.sigmoid(gate_act) * up_act).astype(jnp.bfloat16)
    return jnp.dot(hidden, down_half, preferred_element_type=jnp.float32)


def expert_backward(expert_rows, row_cot, gate_half, up_half, down_half):
    gate_act = jnp.dot(expert_rows, gate_half, preferred_element_type=jnp.float32)
    up_act = jnp.dot(expert_rows, up_half, preferred_element_type=jnp.float32)
    logistic = jax.nn.sigmoid(gate_act)
    swish = gate_act * logistic
    hidden = (swish * up_act).astype(jnp.bfloat16)
    d_hidden = jnp.dot(row_cot, down_half.T, preferred_element_type=jnp.float32)
    d_gate = (d_hidden * up_act * logistic * (1.0 + gate_act * (1.0 - logistic))).astype(
        jnp.bfloat16
    )
    d_up = (d_hidden * swish).astype(jnp.bfloat16)
    grad_down = jnp.dot(hidden.T, row_cot, preferred_element_type=jnp.float32)
    grad_gate = jnp.dot(expert_rows.T, d_gate, preferred_element_type=jnp.float32)
    grad_up = jnp.dot(expert_rows.T, d_up, preferred_element_type=jnp.float32)
    backward_rows = jnp.dot(d_gate, gate_half.T, preferred_element_type=jnp.float32) + jnp.dot(
        d_up, up_half.T, preferred_element_type=jnp.float32
    )
    return (backward_rows, (grad_gate, grad_up, grad_down))


def pair_total(paired):
    return (paired[:, 0].astype(jnp.float32) + paired[:, 1].astype(jnp.float32)).astype(
        jnp.bfloat16
    )


def layer_forward(tokens, ids_block, gates_block, weights, layout):
    experts, capacity = layout
    gate_half, up_half, down_half = weights
    model_width = tokens.shape[1]
    devices = 2 * experts
    placement, weighting = route_tables(ids_block, gates_block, experts, capacity)
    routed = jnp.dot(
        placement.astype(jnp.bfloat16), tokens, preferred_element_type=jnp.float32
    ).astype(jnp.bfloat16)
    outgoing = jnp.repeat(routed.reshape(experts, capacity, model_width), 2, axis=0)
    received = lax.all_to_all(outgoing, "expert", split_axis=0, concat_axis=0, tiled=True)
    item_count = received.shape[1]
    result = expert_forward(
        received.reshape(devices * item_count, model_width), gate_half, up_half, down_half
    )
    partial_out = result.astype(jnp.bfloat16).reshape(devices, item_count, model_width)
    returned = lax.all_to_all(partial_out, "expert", split_axis=0, concat_axis=0, tiled=True)
    expert_out = pair_total(returned.reshape(experts, 2, capacity, model_width))
    expert_out = expert_out.reshape(experts * capacity, model_width)
    mixed_out = tokens.astype(jnp.float32) + jnp.dot(
        weighting.T, expert_out.astype(jnp.float32), precision=HIGHEST
    )
    return mixed_out.astype(jnp.bfloat16)


def layer_backward(tokens, cotangent, ids_block, gates_block, weights, layout):
    experts, capacity = layout
    gate_half, up_half, down_half = weights
    model_width = tokens.shape[1]
    devices = 2 * experts
    placement, weighting = route_tables(ids_block, gates_block, experts, capacity)
    placement_bf = placement.astype(jnp.bfloat16)
    routed = jnp.dot(placement_bf, tokens, preferred_element_type=jnp.float32).astype(jnp.bfloat16)
    row_cot = jnp.dot(weighting, cotangent.astype(jnp.float32), precision=HIGHEST).astype(
        jnp.bfloat16
    )
    out_rows = jnp.repeat(routed.reshape(experts, capacity, model_width), 2, axis=0)
    out_cot = jnp.repeat(row_cot.reshape(experts, capacity, model_width), 2, axis=0)
    got_rows, got_cot = (
        lax.all_to_all(out_rows, "expert", split_axis=0, concat_axis=0, tiled=True),
        lax.all_to_all(out_cot, "expert", split_axis=0, concat_axis=0, tiled=True),
    )
    result, grads = expert_backward(
        got_rows.reshape(devices * capacity, model_width),
        got_cot.reshape(devices * capacity, model_width),
        gate_half,
        up_half,
        down_half,
    )
    returned = lax.all_to_all(
        result.astype(jnp.bfloat16).reshape(devices, capacity, model_width),
        "expert",
        split_axis=0,
        concat_axis=0,
        tiled=True,
    )
    expert_back = pair_total(returned.reshape(experts, 2, capacity, model_width))
    expert_back = expert_back.reshape(experts * capacity, model_width)
    new_cot = cotangent.astype(jnp.float32) + jnp.dot(
        placement_bf.T, expert_back, preferred_element_type=jnp.float32
    )
    return (new_cot.astype(jnp.bfloat16), grads)


def per_device(
    left_in,
    left_new,
    left_saved,
    left_cot,
    right_in,
    right_saved,
    right_cot,
    right_cot_new,
    expert_ids,
    gate_values,
    w_gate,
    w_up,
    w_down,
):
    tokens_dev = left_in.shape[1]
    top_count = expert_ids.shape[-1]
    experts = lax.axis_size("expert") // 2
    capacity = min(tokens_dev, 2 * ((tokens_dev * top_count // experts + 1) // 2) + 2)
    layout = (experts, capacity)
    weights = (w_gate[0, 0], w_up[0, 0], w_down[0, 0])
    section_index = lax.axis_index("section")
    section_count = lax.axis_size("section")
    mirrored = jnp.stack([right_in[0], right_saved[0, 0], right_saved[1, 0], right_cot[0]])
    for bit_index in range(section_count.bit_length() - 1):
        mirrored = swapped(mirrored, "section", bit_index)
    left_zero = layer_forward(
        left_in[0], expert_ids[0, 0, 0], gate_values[0, 0, 0], weights, layout
    )
    back_zero, grads_zero = layer_backward(
        mirrored[1], mirrored[3], expert_ids[0, 1, 0], gate_values[0, 1, 0], weights, layout
    )
    right_one = layer_forward(
        mirrored[0], expert_ids[1, 0, 0], gate_values[1, 0, 0], weights, layout
    )
    back_one, grads_one = layer_backward(
        left_saved[0], left_cot[0], expert_ids[1, 1, 0], gate_values[1, 1, 0], weights, layout
    )
    arriving = passed_along(left_zero, "section", 1)
    left_input = jnp.where(section_index == 0, left_new, arriving)
    left_two = layer_forward(left_input, expert_ids[2, 0, 0], gate_values[2, 0, 0], weights, layout)
    returning = passed_along(back_zero, "section", -1)
    cot_input = jnp.where(section_index == section_count - 1, right_cot_new, returning)
    back_two, grads_two = layer_backward(
        mirrored[2], cot_input, expert_ids[2, 1, 0], gate_values[2, 1, 0], weights, layout
    )
    grad_gate = (grads_zero[0] + grads_one[0] + grads_two[0]).astype(jnp.bfloat16)
    grad_up = (grads_zero[1] + grads_one[1] + grads_two[1]).astype(jnp.bfloat16)
    grad_down = (grads_zero[2] + grads_one[2] + grads_two[2]).astype(jnp.bfloat16)
    left_out = jnp.stack([left_zero, left_two])[:, None]
    right_back = jnp.stack([back_zero, back_two])[:, None]
    return (
        left_out,
        right_one[None],
        back_one[None],
        right_back,
        grad_gate[None, None],
        grad_up[None, None],
        grad_down[None, None],
    )


def solution(mesh):
    in_specs = (
        P("section", "expert", None),
        P("expert", None),
        P("section", "expert", None),
        P("section", "expert", None),
        P("section", "expert", None),
        P(None, "section", "expert", None),
        P("section", "expert", None),
        P("expert", None),
        P(None, None, "section", "expert", None),
        P(None, None, "section", "expert", None),
        P("section", "expert", None, None),
        P("section", "expert", None, None),
        P("section", "expert", None, None),
    )
    out_specs = (
        P(None, "section", "expert", None),
        P("section", "expert", None),
        P("section", "expert", None),
        P(None, "section", "expert", None),
        P("section", "expert", None, None),
        P("section", "expert", None, None),
        P("section", "expert", None, None),
    )
    return jax.shard_map(
        per_device, mesh=mesh, in_specs=in_specs, out_specs=out_specs, check_vma=False
    )
```

profile of v0, /device:TPU:10, one launch (start us, length us, event | category | flops | bytes accessed | tf_op | source)
XLA Modules:
  0.0 291.4 jit_solution(3633031688286923479)
XLA Ops:
  7.0 4.7 %all-to-all-start = ((bf16[4,34,2048]{2,1,0:T(8,128)(2,1)}), bf16[4,34,2048]{2,1,0:T(8,128)(2,1)}, u32[]{:S(2)}, u32[]{:S(2)}) async-start(bf16[4,34,2048]{2,1,0:T(8,128)(2,1)} %bitcast.5), calls=%async_computation | async-start | bytes 1310720 | tf_op jit(solution)/shard_map/all_to_all | solution.py:85
  13.4 8.1 %all-to-all-done = bf16[4,34,2048]{2,1,0:T(8,128)(2,1)} async-done(((bf16[4,34,2048]{2,1,0:T(8,128)(2,1)}), bf16[4,34,2048]{2,1,0:T(8,128)(2,1)}, u32[]{:S(2)}, u32[]{:S(2)}) %all-to-all-start) | async-done | bytes 557088 | tf_op jit(solution)/shard_map/all_to_all | solution.py:85
  23.4 4.8 %all-to-all-start.7 = ((bf16[4,34,2048]{2,1,0:T(8,128)(2,1)}), bf16[4,34,2048]{2,1,0:T(8,128)(2,1)}, u32[]{:S(2)}, u32[]{:S(2)}) async-start(bf16[4,34,2048]{2,1,0:T(8,128)(2,1)} %bitcast.330), calls=%async_computation.7 | async-start | bytes 1310720 | tf_op jit(solution)/shard_map/all_to_all | solution.py:114
  32.4 3.4 %convolution_convert_fusion.2 = bf16[136,2048]{1,0:T(8,128)(2,1)} fusion(bf16[1,1,384,2048]{3,2,1,0:T(8,128)(2,1)} %param.25, bf16[136,2048]{1,0:T(8,128)(2,1)} %reshape.953, bf16[1,1,2048,384]{3,2,1,0:T(8,128)(2,1)S(1)} %copy-done, f32[136,384]{1,0:T(8,128)} %fusion.49), kind=kOutput, calls=%fused_computation.14 | convolution fusion | flops 428410880 | bytes 4468736 | tf_op jit(solution)/shard_map/dot_general | solution.py:46
  38.2 4.7 %all-to-all-start.6 = ((bf16[4,34,2048]{2,1,0:T(8,128)(2,1)}), bf16[4,34,2048]{2,1,0:T(8,128)(2,1)}, u32[]{:S(2)}, u32[]{:S(2)}) async-start(bf16[4,34,2048]{2,1,0:T(8,128)(2,1)} %bitcast.331), calls=%async_computation.6 | async-start | bytes 1310720 | tf_op jit(solution)/shard_map/all_to_all | solution.py:115
  51.3 4.7 %all-to-all-start.1 = ((bf16[4,34,2048]{2,1,0:T(8,128)(2,1)}), bf16[4,34,2048]{2,1,0:T(8,128)(2,1)}, u32[]{:S(2)}, u32[]{:S(2)}) async-start(bf16[4,34,2048]{2,1,0:T(8,128)(2,1)} %reshape.954), calls=%async_computation.1 | async-start | bytes 1310720 | tf_op jit(solution)/shard_map/all_to_all | solution.py:91
  80.2 4.2 %all-to-all-start.2 = ((bf16[4,34,2048]{2,1,0:T(8,128)(2,1)}), bf16[4,34,2048]{2,1,0:T(8,128)(2,1)}, u32[]{:S(2)}, u32[]{:S(2)}) async-start(bf16[4,34,2048]{2,1,0:T(8,128)(2,1)} %bitcast.327), calls=%async_computation.2 | async-start | bytes 1310720 | tf_op jit(solution)/shard_map/all_to_all | solution.py:85
  89.4 3.5 %fusion.100 = f32[384,2048]{1,0:T(8,128)} fusion(bf16[136,2048]{1,0:T(8,128)(2,1)} %reshape.968, f32[136,384]{1,0:T(8,128)S(1)} %copy-done.23, f32[136,384]{1,0:T(8,128)} %fusion.43), kind=kOutput, calls=%fused_computation.147 | convolution fusion | flops 214222848 | bytes 4120576 | tf_op jit(solution)/shard_map/dot_general | solution.py:60
  93.2 4.7 %all-to-all-start.8 = ((bf16[4,34,2048]{2,1,0:T(8,128)(2,1)}), bf16[4,34,2048]{2,1,0:T(8,128)(2,1)}, u32[]{:S(2)}, u32[]{:S(2)}) async-start(bf16[4,34,2048]{2,1,0:T(8,128)(2,1)} %reshape.972), calls=%async_computation.8 | async-start | bytes 1310720 | tf_op jit(solution)/shard_map/all_to_all | solution.py:124
  109.0 4.4 %all-to-all-start.3 = ((bf16[4,34,2048]{2,1,0:T(8,128)(2,1)}), bf16[4,34,2048]{2,1,0:T(8,128)(2,1)}, u32[]{:S(2)}, u32[]{:S(2)}) async-start(bf16[4,34,2048]{2,1,0:T(8,128)(2,1)} %reshape.959), calls=%async_computation.3 | async-start | bytes 1310720 | tf_op jit(solution)/shard_map/all_to_all | solution.py:91
  117.3 3.8 %all-to-all-done.3 = bf16[4,34,2048]{2,1,0:T(8,128)(2,1)} async-done(((bf16[4,34,2048]{2,1,0:T(8,128)(2,1)}), bf16[4,34,2048]{2,1,0:T(8,128)(2,1)}, u32[]{:S(2)}, u32[]{:S(2)}) %all-to-all-start.3) | async-done | bytes 557088 | tf_op jit(solution)/shard_map/all_to_all | solution.py:91
  126.2 26.5 %collective-permute-done.3 = bf16[4,64,2048]{2,1,0:T(8,128)(2,1)} collective-permute-done((bf16[4,64,2048]{2,1,0:T(8,128)(2,1)}, bf16[4,64,2048]{2,1,0:T(8,128)(2,1)}, u32[]{:S(2)}, u32[]{:S(2)}) %collective-permute-start.3) | collective-permute-done | bytes 1048608 | tf_op jit(solution)/shard_map/ppermute | solution.py:16
  158.9 4.4 %all-to-all-start.10 = ((bf16[4,34,2048]{2,1,0:T(8,128)(2,1)}), bf16[4,34,2048]{2,1,0:T(8,128)(2,1)}, u32[]{:S(2)}, u32[]{:S(2)}) async-start(bf16[4,34,2048]{2,1,0:T(8,128)(2,1)} %bitcast.329), calls=%async_computation.10 | async-start | bytes 1310720 | tf_op jit(solution)/shard_map/all_to_all | solution.py:114
  173.8 4.7 %all-to-all-start.9 = ((bf16[4,34,2048]{2,1,0:T(8,128)(2,1)}), bf16[4,34,2048]{2,1,0:T(8,128)(2,1)}, u32[]{:S(2)}, u32[]{:S(2)}) async-start(bf16[4,34,2048]{2,1,0:T(8,128)(2,1)} %bitcast.332), calls=%async_computation.9 | async-start | bytes 1310720 | tf_op jit(solution)/shard_map/all_to_all | solution.py:115
  188.7 4.7 %all-to-all-start.4 = ((bf16[4,34,2048]{2,1,0:T(8,128)(2,1)}), bf16[4,34,2048]{2,1,0:T(8,128)(2,1)}, u32[]{:S(2)}, u32[]{:S(2)}) async-start(bf16[4,34,2048]{2,1,0:T(8,128)(2,1)} %bitcast.325), calls=%async_computation.4 | async-start | bytes 1310720 | tf_op jit(solution)/shard_map/all_to_all | solution.py:85
  206.2 4.2 %all-to-all-start.13 = ((bf16[4,34,2048]{2,1,0:T(8,128)(2,1)}), bf16[4,34,2048]{2,1,0:T(8,128)(2,1)}, u32[]{:S(2)}, u32[]{:S(2)}) async-start(bf16[4,34,2048]{2,1,0:T(8,128)(2,1)} %bitcast.328), calls=%async_computation.13 | async-start | bytes 1310720 | tf_op jit(solution)/shard_map/all_to_all | solution.py:114
  219.3 4.2 %all-to-all-start.11 = ((bf16[4,34,2048]{2,1,0:T(8,128)(2,1)}), bf16[4,34,2048]{2,1,0:T(8,128)(2,1)}, u32[]{:S(2)}, u32[]{:S(2)}) async-start(bf16[4,34,2048]{2,1,0:T(8,128)(2,1)} %reshape.980), calls=%async_computation.11 | async-start | bytes 1310720 | tf_op jit(solution)/shard_map/all_to_all | solution.py:124
  229.8 3.5 %fusion.99 = f32[384,2048]{1,0:T(8,128)} fusion(bf16[136,2048]{1,0:T(8,128)(2,1)} %reshape.976, f32[136,384]{1,0:T(8,128)S(1)} %copy-done.24, f32[136,384]{1,0:T(8,128)} %fusion.39), kind=kOutput, calls=%fused_computation.146 | convolution fusion | flops 214222848 | bytes 4120576 | tf_op jit(solution)/shard_map/dot_general | solution.py:60
  233.3 4.2 %all-to-all-start.5 = ((bf16[4,34,2048]{2,1,0:T(8,128)(2,1)}), bf16[4,34,2048]{2,1,0:T(8,128)(2,1)}, u32[]{:S(2)}, u32[]{:S(2)}) async-start(bf16[4,34,2048]{2,1,0:T(8,128)(2,1)} %reshape.964), calls=%async_computation.5 | async-start | bytes 1310720 | tf_op jit(solution)/shard_map/all_to_all | solution.py:91
  240.8 4.1 %collective-permute-start.4 = (bf16[64,2048]{1,0:T(8,128)(2,1)S(1)}, bf16[64,2048]{1,0:T(8,128)(2,1)S(1)}, u32[]{:S(2)}, u32[]{:S(2)}) collective-permute-start(bf16[64,2048]{1,0:T(8,128)(2,1)S(1)} %add_convert_fusion.10), channel_id=1, source_target_pairs={{4,0},{8,4},{12,8},{16,12},{20,16},{24,20},{28,24},{5,1},{9,5},{13... | collective-permute-start | bytes 786440 | tf_op jit(solution)/shard_map/ppermute | solution.py:22
  252.6 4.4 %all-to-all-start.12 = ((bf16[4,34,2048]{2,1,0:T(8,128)(2,1)}), bf16[4,34,2048]{2,1,0:T(8,128)(2,1)}, u32[]{:S(2)}, u32[]{:S(2)}) async-start(bf16[4,34,2048]{2,1,0:T(8,128)(2,1)} %bitcast.326), calls=%async_computation.12 | async-start | bytes 1310720 | tf_op jit(solution)/shard_map/all_to_all | solution.py:115
  261.2 5.8 %all-to-all-done.12 = bf16[4,34,2048]{2,1,0:T(8,128)(2,1)} async-done(((bf16[4,34,2048]{2,1,0:T(8,128)(2,1)}), bf16[4,34,2048]{2,1,0:T(8,128)(2,1)}, u32[]{:S(2)}, u32[]{:S(2)}) %all-to-all-start.12) | async-done | bytes 557088 | tf_op jit(solution)/shard_map/all_to_all | solution.py:115
  273.9 4.1 %all-to-all-start.14 = ((bf16[4,34,2048]{2,1,0:T(8,128)(2,1)}), bf16[4,34,2048]{2,1,0:T(8,128)(2,1)S(1)}, u32[]{:S(2)}, u32[]{:S(2)}) async-start(bf16[4,34,2048]{2,1,0:T(8,128)(2,1)} %reshape.988), calls=%async_computation.14 | async-start | bytes 1310720 | tf_op jit(solution)/shard_map/all_to_all | solution.py:124
  278.0 4.9 %fusion.1 = bf16[1,1,2048,384]{3,2,1,0:T(8,128)(2,1)} fusion(bf16[136,2048]{1,0:T(8,128)(2,1)S(1)} %copy-done.2, bf16[136,384]{1,0:T(8,128)(2,1)S(1)} %copy-done.27, f32[2048,384]{1,0:T(8,128)} %fusion.190, f32[2048,384]{1,0:T(8,128)} %fusion.191), kind=kOutput, calls=%fused_computation.4 | convolution fusion | flops 216268800 | bytes 8525824 | tf_op jit(solution)/shard_map/dot_general | solution.py:62
  (194 shorter events, 159.6 us)
Async XLA Ops:
  0.6 31.8 %copy-start = (bf16[1,1,2048,384]{3,2,1,0:T(8,128)(2,1)S(1)}, bf16[1,1,2048,384]{3,2,1,0:T(8,128)(2,1)}, u32[]{:S(2)}) copy-start(bf16[1,1,2048,384]{3,2,1,0:T(8,128)(2,1)} %param.24) | copy-start | bytes 4718596
  4.0 69.5 %collective-permute-start.1 = (bf16[4,64,2048]{2,1,0:T(8,128)(2,1)}, bf16[4,64,2048]{2,1,0:T(8,128)(2,1)}, u32[]{:S(2)}, u32[]{:S(2)}) collective-permute-start(bf16[4,64,2048]{2,1,0:T(8,128)(2,1)} %pad_maximum_fusion), channel_id=1, source_target_pairs={{0,4},{4,0},{8,12},{12,8},{16,20},{20,16},{24,28},{28,24},{1,5},{5... | collective-permute-start | bytes 3145736 | tf_op jit(solution)/shard_map/ppermute | solution.py:16
  7.0 14.5 %all-to-all-start = ((bf16[4,34,2048]{2,1,0:T(8,128)(2,1)}), bf16[4,34,2048]{2,1,0:T(8,128)(2,1)}, u32[]{:S(2)}, u32[]{:S(2)}) async-start(bf16[4,34,2048]{2,1,0:T(8,128)(2,1)} %bitcast.5), calls=%async_computation | async-start | bytes 1310720 | tf_op jit(solution)/shard_map/all_to_all | solution.py:85
  13.4 16.8 %copy-start.1 = (bf16[1,1,2048,384]{3,2,1,0:T(8,128)(2,1)S(1)}, bf16[1,1,2048,384]{3,2,1,0:T(8,128)(2,1)}, u32[]{:S(2)}) copy-start(bf16[1,1,2048,384]{3,2,1,0:T(8,128)(2,1)} %param.23) | copy-start | bytes 4718596
  23.4 13.8 %all-to-all-start.7 = ((bf16[4,34,2048]{2,1,0:T(8,128)(2,1)}), bf16[4,34,2048]{2,1,0:T(8,128)(2,1)}, u32[]{:S(2)}, u32[]{:S(2)}) async-start(bf16[4,34,2048]{2,1,0:T(8,128)(2,1)} %bitcast.330), calls=%async_computation.7 | async-start | bytes 1310720 | tf_op jit(solution)/shard_map/all_to_all | solution.py:114
  38.2 13.1 %all-to-all-start.6 = ((bf16[4,34,2048]{2,1,0:T(8,128)(2,1)}), bf16[4,34,2048]{2,1,0:T(8,128)(2,1)}, u32[]{:S(2)}, u32[]{:S(2)}) async-start(bf16[4,34,2048]{2,1,0:T(8,128)(2,1)} %bitcast.331), calls=%async_computation.6 | async-start | bytes 1310720 | tf_op jit(solution)/shard_map/all_to_all | solution.py:115
  46.5 11.6 %copy-start.22 = (f32[136,384]{1,0:T(8,128)}, f32[136,384]{1,0:T(8,128)S(1)}, u32[]{:S(2)}) copy-start(f32[136,384]{1,0:T(8,128)S(1)} %fusion.25) | copy-start | bytes 626692
  51.3 14.0 %all-to-all-start.1 = ((bf16[4,34,2048]{2,1,0:T(8,128)(2,1)}), bf16[4,34,2048]{2,1,0:T(8,128)(2,1)}, u32[]{:S(2)}, u32[]{:S(2)}) async-start(bf16[4,34,2048]{2,1,0:T(8,128)(2,1)} %reshape.954), calls=%async_computation.1 | async-start | bytes 1310720 | tf_op jit(solution)/shard_map/all_to_all | solution.py:91
  68.8 7.8 %collective-permute-start = (bf16[64,2048]{1,0:T(8,128)(2,1)S(1)}, bf16[64,2048]{1,0:T(8,128)(2,1)S(1)}, u32[]{:S(2)}, u32[]{:S(2)}) collective-permute-start(bf16[64,2048]{1,0:T(8,128)(2,1)S(1)} %fusion.6), channel_id=1, source_target_pairs={{0,4},{4,8},{8,12},{12,16},{16,20},{20,24},{24,28},{1,5},{5,9},{9,... | collective-permute-start | bytes 786440 | tf_op jit(solution)/shard_map/ppermute | solution.py:22
  73.5 33.2 %collective-permute-start.2 = (bf16[4,64,2048]{2,1,0:T(8,128)(2,1)}, bf16[4,64,2048]{2,1,0:T(8,128)(2,1)}, u32[]{:S(2)}, u32[]{:S(2)}) collective-permute-start(bf16[4,64,2048]{2,1,0:T(8,128)(2,1)} %collective-permute-done.1), channel_id=1, source_target_pairs={{0,8},{8,0},{4,12},{12,4},{16,24},{24,16},{20,28},{28,20},{1,9},{9... | collective-permute-start | bytes 3145736 | tf_op jit(solution)/shard_map/ppermute | solution.py:16
  80.2 13.0 %all-to-all-start.2 = ((bf16[4,34,2048]{2,1,0:T(8,128)(2,1)}), bf16[4,34,2048]{2,1,0:T(8,128)(2,1)}, u32[]{:S(2)}, u32[]{:S(2)}) async-start(bf16[4,34,2048]{2,1,0:T(8,128)(2,1)} %bitcast.327), calls=%async_computation.2 | async-start | bytes 1310720 | tf_op jit(solution)/shard_map/all_to_all | solution.py:85
  93.2 15.8 %all-to-all-start.8 = ((bf16[4,34,2048]{2,1,0:T(8,128)(2,1)}), bf16[4,34,2048]{2,1,0:T(8,128)(2,1)}, u32[]{:S(2)}, u32[]{:S(2)}) async-start(bf16[4,34,2048]{2,1,0:T(8,128)(2,1)} %reshape.972), calls=%async_computation.8 | async-start | bytes 1310720 | tf_op jit(solution)/shard_map/all_to_all | solution.py:124
  106.8 45.9 %collective-permute-start.3 = (bf16[4,64,2048]{2,1,0:T(8,128)(2,1)}, bf16[4,64,2048]{2,1,0:T(8,128)(2,1)}, u32[]{:S(2)}, u32[]{:S(2)}) collective-permute-start(bf16[4,64,2048]{2,1,0:T(8,128)(2,1)} %collective-permute-done.2), channel_id=1, source_target_pairs={{0,16},{16,0},{4,20},{20,4},{8,24},{24,8},{12,28},{28,12},{1,17},{... | collective-permute-start | bytes 3145736 | tf_op jit(solution)/shard_map/ppermute | solution.py:16
  109.0 12.1 %all-to-all-start.3 = ((bf16[4,34,2048]{2,1,0:T(8,128)(2,1)}), bf16[4,34,2048]{2,1,0:T(8,128)(2,1)}, u32[]{:S(2)}, u32[]{:S(2)}) async-start(bf16[4,34,2048]{2,1,0:T(8,128)(2,1)} %reshape.959), calls=%async_computation.3 | async-start | bytes 1310720 | tf_op jit(solution)/shard_map/all_to_all | solution.py:91
  158.9 13.1 %all-to-all-start.10 = ((bf16[4,34,2048]{2,1,0:T(8,128)(2,1)}), bf16[4,34,2048]{2,1,0:T(8,128)(2,1)}, u32[]{:S(2)}, u32[]{:S(2)}) async-start(bf16[4,34,2048]{2,1,0:T(8,128)(2,1)} %bitcast.329), calls=%async_computation.10 | async-start | bytes 1310720 | tf_op jit(solution)/shard_map/all_to_all | solution.py:114
  173.8 13.0 %all-to-all-start.9 = ((bf16[4,34,2048]{2,1,0:T(8,128)(2,1)}), bf16[4,34,2048]{2,1,0:T(8,128)(2,1)}, u32[]{:S(2)}, u32[]{:S(2)}) async-start(bf16[4,34,2048]{2,1,0:T(8,128)(2,1)} %bitcast.332), calls=%async_computation.9 | async-start | bytes 1310720 | tf_op jit(solution)/shard_map/all_to_all | solution.py:115
  188.7 16.6 %all-to-all-start.4 = ((bf16[4,34,2048]{2,1,0:T(8,128)(2,1)}), bf16[4,34,2048]{2,1,0:T(8,128)(2,1)}, u32[]{:S(2)}, u32[]{:S(2)}) async-start(bf16[4,34,2048]{2,1,0:T(8,128)(2,1)} %bitcast.325), calls=%async_computation.4 | async-start | bytes 1310720 | tf_op jit(solution)/shard_map/all_to_all | solution.py:85
  206.2 13.1 %all-to-all-start.13 = ((bf16[4,34,2048]{2,1,0:T(8,128)(2,1)}), bf16[4,34,2048]{2,1,0:T(8,128)(2,1)}, u32[]{:S(2)}, u32[]{:S(2)}) async-start(bf16[4,34,2048]{2,1,0:T(8,128)(2,1)} %bitcast.328), calls=%async_computation.13 | async-start | bytes 1310720 | tf_op jit(solution)/shard_map/all_to_all | solution.py:114
  219.3 14.0 %all-to-all-start.11 = ((bf16[4,34,2048]{2,1,0:T(8,128)(2,1)}), bf16[4,34,2048]{2,1,0:T(8,128)(2,1)}, u32[]{:S(2)}, u32[]{:S(2)}) async-start(bf16[4,34,2048]{2,1,0:T(8,128)(2,1)} %reshape.980), calls=%async_computation.11 | async-start | bytes 1310720 | tf_op jit(solution)/shard_map/all_to_all | solution.py:124
  233.3 18.4 %all-to-all-start.5 = ((bf16[4,34,2048]{2,1,0:T(8,128)(2,1)}), bf16[4,34,2048]{2,1,0:T(8,128)(2,1)}, u32[]{:S(2)}, u32[]{:S(2)}) async-start(bf16[4,34,2048]{2,1,0:T(8,128)(2,1)} %reshape.964), calls=%async_computation.5 | async-start | bytes 1310720 | tf_op jit(solution)/shard_map/all_to_all | solution.py:91
  239.5 10.1 %copy-start.12 = (bf16[64,2048]{1,0:T(8,128)(2,1)S(1)}, bf16[64,2048]{1,0:T(8,128)(2,1)}, u32[]{:S(2)}) copy-start(bf16[64,2048]{1,0:T(8,128)(2,1)} %param.20) | copy-start | bytes 786436
  240.8 8.0 %collective-permute-start.4 = (bf16[64,2048]{1,0:T(8,128)(2,1)S(1)}, bf16[64,2048]{1,0:T(8,128)(2,1)S(1)}, u32[]{:S(2)}, u32[]{:S(2)}) collective-permute-start(bf16[64,2048]{1,0:T(8,128)(2,1)S(1)} %add_convert_fusion.10), channel_id=1, source_target_pairs={{4,0},{8,4},{12,8},{16,12},{20,16},{24,20},{28,24},{5,1},{9,5},{13... | collective-permute-start | bytes 786440 | tf_op jit(solution)/shard_map/ppermute | solution.py:22
  252.6 14.4 %all-to-all-start.12 = ((bf16[4,34,2048]{2,1,0:T(8,128)(2,1)}), bf16[4,34,2048]{2,1,0:T(8,128)(2,1)}, u32[]{:S(2)}, u32[]{:S(2)}) async-start(bf16[4,34,2048]{2,1,0:T(8,128)(2,1)} %bitcast.326), calls=%async_computation.12 | async-start | bytes 1310720 | tf_op jit(solution)/shard_map/all_to_all | solution.py:115
  273.9 14.4 %all-to-all-start.14 = ((bf16[4,34,2048]{2,1,0:T(8,128)(2,1)}), bf16[4,34,2048]{2,1,0:T(8,128)(2,1)S(1)}, u32[]{:S(2)}, u32[]{:S(2)}) async-start(bf16[4,34,2048]{2,1,0:T(8,128)(2,1)} %reshape.988), calls=%async_computation.14 | async-start | bytes 1310720 | tf_op jit(solution)/shard_map/all_to_all | solution.py:124
  (29 other events, 115.9 us)
where the time goes:
time: 294 us; the launch traced here: 291 us
  matrix products  87.9 us (30%)
  starting transfers between devices  75.4 us (26%)
  local copies, waits for them, and re-layouts  57.8 us (20%)
  waiting for transfers between devices  55.9 us (19%)
  other arithmetic  13.2 us (4%)
    ppermute x3, waiting for transfers between devices, swapped(): return lax.ppermute(block, axis, route)  26.5 us
    all_to_all x3, starting transfers between devices, layer_backward(): lax.all_to_all(out_cot, 'expert', split_axis=0, concat_axis=0, tiled=True)  13.9 us
    all_to_all x3, starting transfers between devices, layer_forward(): lax.all_to_all(outgoing, 'expert', split_axis=0, concat_axis=0, tiled=True)  13.6 us
    all_to_all x3, starting transfers between devices, layer_backward(): lax.all_to_all(out_rows, 'expert', split_axis=0, concat_axis=0, tiled=True)  13.4 us
    all_to_all x3, starting transfers between devices, layer_forward(): lax.all_to_all(partial_out, 'expert', split_axis=0, concat_axis=0, tiled=...  13.3 us
    all_to_all x3, starting transfers between devices, layer_backward(): lax.all_to_all(result.astype(jnp.bfloat16).reshape(devices, capacity, mod...  13 us
    dot_general x3, matrix products, expert_forward(): return jnp.dot(hidden, down_half, preferred_element_type=jnp.float32)  9.88 us
    dot_general x3, matrix products, expert_backward(): grad_up = jnp.dot(expert_rows.T, d_up, preferred_element_type=jnp.float32)  9.8 us
  transfers between devices with their start and end apart: 20, of which 11 were waited for; matrix products, arithmetic and copies ran while one was open for 45% of the time, Pallas kernels for 0%

commit v1 on v0

v1 whole, which is shorter than its diff:
```python
import functools

import jax
import jax.numpy as jnp
from jax import lax
from jax.experimental import pallas as pl
from jax.experimental.pallas import tpu as pltpu
from jax.sharding import PartitionSpec as P

LANES = 128
F32 = jnp.float32
BF16 = jnp.bfloat16
VMEM_LIMIT = 40 * 1024 * 1024


class Layout:
    def __init__(self, peers, tokens, width):
        self.peers = peers
        self.experts = peers // 2
        self.tokens = tokens
        self.width = width
        self.cap = min(tokens, 2 * ((tokens // self.experts + 1) // 2) + 2)
        self.main = self.cap // 8 * 8
        self.extra = self.cap - self.main
        self.slabs = width // LANES
        self.per_group = self.main // self.extra if self.extra else 1
        self.groups = -(-self.slabs // self.per_group) if self.extra else 0
        self.packed = width + self.groups * LANES
        self.slots = -(-(self.experts * self.cap) // 16) * 16
        self.rows = peers * self.cap
        self.rows_held = -(-self.rows // 16) * 16


def slab_place(lay, slab):
    group, at = divmod(slab, lay.per_group)
    return at * lay.extra, lay.width + group * LANES


def pack_extra(lay, rows, start, out_ref, lead, stage):
    if not lay.extra:
        return
    if lay.slabs % lay.per_group:
        stage[...] = jnp.zeros_like(stage)
    part = rows[start : start + lay.extra, :]
    for slab in range(lay.slabs):
        row, col = slab_place(lay, slab)
        stage[row : row + lay.extra, col - lay.width : col - lay.width + LANES] = part[
            :, slab * LANES : (slab + 1) * LANES
        ]
    out_ref[lead, :, lay.width :] = stage[...].astype(BF16)


def unpack_extra(lay, packed, stage, into, row_at):
    stage[...] = packed
    for slab in range(lay.slabs):
        row, col = slab_place(lay, slab)
        into[row_at : row_at + lay.extra, slab * LANES : (slab + 1) * LANES] = stage[
            row : row + lay.extra, col - lay.width : col - lay.width + LANES
        ]


def stacked_main(lay, blocks):
    if lay.main % 16:
        return jnp.concatenate([b.astype(F32) for b in blocks], axis=0).astype(BF16)
    return jnp.concatenate(blocks, axis=0)


def slot_onehot(lay, ids, own_expert):
    tokens = lay.tokens
    down = lax.broadcasted_iota(jnp.int32, (tokens, tokens), 0)
    across = lax.broadcasted_iota(jnp.int32, (tokens, tokens), 1)
    ids_row = jnp.sum(jnp.where(down == across, ids, 0), axis=0, keepdims=True)
    earlier = jnp.logical_and(ids == ids_row, down < across)
    rank = jnp.sum(earlier.astype(jnp.int32), axis=0, keepdims=True)
    near = ids_row ^ own_expert
    slot = jnp.where(
        rank < lay.main,
        near * lay.main + rank,
        lay.experts * lay.main + near * lay.extra + rank - lay.main,
    )
    place = lax.broadcasted_iota(jnp.int32, (lay.slots, tokens), 0)
    return (place == slot).astype(F32).astype(BF16)


def stage_shape(lay):
    return pltpu.VMEM((lay.main, max(1, lay.groups) * LANES), F32)


def route_kernel(lay, plan, *refs):
    scalars = refs[0]
    at = 1
    items = []
    for has_gates, has_choice in plan:
        item = {"tokens": refs[at], "ids": refs[at + 1]}
        at += 2
        if has_gates:
            item["gates"] = refs[at]
            at += 1
        if has_choice:
            item["fresh"] = refs[at]
            at += 1
        items.append(item)
    outs = refs[at : at + lay.experts]
    stage = refs[at + lay.experts]
    for lead, item in enumerate(items):
        tokens = item["tokens"][...]
        if "fresh" in item:
            tokens = jnp.where(scalars[1] == 1, item["fresh"][...], tokens)
        if "gates" in item:
            tokens = (item["gates"][...] * tokens.astype(F32)).astype(BF16)
        onehot = slot_onehot(lay, item["ids"][...], scalars[0])
        rows = jnp.dot(onehot, tokens, preferred_element_type=F32)
        for j, out in enumerate(outs):
            out[lead, :, : lay.width] = rows[j * lay.main : (j + 1) * lay.main].astype(BF16)
            pack_extra(lay, rows, lay.experts * lay.main + j * lay.extra, out, lead, stage)


VMEM_SPEC = pl.BlockSpec(memory_space=pltpu.VMEM)
SMEM_SPEC = pl.BlockSpec(memory_space=pltpu.SMEM)


def cost(flops, arrays):
    moved = sum(a.size * a.dtype.itemsize for a in arrays)
    return pl.CostEstimate(flops=int(flops), bytes_accessed=int(moved), transcendentals=0)


def call(kernel, args, outs, scratch, flops, smem_first=False):
    specs = [VMEM_SPEC] * len(args)
    if smem_first:
        specs[0] = SMEM_SPEC
    return pl.pallas_call(
        kernel,
        out_shape=outs,
        in_specs=specs,
        out_specs=[VMEM_SPEC] * len(outs),
        scratch_shapes=scratch,
        compiler_params=pltpu.CompilerParams(vmem_limit_bytes=VMEM_LIMIT),
        cost_estimate=cost(flops, list(args) + list(outs)),
    )(*args)


def route(lay, scalars, items):
    args = [scalars]
    plan = []
    for tokens, ids, gates, fresh in items:
        args += [tokens, ids]
        if gates is not None:
            args.append(gates)
        if fresh is not None:
            args.append(fresh)
        plan.append((gates is not None, fresh is not None))
    out = jax.ShapeDtypeStruct((len(items), lay.main, lay.packed), BF16)
    return call(
        functools.partial(route_kernel, lay, tuple(plan)),
        args,
        [out] * lay.experts,
        [stage_shape(lay)],
        2 * lay.slots * lay.tokens * lay.width * len(items),
        smem_first=True,
    )


def exchange(lay, by_distance):
    got = [by_distance[0]]
    for d in range(1, lay.peers):
        pairs = [(i, i ^ d) for i in range(lay.peers)]
        got.append(lax.ppermute(by_distance[d], "expert", pairs))
    return got


def dispatch(lay, payloads):
    return exchange(lay, [payloads[d // 2] for d in range(lay.peers)])


def load_rows(lay, refs, lead, stage, extra_rows):
    main = stacked_main(lay, [r[lead, :, : lay.width] for r in refs])
    if not lay.extra:
        return main
    extra_rows[...] = jnp.zeros_like(extra_rows)
    for d, ref in enumerate(refs):
        unpack_extra(lay, ref[lead, :, lay.width :].astype(F32), stage, extra_rows, d * lay.extra)
    return jnp.concatenate([main, extra_rows[...].astype(BF16)], axis=0)


def store_parts(lay, rows, refs, stage):
    for d, ref in enumerate(refs):
        ref[0, :, : lay.width] = rows[d * lay.main : (d + 1) * lay.main].astype(BF16)
        pack_extra(lay, rows, lay.peers * lay.main + d * lay.extra, ref, 0, stage)


def extra_shape(lay):
    return pltpu.VMEM((lay.rows_held - lay.peers * lay.main, lay.width), F32)


NT = (((1,), (1,)), ((), ()))
TN = (((0,), (0,)), ((), ()))


def forward_kernel(lay, lead, *refs):
    blocks = refs[: lay.peers]
    w_gate, w_up, w_down = refs[lay.peers : lay.peers + 3]
    outs = refs[lay.peers + 3 : 2 * lay.peers + 3]
    stage, extra_rows = refs[2 * lay.peers + 3 :]
    rows = load_rows(lay, blocks, lead, stage, extra_rows)
    gate = jnp.dot(rows, w_gate[...], preferred_element_type=F32)
    up = jnp.dot(rows, w_up[...], preferred_element_type=F32)
    hidden = (gate * jax.nn.sigmoid(gate) * up).astype(BF16)
    part = jnp.dot(hidden, w_down[...], preferred_element_type=F32)
    store_parts(lay, part, outs, stage)


def forward(lay, blocks, lead, weights):
    out = jax.ShapeDtypeStruct((1, lay.main, lay.packed), BF16)
    return call(
        functools.partial(forward_kernel, lay, lead),
        list(blocks) + list(weights),
        [out] * lay.peers,
        [stage_shape(lay), extra_shape(lay)],
        2 * 3 * lay.rows * lay.width * weights[0].shape[1],
    )


def backward_kernel(lay, row_lead, cot_lead, *refs):
    n = lay.peers
    row_blocks, cot_blocks = refs[:n], refs[n : 2 * n]
    w_gate, w_up, w_down = refs[2 * n : 2 * n + 3]
    outs = refs[2 * n + 3 : 3 * n + 3]
    rows_out, cot_out, d_gate_out, d_up_out, hidden_out = refs[3 * n + 3 : 3 * n + 8]
    stage, extra_rows = refs[3 * n + 8 :]
    rows = load_rows(lay, row_blocks, row_lead, stage, extra_rows)
    rows_out[...] = rows
    gate = jnp.dot(rows, w_gate[...], preferred_element_type=F32)
    up = jnp.dot(rows, w_up[...], preferred_element_type=F32)
    row_cot = load_rows(lay, cot_blocks, cot_lead, stage, extra_rows)
    cot_out[...] = row_cot
    d_hidden = lax.dot_general(row_cot, w_down[...], NT, preferred_element_type=F32)
    logistic = jax.nn.sigmoid(gate)
    swish = gate * logistic
    hidden_out[...] = (swish * up).astype(BF16)
    d_gate = (d_hidden * up * logistic * (1.0 + gate * (1.0 - logistic))).astype(BF16)
    d_up = (d_hidden * swish).astype(BF16)
    d_gate_out[...] = d_gate
    d_up_out[...] = d_up
    back = lax.dot_general(d_gate, w_gate[...], NT, preferred_element_type=F32)
    back = back + lax.dot_general(d_up, w_up[...], NT, preferred_element_type=F32)
    store_parts(lay, back, outs, stage)


def backward(lay, rows, row_lead, cots, cot_lead, weights):
    half = weights[0].shape[1]
    out = jax.ShapeDtypeStruct((1, lay.main, lay.packed), BF16)
    wide = jax.ShapeDtypeStruct((lay.rows_held, lay.width), BF16)
    narrow = jax.ShapeDtypeStruct((lay.rows_held, half), BF16)
    got = call(
        functools.partial(backward_kernel, lay, row_lead, cot_lead),
        list(rows) + list(cots) + list(weights),
        [out] * lay.peers + [wide, wide, narrow, narrow, narrow],
        [stage_shape(lay), extra_shape(lay)],
        2 * 5 * lay.rows * lay.width * half,
    )
    return got[: lay.peers], got[lay.peers :]


def combine_kernel(lay, has_gates, has_choice, has_first, *refs):
    scalars, tokens_ref, ids_ref = refs[:3]
    at = 3
    tokens = tokens_ref[...]
    if has_choice:
        tokens = jnp.where(scalars[1] == 1, refs[at][...], tokens)
        at += 1
    if has_gates:
        gates = refs[at][...]
        at += 1
    if has_first:
        first = refs[at]
        at += 1
    parts = refs[at : at + lay.peers]
    out, stage, extra_rows = refs[at + lay.peers :]
    mains = []
    if lay.extra:
        extra_rows[...] = jnp.zeros_like(extra_rows)
    for j in range(lay.experts):
        total = parts[2 * j][0].astype(F32) + parts[2 * j + 1][0].astype(F32)
        mains.append(total[:, : lay.width].astype(BF16))
        if lay.extra:
            unpack_extra(lay, total[:, lay.width :], stage, extra_rows, j * lay.extra)
    outputs = stacked_main(lay, mains)
    if lay.slots > lay.experts * lay.main:
        outputs = jnp.concatenate([outputs, extra_rows[...].astype(BF16)], axis=0)
    onehot = slot_onehot(lay, ids_ref[...], scalars[0])
    picked = lax.dot_general(onehot, outputs, TN, preferred_element_type=F32)
    if has_gates:
        picked = picked * gates
    mixed = (tokens.astype(F32) + picked).astype(BF16)
    if has_first:
        out[0] = first[...]
        out[1] = mixed
    else:
        out[...] = mixed


def combine(lay, scalars, tokens, ids, gates, parts, fresh=None, first=None):
    args = [scalars, tokens, ids]
    if fresh is not None:
        args.append(fresh)
    if gates is not None:
        args.append(gates)
    if first is not None:
        args.append(first)
    args += list(parts)
    shape = (lay.tokens, lay.width)
    if first is not None:
        shape = (2,) + shape
    spare = max(8, lay.slots - lay.experts * lay.main)
    return call(
        functools.partial(
            combine_kernel, lay, gates is not None, fresh is not None, first is not None
        ),
        args,
        [jax.ShapeDtypeStruct(shape, BF16)],
        [stage_shape(lay), pltpu.VMEM((spare, lay.width), F32)],
        2 * lay.slots * lay.tokens * lay.width,
        smem_first=True,
    )[0]


def gradient_kernel(passes, *refs):
    wide = refs[: 2 * passes]
    narrow = refs[2 * passes : 5 * passes]
    grad_gate, grad_up, grad_down = refs[5 * passes :]

    def total(left, right):
        terms = [
            lax.dot_general(a[...], b[...], TN, preferred_element_type=F32)
            for a, b in zip(left, right)
        ]
        return functools.reduce(jnp.add, terms).astype(BF16)

    rows, cots = wide[:passes], wide[passes:]
    d_gate, d_up, hidden = narrow[:passes], narrow[passes : 2 * passes], narrow[2 * passes :]
    grad_gate[...] = total(rows, d_gate)
    grad_up[...] = total(rows, d_up)
    grad_down[...] = total(hidden, cots)


def gradients(kept, half):
    passes = len(kept)
    held, width = kept[0][0].shape
    tile = 2 * LANES if width % (2 * LANES) == 0 else width
    args = [k[i] for i in range(5) for k in kept]
    wide = pl.BlockSpec((held, tile), lambda i: (0, i))
    narrow = pl.BlockSpec((held, half), lambda i: (0, 0))
    tall = pl.BlockSpec((tile, half), lambda i: (i, 0))
    flat = pl.BlockSpec((half, tile), lambda i: (0, i))
    outs = [
        jax.ShapeDtypeStruct((width, half), BF16),
        jax.ShapeDtypeStruct((width, half), BF16),
        jax.ShapeDtypeStruct((half, width), BF16),
    ]
    return pl.pallas_call(
        functools.partial(gradient_kernel, passes),
        grid=(width // tile,),
        out_shape=outs,
        in_specs=[wide] * (2 * passes) + [narrow] * (3 * passes),
        out_specs=[tall, tall, flat],
        compiler_params=pltpu.CompilerParams(vmem_limit_bytes=VMEM_LIMIT),
        cost_estimate=cost(2 * 3 * passes * held * width * half, args + outs),
    )(*args)


def mirrored(value):
    count = lax.axis_size("section")
    return lax.ppermute(value, "section", [(i, count - 1 - i) for i in range(count)])


def passed_along(value, by):
    count = lax.axis_size("section")
    pairs = [(i, i + by) for i in range(count) if 0 <= i + by < count]
    return lax.ppermute(value, "section", pairs)


def per_device(
    left_in,
    left_new,
    left_saved,
    left_cot,
    right_in,
    right_saved,
    right_cot,
    right_cot_new,
    expert_ids,
    gate_values,
    w_gate,
    w_up,
    w_down,
):
    peers = lax.axis_size("expert")
    tokens, width = left_in.shape[1:]
    assert expert_ids.shape[-1] == 1
    lay = Layout(peers, tokens, width)
    weights = (w_gate[0, 0], w_up[0, 0], w_down[0, 0])
    half = w_gate.shape[-1]
    section = lax.axis_index("section")
    own_expert = lax.axis_index("expert") // 2
    is_first = (section == 0).astype(jnp.int32)
    is_last = (section == lax.axis_size("section") - 1).astype(jnp.int32)
    left_scalars = jnp.stack([own_expert, is_first]).astype(jnp.int32)
    right_scalars = jnp.stack([own_expert, is_last]).astype(jnp.int32)

    def ids(slot, side):
        return expert_ids[slot, side, 0]

    def gates(slot, side):
        return gate_values[slot, side, 0]

    saved_zero = mirrored(right_saved[0, 0])
    cot_zero = mirrored(right_cot[0])

    sent = route(lay, left_scalars, [(left_in[0], ids(0, 0), None, None)])
    rows_f0 = dispatch(lay, sent)
    sent = route(
        lay,
        left_scalars,
        [
            (left_saved[0], ids(1, 1), None, None),
            (left_cot[0], ids(1, 1), gates(1, 1), None),
        ],
    )
    rows_b1 = dispatch(lay, sent)
    parts_f0 = exchange(lay, forward(lay, rows_f0, 0, weights))
    left_zero = combine(lay, left_scalars, left_in[0], ids(0, 0), gates(0, 0), parts_f0)
    arriving = passed_along(left_zero, 1)

    right_first = mirrored(right_in[0])
    saved_two = mirrored(right_saved[1, 0])

    sent = route(
        lay,
        right_scalars,
        [(saved_zero, ids(0, 1), None, None), (cot_zero, ids(0, 1), gates(0, 1), None)],
    )
    rows_b0 = dispatch(lay, sent)
    parts, kept_b1 = backward(lay, rows_b1, 0, rows_b1, 1, weights)
    parts_b1 = exchange(lay, parts)
    back_one = combine(lay, right_scalars, left_cot[0], ids(1, 1), None, parts_b1)
    parts, kept_b0 = backward(lay, rows_b0, 0, rows_b0, 1, weights)
    parts_b0 = exchange(lay, parts)
    back_zero = combine(lay, right_scalars, cot_zero, ids(0, 1), None, parts_b0)
    returning = passed_along(back_zero, -1)

    sent = route(
        lay,
        right_scalars,
        [(right_first, ids(1, 0), None, None), (saved_two, ids(2, 1), None, None)],
    )
    rows_f1 = dispatch(lay, sent)
    sent = route(lay, left_scalars, [(arriving, ids(2, 0), None, left_new)])
    rows_f2 = dispatch(lay, sent)
    parts_f2 = exchange(lay, forward(lay, rows_f2, 0, weights))
    left_out = combine(
        lay, left_scalars, arriving, ids(2, 0), gates(2, 0), parts_f2, left_new, left_zero
    )
    parts_f1 = exchange(lay, forward(lay, rows_f1, 0, weights))
    right_out = combine(lay, right_scalars, right_first, ids(1, 0), gates(1, 0), parts_f1)

    sent = route(lay, right_scalars, [(returning, ids(2, 1), gates(2, 1), right_cot_new)])
    cots_b2 = dispatch(lay, sent)
    parts, kept_b2 = backward(lay, rows_f1, 1, cots_b2, 0, weights)
    parts_b2 = exchange(lay, parts)
    grad_gate, grad_up, grad_down = gradients((kept_b0, kept_b1, kept_b2), half)
    right_back = combine(
        lay, right_scalars, returning, ids(2, 1), None, parts_b2, right_cot_new, back_zero
    )
    return (
        left_out[:, None],
        right_out[None],
        back_one[None],
        right_back[:, None],
        grad_gate[None, None],
        grad_up[None, None],
        grad_down[None, None],
    )


def solution(mesh):
    in_specs = (
        P("section", "expert", None),
        P("expert", None),
        P("section", "expert", None),
        P("section", "expert", None),
        P("section", "expert", None),
        P(None, "section", "expert", None),
        P("section", "expert", None),
        P("expert", None),
        P(None, None, "section", "expert", None),
        P(None, None, "section", "expert", None),
        P("section", "expert", None, None),
        P("section", "expert", None, None),
        P("section", "expert", None, None),
    )
    out_specs = (
        P(None, "section", "expert", None),
        P("section", "expert", None),
        P("section", "expert", None),
        P(None, "section", "expert", None),
        P("section", "expert", None, None),
        P("section", "expert", None, None),
        P("section", "expert", None, None),
    )
    return jax.shard_map(
        per_device, mesh=mesh, in_specs=in_specs, out_specs=out_specs, check_vma=False
    )
```

time: 294 us -> 176 us (0.60)
  matrix products: 87.9 us -> 0 us
  Pallas kernels: 0 us -> 49.2 us
  waiting for transfers between devices: 55.9 us -> 25.7 us
  starting transfers between devices: 75.4 us -> 54.9 us
  local copies, waits for them, and re-layouts: 57.8 us -> 43.6 us
  other arithmetic: 13.2 us -> 0.15 us
    dot_general x45 -> x0, matrix products: 87.9 us -> none  [the longest x3 9.88 us: expert_forward(): return jnp.dot(hidden, down_half, preferred_element_type=jnp.float32)]
    all_to_all x15 -> x0, starting transfers between devices: 67.1 us -> none  [the longest x3 13.9 us: layer_backward(): lax.all_to_all(out_cot, 'expert', split_axis=0, concat_axis=0, tiled=True)]
    pallas_call x0 -> x19, Pallas kernels: none -> 49.2 us  [the longest x18 41.3 us: call(): pl.pallas_call(kernel, out_shape=outs, in_specs=specs, out_specs=[VMEM_SP...]
    ppermute x5 -> x42, starting transfers between devices: 8.37 us -> 54.9 us  [the longest x36 47.4 us: exchange(): got.append(lax.ppermute(by_distance[d], 'expert', pairs))]
    reshape x24 -> x0, local copies, waits for them, and re-layouts: 37.4 us -> none  [the longest x3 6.22 us: layer_forward(): result.astype(jnp.bfloat16).reshape(devices, item_count, model_width)]
    unnamed x66 -> x156, local copies, waits for them, and re-layouts: 4.15 us -> 32.4 us
    all_to_all x15 -> x0, waiting for transfers between devices: 24.7 us -> none  [the longest x3 9.09 us: layer_backward(): lax.all_to_all(out_cot, 'expert', split_axis=0, concat_axis=0, tiled=True)]
    squeeze x0 -> x15, local copies, waits for them, and re-layouts: none -> 11.2 us  [the longest x7 5.46 us: gates(): return gate_values[slot, side, 0]]
  transfers between devices with their start and end apart: 20 -> 42, of which waited for: 11 -> 6; matrix products, arithmetic and copies ran while one was open for 45% -> 6% of each run, Pallas kernels for 0% -> 24%
where the time goes in v1:
time: 176 us; the launch traced here: 175 us
  starting transfers between devices  54.9 us (31%)
  Pallas kernels  49.2 us (28%)
  local copies, waits for them, and re-layouts  43.6 us (25%)
  waiting for transfers between devices  25.7 us (15%)
    ppermute x36, starting transfers between devices, exchange(): got.append(lax.ppermute(by_distance[d], 'expert', pairs))  47.4 us
    pallas_call x18, Pallas kernels, call(): pl.pallas_call(kernel, out_shape=outs, in_specs=specs, out_specs=[VMEM_SP...  41.3 us
    unnamed x156, local copies, waits for them, and re-layouts  32.4 us
    ppermute x4, waiting for transfers between devices, mirrored(): lax.ppermute(value, 'section', [(i, count - 1 - i) for i in range(count)])  17.1 us
    ppermute x36, waiting for transfers between devices, exchange(): got.append(lax.ppermute(by_distance[d], 'expert', pairs))  8.54 us
    pallas_call x1, Pallas kernels, gradients(): pl.pallas_call(functools.partial(gradient_kernel, passes), grid=(width //...  7.92 us
    squeeze x7, local copies, waits for them, and re-layouts, gates(): return gate_values[slot, side, 0]  5.46 us
    ppermute x2, starting transfers between devices, passed_along(): return lax.ppermute(value, 'section', pairs)  4 us
  transfers between devices with their start and end apart: 42, of which 6 were waited for; matrix products, arithmetic and copies ran while one was open for 6% of the time, Pallas kernels for 24%

profile of v1, /device:TPU:10, one launch (start us, length us, event | category | flops | bytes accessed | tf_op | source)
XLA Modules:
  0.0 174.6 jit_solution(1124674232661236853)
XLA Ops:
  11.1 2.3 %collective-permute-done.refs_1_ = bf16[1,32,2176]{2,1,0:T(8,128)(2,1)S(1)} collective-permute-done((bf16[1,32,2176]{2,1,0:T(8,128)(2,1)S(1)}, bf16[1,32,2176]{2,1,0:T(8,128)(2,1)S(1)}, u32[]{:S(2)}, u32[]{:S(2)}) %collective-permute-start) | collective-permute-done | bytes 139296 | tf_op jit(solution)/shard_map/ppermute | solution.py:167
  19.4 2.0 %shard_map.181 = (bf16[1,32,2176]{2,1,0:T(8,128)(2,1)S(1)}, bf16[1,32,2176]{2,1,0:T(8,128)(2,1)}, bf16[1,32,2176]{2,1,0:T(8,128)(2,1)}, bf16[1,32,2176]{2,1,0:T(8,128)(2,1)}) custom-call(bf16[1,32,2176]{2,1,0:T(8,128)(2,1)S(1)} %get-tuple-element.61.refs_0_, bf16[1,32,2176]{2,1,0:T(8,128)(2,1)S(1)} %collective-permute-done.refs_1_, ...), custom_call_target="tpu_custom_call" | custom-call | flops 641728512 | bytes 5832704 | tf_op jit(solution)/shard_map/pallas_call | solution.py:131
  23.5 13.7 %collective-permute-done.13.refs_1_ = bf16[64,2048]{1,0:T(8,128)(2,1)S(1)} collective-permute-done((bf16[64,2048]{1,0:T(8,128)(2,1)}, bf16[64,2048]{1,0:T(8,128)(2,1)S(1)}, u32[]{:S(2)}, u32[]{:S(2)}) %collective-permute-start.13) | collective-permute-done | bytes 262176 | tf_op jit(solution)/shard_map/ppermute | solution.py:373
  39.4 3.4 %collective-permute-done.27.refs_3_.refs_1_ = bf16[64,2048]{1,0:T(8,128)(2,1)S(1)} collective-permute-done((bf16[64,2048]{1,0:T(8,128)(2,1)}, bf16[64,2048]{1,0:T(8,128)(2,1)S(1)}, u32[]{:S(2)}, u32[]{:S(2)}) %collective-permute-start.27) | collective-permute-done | bytes 262176 | tf_op jit(solution)/shard_map/ppermute | solution.py:373
  43.5 2.5 %collective-permute-start.5 = (bf16[1,32,2176]{2,1,0:T(8,128)(2,1)}, bf16[1,32,2176]{2,1,0:T(8,128)(2,1)}, u32[]{:S(2)}, u32[]{:S(2)}) collective-permute-start(bf16[1,32,2176]{2,1,0:T(8,128)(2,1)} %get-tuple-element.66), channel_id=1, source_target_pairs={{0,3},{1,2},{2,1},{3,0},{4,7},{5,6},{6,5},{7,4},{8,11},{9,10},{10,... | collective-permute-start | bytes 417800 | tf_op jit(solution)/shard_map/ppermute | solution.py:167
  52.6 2.2 %shard_map.192 = (bf16[2,32,2176]{2,1,0:T(8,128)(2,1)}, bf16[2,32,2176]{2,1,0:T(8,128)(2,1)}) custom-call(s32[2]{0:T(128)S(1)} %pad_add_fusion.1.refs_0_, bf16[64,2048]{1,0:T(8,128)(2,1)} %collective-permute-done.28.refs_1_, s32[64,1]{1,0:T(8,128)S(1)} %copy.37.refs_2_.refs_4_, bf16[64,2048]{1,0:T(8,128)(2,1)S(1)} %copy-done.17, ...), custom_call_target="tpu_custom_call" | custom-call | flops 41943040 | bytes 1082120 | tf_op jit(solution)/shard_map/pallas_call | solution.py:131
  60.1 2.1 %shard_map.182.refs_5_ = bf16[64,2048]{1,0:T(8,128)(2,1)} custom-call(s32[2]{0:T(128)S(1)} %copy-done.52, bf16[64,2048]{1,0:T(8,128)(2,1)S(1)} %bitcast.69, s32[64,1]{1,0:T(8,128)S(1)} %copy.21.refs_2_, f32[64,1]{1,0:T(8,128)S(1)} %copy.22.refs_3_, bf16[1,32,2176]{2,1,0:T(8,128)(2,1)S(1)} %copy-done.40, bf16[1,32,2176]{2,1,0:T(8,128)(2,1)} %collective-permute-done.3.refs_5_, ...), custom_call_target="tpu_custom_call" | custom-call | flops 20971520 | bytes 1081864 | tf_op jit(solution)/shard_map/pallas_call | solution.py:131
  68.6 2.1 %shard_map.186 = (bf16[2,32,2176]{2,1,0:T(8,128)(2,1)S(1)}, bf16[2,32,2176]{2,1,0:T(8,128)(2,1)}) custom-call(s32[2]{0:T(128)S(1)} %copy-done.45, bf16[64,2048]{1,0:T(8,128)(2,1)S(1)} %copy-done.22, s32[64,1]{1,0:T(8,128)S(1)} %copy.28.refs_2_, bf16[64,2048]{1,0:T(8,128)(2,1)} %collective-permute-done.14.refs_3_, s32[64,1]{1,0:T(8,128)S(1)} %copy.27.refs_4_.refs_2_), custom_call_target="tpu_custom_call" | custom-call | flops 41943040 | bytes 1081864 | tf_op jit(solution)/shard_map/pallas_call | solution.py:131
  71.4 2.3 %collective-permute-start.17 = (bf16[2,32,2176]{2,1,0:T(8,128)(2,1)}, bf16[2,32,2176]{2,1,0:T(8,128)(2,1)}, u32[]{:S(2)}, u32[]{:S(2)}) collective-permute-start(bf16[2,32,2176]{2,1,0:T(8,128)(2,1)} %get-tuple-element.74), channel_id=1, source_target_pairs={{0,3},{1,2},{2,1},{3,0},{4,7},{5,6},{6,5},{7,4},{8,11},{9,10},{10,... | collective-permute-start | bytes 835592 | tf_op jit(solution)/shard_map/ppermute | solution.py:167
  74.2 2.3 %collective-permute-done.31.refs_3_.refs_7_ = bf16[2,32,2176]{2,1,0:T(8,128)(2,1)} collective-permute-done((bf16[2,32,2176]{2,1,0:T(8,128)(2,1)}, bf16[2,32,2176]{2,1,0:T(8,128)(2,1)}, u32[]{:S(2)}, u32[]{:S(2)}) %collective-permute-start.31) | collective-permute-done | bytes 278560 | tf_op jit(solution)/shard_map/ppermute | solution.py:167
  81.9 3.4 %collective-permute-done.30.refs_2_.refs_6_ = bf16[2,32,2176]{2,1,0:T(8,128)(2,1)} collective-permute-done((bf16[2,32,2176]{2,1,0:T(8,128)(2,1)}, bf16[2,32,2176]{2,1,0:T(8,128)(2,1)}, u32[]{:S(2)}, u32[]{:S(2)}) %collective-permute-start.30) | collective-permute-done | bytes 278560 | tf_op jit(solution)/shard_map/ppermute | solution.py:167
  88.1 4.1 %shard_map.193 = (bf16[1,32,2176]{2,1,0:T(8,128)(2,1)S(1)}, bf16[1,32,2176]{2,1,0:T(8,128)(2,1)S(1)}, bf16[1,32,2176]{2,1,0:T(8,128)(2,1)S(1)}, bf16[1,32,2176]{...) custom-call(bf16[2,32,2176]{2,1,0:T(8,128)(2,1)} %get-tuple-element., ...), custom_call_target="tpu_custom_call" | custom-call | flops 1069547520 | bytes 9015296 | tf_op jit(solution)/shard_map/pallas_call | solution.py:131
  101.5 4.0 %shard_map.190 = (bf16[1,32,2176]{2,1,0:T(8,128)(2,1)S(1)}, bf16[1,32,2176]{2,1,0:T(8,128)(2,1)S(1)}, bf16[1,32,2176]{2,1,0:T(8,128)(2,1)S(1)}, bf16[1,32,2176]{...) custom-call(bf16[2,32,2176]{2,1,0:T(8,128)(2,1)S(1)} %copy-done.9, ...), custom_call_target="tpu_custom_call" | custom-call | flops 1069547520 | bytes 9015296 | tf_op jit(solution)/shard_map/pallas_call | solution.py:131
  107.6 2.6 %collective-permute-start.25 = (bf16[1,32,2176]{2,1,0:T(8,128)(2,1)S(1)}, bf16[1,32,2176]{2,1,0:T(8,128)(2,1)S(1)}, u32[]{:S(2)}, u32[]{:S(2)}) collective-permute-start(bf16[1,32,2176]{2,1,0:T(8,128)(2,1)S(1)} %get-tuple-element.83), channel_id=1, source_target_pairs={{0,2},{1,3},{2,0},{3,1},{4,6},{5,7},{6,4},{7,5},{8,10},{9,11},{10,... | collective-permute-start | bytes 417800 | tf_op jit(solution)/shard_map/ppermute | solution.py:167
  113.4 2.1 %collective-permute-start.35 = (bf16[64,2048]{1,0:T(8,128)(2,1)}, bf16[64,2048]{1,0:T(8,128)(2,1)}, u32[]{:S(2)}, u32[]{:S(2)}) collective-permute-start(bf16[64,2048]{1,0:T(8,128)(2,1)} %shard_map.194.refs_4_), channel_id=1, source_target_pairs={{4,0},{8,4},{12,8},{16,12},{20,16},{24,20},{28,24},{5,1},{9,5},{13... | collective-permute-start | bytes 786440 | tf_op jit(solution)/shard_map/ppermute | solution.py:379
  115.5 3.2 %shard_map.187 = (bf16[1,32,2176]{2,1,0:T(8,128)(2,1)S(1)}, bf16[1,32,2176]{2,1,0:T(8,128)(2,1)}, bf16[1,32,2176]{2,1,0:T(8,128)(2,1)}, bf16[1,32,2176]{2,1,0:T(8,128)(2,1)}) custom-call(bf16[2,32,2176]{2,1,0:T(8,128)(2,1)S(1)} %get-tuple-element.73.refs_0_, bf16[2,32,2176]{2,1,0:T(8,128)(2,1)} %collective-permute-done.15.refs_1_, ...), custom_call_target="tpu_custom_call" | custom-call | flops 641728512 | bytes 6389760 | tf_op jit(solution)/shard_map/pallas_call | solution.py:131
  128.1 2.0 %collective-permute-start.11 = (bf16[1,32,2176]{2,1,0:T(8,128)(2,1)}, bf16[1,32,2176]{2,1,0:T(8,128)(2,1)}, u32[]{:S(2)}, u32[]{:S(2)}) collective-permute-start(bf16[1,32,2176]{2,1,0:T(8,128)(2,1)} %copy-done.64), channel_id=1, source_target_pairs={{0,2},{1,3},{2,0},{3,1},{4,6},{5,7},{6,4},{7,5},{8,10},{9,11},{10,... | collective-permute-start | bytes 417800 | tf_op jit(solution)/shard_map/ppermute | solution.py:167
  133.9 2.0 %shard_map.195 = (bf16[1,32,2176]{2,1,0:T(8,128)(2,1)}, bf16[1,32,2176]{2,1,0:T(8,128)(2,1)}) custom-call(s32[2]{0:T(128)S(1)} %copy-done.47, bf16[64,2048]{1,0:T(8,128)(2,1)} %collective-permute-done.35.refs_1_, s32[64,1]{1,0:T(8,128)S(1)} %copy.27.refs_4_.refs_2_, f32[64,1]{1,0:T(8,128)S(1)} %copy-done.43, bf16[64,2048]{1,0:T(8,128)(2,1)S(1)} %copy-done.19), custom_call_target="tpu_custom_call" | custom-call | flops 20971520 | bytes 803336 | tf_op jit(solution)/shard_map/pallas_call | solution.py:131
  136.0 2.9 %collective-permute-start.38 = (bf16[1,32,2176]{2,1,0:T(8,128)(2,1)}, bf16[1,32,2176]{2,1,0:T(8,128)(2,1)}, u32[]{:S(2)}, u32[]{:S(2)}) collective-permute-start(bf16[1,32,2176]{2,1,0:T(8,128)(2,1)} %get-tuple-element.92), channel_id=1, source_target_pairs={{0,3},{1,2},{2,1},{3,0},{4,7},{5,6},{6,5},{7,4},{8,11},{9,10},{10,... | collective-permute-start | bytes 417800 | tf_op jit(solution)/shard_map/ppermute | solution.py:167
  152.2 2.1 %shard_map.188 = bf16[64,2048]{1,0:T(8,128)(2,1)} custom-call(s32[2]{0:T(128)S(1)} %copy-done.49, bf16[64,2048]{1,0:T(8,128)(2,1)S(1)} %copy-done.23, s32[64,1]{1,0:T(8,128)S(1)} %copy-done.25, f32[64,1]{1,0:T(8,128)S(1)} %copy-done.42, bf16[1,32,2176]{2,1,0:T(8,128)(2,1)S(1)} %copy-done.38, bf16[1,32,2176]{2,1,0:T(8,128)(2,1)} %collective-permute-done.18.refs_5_, ...), custom_call_target="tpu_custom_call" | custom-call | flops 20971520 | bytes 1081864 | tf_op jit(solution)/shard_map/pallas_call | solution.py:131
  154.3 2.3 %shard_map.185 = bf16[2,64,2048]{2,1,0:T(8,128)(2,1)} custom-call(s32[2]{0:T(128)S(1)} %copy-done.54, bf16[64,2048]{1,0:T(8,128)(2,1)} %collective-permute-done.6.refs_1_, s32[64,1]{1,0:T(8,128)S(1)} %copy.24.refs_2_, bf16[64,2048]{1,0:T(8,128)(2,1)S(1)} %copy-done.11, f32[64,1]{1,0:T(8,128)S(1)} %copy-done.41, bf16[64,2048]{1,0:T(8,128)(2,1)} %shard_map.182.refs_5_, ...), custom_call_target="tpu_custom_call" | custom-call | flops 20971520 | bytes 1868296 | tf_op jit(solution)/shard_map/pallas_call | solution.py:131
  156.8 4.0 %shard_map.196 = (bf16[1,32,2176]{2,1,0:T(8,128)(2,1)S(1)}, bf16[1,32,2176]{2,1,0:T(8,128)(2,1)S(1)}, bf16[1,32,2176]{2,1,0:T(8,128)(2,1)S(1)}, bf16[1,32,2176]{...) custom-call(bf16[2,32,2176]{2,1,0:T(8,128)(2,1)S(1)} %get-tuple-elem, ...), custom_call_target="tpu_custom_call" | custom-call | flops 1069547520 | bytes 8458240 | tf_op jit(solution)/shard_map/pallas_call | solution.py:131
  164.5 7.9 %shard_map.198 = (bf16[2048,384]{1,0:T(8,128)(2,1)}, bf16[2048,384]{1,0:T(8,128)(2,1)}, bf16[384,2048]{1,0:T(8,128)(2,1)}) custom-call(bf16[144,2048]{1,0:T(8,128)(2,1)S(1)} %copy-done.56, bf16[144,2048]{1,0:T(8,128)(2,1)S(1)} %copy-done.60, bf16[144,2048]{1,0:T(8,128)(2,1)S(1)} %get-tuple-element.99.refs_2_, bf16[144,2048]{1,0:T(8,128)(2,1)S(1)} %copy-done.58, ...), custom_call_target="tpu_custom_call" | custom-call | flops 2038431744 | bytes 9252864 | tf_op jit(solution)/shard_map/pallas_call | solution.py:360
  172.4 2.2 %shard_map.197 = bf16[2,64,2048]{2,1,0:T(8,128)(2,1)} custom-call(s32[2]{0:T(128)S(1)} %copy-done.50, bf16[64,2048]{1,0:T(8,128)(2,1)} %collective-permute-done.35.refs_1_, s32[64,1]{1,0:T(8,128)S(1)} %copy.27.refs_4_.refs_2_, bf16[64,2048]{1,0:T(8,128)(2,1)S(1)} %copy-done.20, bf16[64,2048]{1,0:T(8,128)(2,1)} %shard_map.194.refs_4_, ...), custom_call_target="tpu_custom_call" | custom-call | flops 20971520 | bytes 1868040 | tf_op jit(solution)/shard_map/pallas_call | solution.py:131
  (252 shorter events, 93.8 us)
Async XLA Ops:
  6.0 31.2 %collective-permute-start.13 = (bf16[64,2048]{1,0:T(8,128)(2,1)}, bf16[64,2048]{1,0:T(8,128)(2,1)S(1)}, u32[]{:S(2)}, u32[]{:S(2)}) collective-permute-start(bf16[64,2048]{1,0:T(8,128)(2,1)} %bitcast.77), channel_id=1, source_target_pairs={{0,28},{4,24},{8,20},{12,16},{16,12},{20,8},{24,4},{28,0},{1,29},{... | collective-permute-start | bytes 786440 | tf_op jit(solution)/shard_map/ppermute | solution.py:373
  6.5 36.3 %collective-permute-start.27 = (bf16[64,2048]{1,0:T(8,128)(2,1)}, bf16[64,2048]{1,0:T(8,128)(2,1)S(1)}, u32[]{:S(2)}, u32[]{:S(2)}) collective-permute-start(bf16[64,2048]{1,0:T(8,128)(2,1)} %bitcast.78), channel_id=1, source_target_pairs={{0,28},{4,24},{8,20},{12,16},{16,12},{20,8},{24,4},{28,0},{1,29},{... | collective-permute-start | bytes 786440 | tf_op jit(solution)/shard_map/ppermute | solution.py:373
  13.4 35.2 %collective-permute-start.28 = (bf16[64,2048]{1,0:T(8,128)(2,1)}, bf16[64,2048]{1,0:T(8,128)(2,1)}, u32[]{:S(2)}, u32[]{:S(2)}) collective-permute-start(bf16[64,2048]{1,0:T(8,128)(2,1)} %get-tuple-element.122), channel_id=1, source_target_pairs={{0,28},{4,24},{8,20},{12,16},{16,12},{20,8},{24,4},{28,0},{1,29},{... | collective-permute-start | bytes 786440 | tf_op jit(solution)/shard_map/ppermute | solution.py:373
  13.8 48.5 %collective-permute-start.14 = (bf16[64,2048]{1,0:T(8,128)(2,1)}, bf16[64,2048]{1,0:T(8,128)(2,1)}, u32[]{:S(2)}, u32[]{:S(2)}) collective-permute-start(bf16[64,2048]{1,0:T(8,128)(2,1)} %get-tuple-element.123), channel_id=1, source_target_pairs={{0,28},{4,24},{8,20},{12,16},{16,12},{20,8},{24,4},{28,0},{1,29},{... | collective-permute-start | bytes 786440 | tf_op jit(solution)/shard_map/ppermute | solution.py:373
  22.1 28.1 %collective-permute-start.3 = (bf16[1,32,2176]{2,1,0:T(8,128)(2,1)}, bf16[1,32,2176]{2,1,0:T(8,128)(2,1)}, u32[]{:S(2)}, u32[]{:S(2)}) collective-permute-start(bf16[1,32,2176]{2,1,0:T(8,128)(2,1)} %get-tuple-element.64), channel_id=1, source_target_pairs={{0,1},{1,0},{2,3},{3,2},{4,5},{5,4},{6,7},{7,6},{8,9},{9,8},{10,11... | collective-permute-start | bytes 417800 | tf_op jit(solution)/shard_map/ppermute | solution.py:167
  37.9 16.9 %collective-permute-start.4 = (bf16[1,32,2176]{2,1,0:T(8,128)(2,1)}, bf16[1,32,2176]{2,1,0:T(8,128)(2,1)}, u32[]{:S(2)}, u32[]{:S(2)}) collective-permute-start(bf16[1,32,2176]{2,1,0:T(8,128)(2,1)} %get-tuple-element.65), channel_id=1, source_target_pairs={{0,2},{1,3},{2,0},{3,1},{4,6},{5,7},{6,4},{7,5},{8,10},{9,11},{10,... | collective-permute-start | bytes 417800 | tf_op jit(solution)/shard_map/ppermute | solution.py:167
  50.1 20.6 %collective-permute-start.23 = (bf16[2,32,2176]{2,1,0:T(8,128)(2,1)}, bf16[2,32,2176]{2,1,0:T(8,128)(2,1)}, u32[]{:S(2)}, u32[]{:S(2)}) collective-permute-start(bf16[2,32,2176]{2,1,0:T(8,128)(2,1)} %get-tuple-element.80), channel_id=1, source_target_pairs={{0,3},{1,2},{2,1},{3,0},{4,7},{5,6},{6,5},{7,4},{8,11},{9,10},{10,... | collective-permute-start | bytes 835592 | tf_op jit(solution)/shard_map/ppermute | solution.py:167
  54.7 19.0 %collective-permute-start.29 = (bf16[2,32,2176]{2,1,0:T(8,128)(2,1)}, bf16[2,32,2176]{2,1,0:T(8,128)(2,1)}, u32[]{:S(2)}, u32[]{:S(2)}) collective-permute-start(bf16[2,32,2176]{2,1,0:T(8,128)(2,1)} %get-tuple-element.85.refs_0_.refs_4_), channel_id=1, source_target_pairs={{0,1},{1,0},{2,3},{3,2},{4,5},{5,4},{6,7},{7,6},{8,9},{9,8},{10,11... | collective-permute-start | bytes 835592 | tf_op jit(solution)/shard_map/ppermute | solution.py:167
  56.2 20.3 %collective-permute-start.31 = (bf16[2,32,2176]{2,1,0:T(8,128)(2,1)}, bf16[2,32,2176]{2,1,0:T(8,128)(2,1)}, u32[]{:S(2)}, u32[]{:S(2)}) collective-permute-start(bf16[2,32,2176]{2,1,0:T(8,128)(2,1)} %get-tuple-element.86), channel_id=1, source_target_pairs={{0,3},{1,2},{2,1},{3,0},{4,7},{5,6},{6,5},{7,4},{8,11},{9,10},{10,... | collective-permute-start | bytes 835592 | tf_op jit(solution)/shard_map/ppermute | solution.py:167
  64.2 21.1 %collective-permute-start.30 = (bf16[2,32,2176]{2,1,0:T(8,128)(2,1)}, bf16[2,32,2176]{2,1,0:T(8,128)(2,1)}, u32[]{:S(2)}, u32[]{:S(2)}) collective-permute-start(bf16[2,32,2176]{2,1,0:T(8,128)(2,1)} %get-tuple-element.86), channel_id=1, source_target_pairs={{0,2},{1,3},{2,0},{3,1},{4,6},{5,7},{6,4},{7,5},{8,10},{9,11},{10,... | collective-permute-start | bytes 835592 | tf_op jit(solution)/shard_map/ppermute | solution.py:167
  70.7 25.0 %collective-permute-start.22 = (bf16[2,32,2176]{2,1,0:T(8,128)(2,1)}, bf16[2,32,2176]{2,1,0:T(8,128)(2,1)}, u32[]{:S(2)}, u32[]{:S(2)}) collective-permute-start(bf16[2,32,2176]{2,1,0:T(8,128)(2,1)} %get-tuple-element.80), channel_id=1, source_target_pairs={{0,2},{1,3},{2,0},{3,1},{4,6},{5,7},{6,4},{7,5},{8,10},{9,11},{10,... | collective-permute-start | bytes 835592 | tf_op jit(solution)/shard_map/ppermute | solution.py:167
  71.4 25.0 %collective-permute-start.17 = (bf16[2,32,2176]{2,1,0:T(8,128)(2,1)}, bf16[2,32,2176]{2,1,0:T(8,128)(2,1)}, u32[]{:S(2)}, u32[]{:S(2)}) collective-permute-start(bf16[2,32,2176]{2,1,0:T(8,128)(2,1)} %get-tuple-element.74), channel_id=1, source_target_pairs={{0,3},{1,2},{2,1},{3,0},{4,7},{5,6},{6,5},{7,4},{8,11},{9,10},{10,... | collective-permute-start | bytes 835592 | tf_op jit(solution)/shard_map/ppermute | solution.py:167
  73.7 24.1 %collective-permute-start.16 = (bf16[2,32,2176]{2,1,0:T(8,128)(2,1)}, bf16[2,32,2176]{2,1,0:T(8,128)(2,1)}, u32[]{:S(2)}, u32[]{:S(2)}) collective-permute-start(bf16[2,32,2176]{2,1,0:T(8,128)(2,1)} %get-tuple-element.74), channel_id=1, source_target_pairs={{0,2},{1,3},{2,0},{3,1},{4,6},{5,7},{6,4},{7,5},{8,10},{9,11},{10,... | collective-permute-start | bytes 835592 | tf_op jit(solution)/shard_map/ppermute | solution.py:167
  76.5 23.0 %collective-permute-start.15 = (bf16[2,32,2176]{2,1,0:T(8,128)(2,1)S(1)}, bf16[2,32,2176]{2,1,0:T(8,128)(2,1)}, u32[]{:S(2)}, u32[]{:S(2)}) collective-permute-start(bf16[2,32,2176]{2,1,0:T(8,128)(2,1)S(1)} %get-tuple-element.73.refs_0_), channel_id=1, source_target_pairs={{0,1},{1,0},{2,3},{3,2},{4,5},{5,4},{6,7},{7,6},{8,9},{9,8},{10,11... | collective-permute-start | bytes 835592 | tf_op jit(solution)/shard_map/ppermute | solution.py:167
  100.7 18.0 %collective-permute-start.8 = (bf16[1,32,2176]{2,1,0:T(8,128)(2,1)S(1)}, bf16[1,32,2176]{2,1,0:T(8,128)(2,1)S(1)}, u32[]{:S(2)}, u32[]{:S(2)}) collective-permute-start(bf16[1,32,2176]{2,1,0:T(8,128)(2,1)S(1)} %get-tuple-element.68), channel_id=1, source_target_pairs={{0,2},{1,3},{2,0},{3,1},{4,6},{5,7},{6,4},{7,5},{8,10},{9,11},{10,... | collective-permute-start | bytes 417800 | tf_op jit(solution)/shard_map/ppermute | solution.py:167
  105.6 15.8 %collective-permute-start.24 = (bf16[1,32,2176]{2,1,0:T(8,128)(2,1)S(1)}, bf16[1,32,2176]{2,1,0:T(8,128)(2,1)S(1)}, u32[]{:S(2)}, u32[]{:S(2)}) collective-permute-start(bf16[1,32,2176]{2,1,0:T(8,128)(2,1)S(1)} %get-tuple-element.82), channel_id=1, source_target_pairs={{0,1},{1,0},{2,3},{3,2},{4,5},{5,4},{6,7},{7,6},{8,9},{9,8},{10,11... | collective-permute-start | bytes 417800 | tf_op jit(solution)/shard_map/ppermute | solution.py:167
  107.6 16.3 %collective-permute-start.25 = (bf16[1,32,2176]{2,1,0:T(8,128)(2,1)S(1)}, bf16[1,32,2176]{2,1,0:T(8,128)(2,1)S(1)}, u32[]{:S(2)}, u32[]{:S(2)}) collective-permute-start(bf16[1,32,2176]{2,1,0:T(8,128)(2,1)S(1)} %get-tuple-element.83), channel_id=1, source_target_pairs={{0,2},{1,3},{2,0},{3,1},{4,6},{5,7},{6,4},{7,5},{8,10},{9,11},{10,... | collective-permute-start | bytes 417800 | tf_op jit(solution)/shard_map/ppermute | solution.py:167
  110.3 15.9 %collective-permute-start.26 = (bf16[1,32,2176]{2,1,0:T(8,128)(2,1)S(1)}, bf16[1,32,2176]{2,1,0:T(8,128)(2,1)S(1)}, u32[]{:S(2)}, u32[]{:S(2)}) collective-permute-start(bf16[1,32,2176]{2,1,0:T(8,128)(2,1)S(1)} %get-tuple-element.84), channel_id=1, source_target_pairs={{0,3},{1,2},{2,1},{3,0},{4,7},{5,6},{6,5},{7,4},{8,11},{9,10},{10,... | collective-permute-start | bytes 417800 | tf_op jit(solution)/shard_map/ppermute | solution.py:167
  113.4 16.8 %collective-permute-start.35 = (bf16[64,2048]{1,0:T(8,128)(2,1)}, bf16[64,2048]{1,0:T(8,128)(2,1)}, u32[]{:S(2)}, u32[]{:S(2)}) collective-permute-start(bf16[64,2048]{1,0:T(8,128)(2,1)} %shard_map.194.refs_4_), channel_id=1, source_target_pairs={{4,0},{8,4},{12,8},{16,12},{20,16},{24,20},{28,24},{5,1},{9,5},{13... | collective-permute-start | bytes 786440 | tf_op jit(solution)/shard_map/ppermute | solution.py:379
  128.1 26.2 %collective-permute-start.11 = (bf16[1,32,2176]{2,1,0:T(8,128)(2,1)}, bf16[1,32,2176]{2,1,0:T(8,128)(2,1)}, u32[]{:S(2)}, u32[]{:S(2)}) collective-permute-start(bf16[1,32,2176]{2,1,0:T(8,128)(2,1)} %copy-done.64), channel_id=1, source_target_pairs={{0,2},{1,3},{2,0},{3,1},{4,6},{5,7},{6,4},{7,5},{8,10},{9,11},{10,... | collective-permute-start | bytes 417800 | tf_op jit(solution)/shard_map/ppermute | solution.py:167
  130.1 24.2 %collective-permute-start.12 = (bf16[1,32,2176]{2,1,0:T(8,128)(2,1)}, bf16[1,32,2176]{2,1,0:T(8,128)(2,1)}, u32[]{:S(2)}, u32[]{:S(2)}) collective-permute-start(bf16[1,32,2176]{2,1,0:T(8,128)(2,1)} %copy-done.63), channel_id=1, source_target_pairs={{0,3},{1,2},{2,1},{3,0},{4,7},{5,6},{6,5},{7,4},{8,11},{9,10},{10,... | collective-permute-start | bytes 417800 | tf_op jit(solution)/shard_map/ppermute | solution.py:167
  135.9 20.9 %collective-permute-start.36 = (bf16[1,32,2176]{2,1,0:T(8,128)(2,1)}, bf16[1,32,2176]{2,1,0:T(8,128)(2,1)}, u32[]{:S(2)}, u32[]{:S(2)}) collective-permute-start(bf16[1,32,2176]{2,1,0:T(8,128)(2,1)} %get-tuple-element.91.refs_4_), channel_id=1, source_target_pairs={{0,1},{1,0},{2,3},{3,2},{4,5},{5,4},{6,7},{7,6},{8,9},{9,8},{10,11... | collective-permute-start | bytes 417800 | tf_op jit(solution)/shard_map/ppermute | solution.py:167
  136.0 20.8 %collective-permute-start.38 = (bf16[1,32,2176]{2,1,0:T(8,128)(2,1)}, bf16[1,32,2176]{2,1,0:T(8,128)(2,1)}, u32[]{:S(2)}, u32[]{:S(2)}) collective-permute-start(bf16[1,32,2176]{2,1,0:T(8,128)(2,1)} %get-tuple-element.92), channel_id=1, source_target_pairs={{0,3},{1,2},{2,1},{3,0},{4,7},{5,6},{6,5},{7,4},{8,11},{9,10},{10,... | collective-permute-start | bytes 417800 | tf_op jit(solution)/shard_map/ppermute | solution.py:167
  138.9 17.9 %collective-permute-start.37 = (bf16[1,32,2176]{2,1,0:T(8,128)(2,1)}, bf16[1,32,2176]{2,1,0:T(8,128)(2,1)}, u32[]{:S(2)}, u32[]{:S(2)}) collective-permute-start(bf16[1,32,2176]{2,1,0:T(8,128)(2,1)} %get-tuple-element.92), channel_id=1, source_target_pairs={{0,2},{1,3},{2,0},{3,1},{4,6},{5,7},{6,4},{7,5},{8,10},{9,11},{10,... | collective-permute-start | bytes 417800 | tf_op jit(solution)/shard_map/ppermute | solution.py:167
  (96 other events, 773.9 us)

commit v2 on v1

--- a/solution.py
+++ b/solution.py
@@ -10,7 +10,7 @@
 LANES = 128
 F32 = jnp.float32
 BF16 = jnp.bfloat16
-VMEM_LIMIT = 40 * 1024 * 1024
+MIB = 1024 * 1024
 
 
 class Layout:
@@ -65,12 +65,19 @@
     return jnp.concatenate(blocks, axis=0)
 
 
-def slot_onehot(lay, ids, own_expert):
+def as_column(row):
+    square = (row.shape[1], row.shape[1])
+    down = lax.broadcasted_iota(jnp.int32, square, 0)
+    across = lax.broadcasted_iota(jnp.int32, square, 1)
+    return jnp.sum(jnp.where(down == across, row, jnp.zeros_like(row)), axis=1, keepdims=True)
+
+
+def slot_onehot(lay, ids_row):
     tokens = lay.tokens
+    own_expert = lax.axis_index("expert") // 2
     down = lax.broadcasted_iota(jnp.int32, (tokens, tokens), 0)
     across = lax.broadcasted_iota(jnp.int32, (tokens, tokens), 1)
-    ids_row = jnp.sum(jnp.where(down == across, ids, 0), axis=0, keepdims=True)
-    earlier = jnp.logical_and(ids == ids_row, down < across)
+    earlier = jnp.logical_and(as_column(ids_row) == ids_row, down < across)
     rank = jnp.sum(earlier.astype(jnp.int32), axis=0, keepdims=True)
     near = ids_row ^ own_expert
     slot = jnp.where(
@@ -86,37 +93,37 @@
     return pltpu.VMEM((lay.main, max(1, lay.groups) * LANES), F32)
 
 
-def route_kernel(lay, plan, *refs):
-    scalars = refs[0]
-    at = 1
+def at_edge(edge):
+    last = lax.axis_size("section") - 1
+    return lax.axis_index("section") == (0 if edge == "first" else last)
+
+
+def route_kernel(lay, plan, ids, gates, *refs):
+    at = 0
     items = []
-    for has_gates, has_choice in plan:
-        item = {"tokens": refs[at], "ids": refs[at + 1]}
-        at += 2
-        if has_gates:
-            item["gates"] = refs[at]
+    for which, lead, scaled, edge in plan:
+        tokens = refs[at][...] if lead is None else refs[at][lead]
+        at += 1
+        if edge is not None:
+            tokens = jnp.where(at_edge(edge), refs[at][...], tokens)
             at += 1
-        if has_choice:
-            item["fresh"] = refs[at]
-            at += 1
-        items.append(item)
-    outs = refs[at : at + lay.experts]
-    stage = refs[at + lay.experts]
-    for lead, item in enumerate(items):
-        tokens = item["tokens"][...]
-        if "fresh" in item:
-            tokens = jnp.where(scalars[1] == 1, item["fresh"][...], tokens)
-        if "gates" in item:
-            tokens = (item["gates"][...] * tokens.astype(F32)).astype(BF16)
-        onehot = slot_onehot(lay, item["ids"][...], scalars[0])
-        rows = jnp.dot(onehot, tokens, preferred_element_type=F32)
+        items.append((which, scaled, tokens))
+    outs = refs[len(refs) - 1 - lay.experts : len(refs) - 1]
+    stage = refs[len(refs) - 1]
+    onehots = {}
+    for lead, (which, scaled, tokens) in enumerate(items):
+        if which not in onehots:
+            onehots[which] = slot_onehot(lay, ids[which])
+        if scaled:
+            tokens = (as_column(gates[which]) * tokens.astype(F32)).astype(BF16)
+        rows = jnp.dot(onehots[which], tokens, preferred_element_type=F32)
         for j, out in enumerate(outs):
             out[lead, :, : lay.width] = rows[j * lay.main : (j + 1) * lay.main].astype(BF16)
             pack_extra(lay, rows, lay.experts * lay.main + j * lay.extra, out, lead, stage)
 
 
 VMEM_SPEC = pl.BlockSpec(memory_space=pltpu.VMEM)
-SMEM_SPEC = pl.BlockSpec(memory_space=pltpu.SMEM)
+ANY_SPEC = pl.BlockSpec(memory_space=pl.ANY)
 
 
 def cost(flops, arrays):
@@ -124,31 +131,31 @@
     return pl.CostEstimate(flops=int(flops), bytes_accessed=int(moved), transcendentals=0)
 
 
-def call(kernel, args, outs, scratch, flops, smem_first=False):
-    specs = [VMEM_SPEC] * len(args)
-    if smem_first:
-        specs[0] = SMEM_SPEC
+def call(kernel, args, outs, scratch, flops, limit, after=()):
+    specs = [VMEM_SPEC] * len(args) + [ANY_SPEC] * len(after)
+
+    def body(*refs):
+        kernel(*refs[: len(args)], *refs[len(args) + len(after) :])
+
     return pl.pallas_call(
-        kernel,
+        body,
         out_shape=outs,
         in_specs=specs,
         out_specs=[VMEM_SPEC] * len(outs),
         scratch_shapes=scratch,
-        compiler_params=pltpu.CompilerParams(vmem_limit_bytes=VMEM_LIMIT),
+        compiler_params=pltpu.CompilerParams(vmem_limit_bytes=limit * MIB),
         cost_estimate=cost(flops, list(args) + list(outs)),
-    )(*args)
-
-
-def route(lay, scalars, items):
-    args = [scalars]
+    )(*args, *after)
+
+
+def route(lay, tables, items, after=()):
+    args = list(tables)
     plan = []
-    for tokens, ids, gates, fresh in items:
-        args += [tokens, ids]
-        if gates is not None:
-            args.append(gates)
+    for tokens, lead, which, scaled, edge, fresh in items:
+        args.append(tokens)
         if fresh is not None:
             args.append(fresh)
-        plan.append((gates is not None, fresh is not None))
+        plan.append((which, lead, scaled, edge))
     out = jax.ShapeDtypeStruct((len(items), lay.main, lay.packed), BF16)
     return call(
         functools.partial(route_kernel, lay, tuple(plan)),
@@ -156,8 +163,42 @@
         [out] * lay.experts,
         [stage_shape(lay)],
         2 * lay.slots * lay.tokens * lay.width * len(items),
-        smem_first=True,
-    )
+        8,
+        after,
+    )
+
+
+def stack_kernel(picks, *refs):
+    count = len(picks)
+    out, sems = refs[count], refs[count + 1]
+    copies = []
+    for at, pick in enumerate(picks):
+        source = refs[at]
+        for i in pick:
+            source = source.at[i]
+        copies.append(pltpu.make_async_copy(source, out.at[at], sems.at[at]))
+    for copy in copies:
+        copy.start()
+    for copy in copies:
+        copy.wait()
+
+
+def stacked(lay, arrays, picks, after=()):
+    count = len(arrays)
+
+    def body(*refs):
+        stack_kernel(picks, *refs[:count], *refs[count + len(after) :])
+
+    out = jax.ShapeDtypeStruct((count, lay.tokens, lay.width), BF16)
+    return pl.pallas_call(
+        body,
+        out_shape=out,
+        in_specs=[ANY_SPEC] * (count + len(after)),
+        out_specs=VMEM_SPEC,
+        scratch_shapes=[pltpu.SemaphoreType.DMA((count,))],
+        compiler_params=pltpu.CompilerParams(vmem_limit_bytes=2 * MIB),
+        cost_estimate=cost(0, [out, out]),
+    )(*arrays, *after)
 
 
 def exchange(lay, by_distance):
@@ -209,7 +250,7 @@
     store_parts(lay, part, outs, stage)
 
 
-def forward(lay, blocks, lead, weights):
+def forward(lay, blocks, lead, weights, after=()):
     out = jax.ShapeDtypeStruct((1, lay.main, lay.packed), BF16)
     return call(
         functools.partial(forward_kernel, lay, lead),
@@ -217,6 +258,8 @@
         [out] * lay.peers,
         [stage_shape(lay), extra_shape(lay)],
         2 * 3 * lay.rows * lay.width * weights[0].shape[1],
+        14,
+        after,
     )
 
 
@@ -225,8 +268,8 @@
     row_blocks, cot_blocks = refs[:n], refs[n : 2 * n]
     w_gate, w_up, w_down = refs[2 * n : 2 * n + 3]
     outs = refs[2 * n + 3 : 3 * n + 3]
-    rows_out, cot_out, d_gate_out, d_up_out, hidden_out = refs[3 * n + 3 : 3 * n + 8]
-    stage, extra_rows = refs[3 * n + 8 :]
+    rows_out, cot_out, d_both_out, hidden_out = refs[3 * n + 3 : 3 * n + 7]
+    stage, extra_rows = refs[3 * n + 7 :]
     rows = load_rows(lay, row_blocks, row_lead, stage, extra_rows)
     rows_out[...] = rows
     gate = jnp.dot(rows, w_gate[...], preferred_element_type=F32)
@@ -239,37 +282,37 @@
     hidden_out[...] = (swish * up).astype(BF16)
     d_gate = (d_hidden * up * logistic * (1.0 + gate * (1.0 - logistic))).astype(BF16)
     d_up = (d_hidden * swish).astype(BF16)
-    d_gate_out[...] = d_gate
-    d_up_out[...] = d_up
+    half = d_gate.shape[1]
+    d_both_out[:, :half] = d_gate
+    d_both_out[:, half:] = d_up
     back = lax.dot_general(d_gate, w_gate[...], NT, preferred_element_type=F32)
     back = back + lax.dot_general(d_up, w_up[...], NT, preferred_element_type=F32)
     store_parts(lay, back, outs, stage)
 
 
-def backward(lay, rows, row_lead, cots, cot_lead, weights):
+def backward(lay, rows, row_lead, cots, cot_lead, weights, after=()):
     half = weights[0].shape[1]
     out = jax.ShapeDtypeStruct((1, lay.main, lay.packed), BF16)
     wide = jax.ShapeDtypeStruct((lay.rows_held, lay.width), BF16)
+    both = jax.ShapeDtypeStruct((lay.rows_held, 2 * half), BF16)
     narrow = jax.ShapeDtypeStruct((lay.rows_held, half), BF16)
     got = call(
         functools.partial(backward_kernel, lay, row_lead, cot_lead),
         list(rows) + list(cots) + list(weights),
-        [out] * lay.peers + [wide, wide, narrow, narrow, narrow],
+        [out] * lay.peers + [wide, wide, both, narrow],
         [stage_shape(lay), extra_shape(lay)],
         2 * 5 * lay.rows * lay.width * half,
+        18,
+        after,
     )
     return got[: lay.peers], got[lay.peers :]
 
 
-def combine_kernel(lay, has_gates, has_choice, has_first, *refs):
-    scalars, tokens_ref, ids_ref = refs[:3]
-    at = 3
-    tokens = tokens_ref[...]
-    if has_choice:
-        tokens = jnp.where(scalars[1] == 1, refs[at][...], tokens)
-        at += 1
-    if has_gates:
-        gates = refs[at][...]
+def combine_kernel(lay, which, lead, scaled, edge, has_first, ids, gates, tokens_ref, *refs):
+    at = 0
+    tokens = tokens_ref[...] if lead is None else tokens_ref[lead]
+    if edge is not None:
+        tokens = jnp.where(at_edge(edge), refs[at][...], tokens)
         at += 1
     if has_first:
         first = refs[at]
@@ -287,10 +330,10 @@
     outputs = stacked_main(lay, mains)
     if lay.slots > lay.experts * lay.main:
         outputs = jnp.concatenate([outputs, extra_rows[...].astype(BF16)], axis=0)
-    onehot = slot_onehot(lay, ids_ref[...], scalars[0])
+    onehot = slot_onehot(lay, ids[which])
     picked = lax.dot_general(onehot, outputs, TN, preferred_element_type=F32)
-    if has_gates:
-        picked = picked * gates
+    if scaled:
+        picked = picked * as_column(gates[which])
     mixed = (tokens.astype(F32) + picked).astype(BF16)
     if has_first:
         out[0] = first[...]
@@ -299,12 +342,12 @@
         out[...] = mixed
 
 
-def combine(lay, scalars, tokens, ids, gates, parts, fresh=None, first=None):
-    args = [scalars, tokens, ids]
+def combine(
+    lay, tables, which, scaled, tokens, parts, lead=None, edge=None, fresh=None, first=None, after=()
+):
+    args = list(tables) + [tokens]
     if fresh is not None:
         args.append(fresh)
-    if gates is not None:
-        args.append(gates)
     if first is not None:
         args.append(first)
     args += list(parts)
@@ -313,42 +356,36 @@
         shape = (2,) + shape
     spare = max(8, lay.slots - lay.experts * lay.main)
     return call(
-        functools.partial(
-            combine_kernel, lay, gates is not None, fresh is not None, first is not None
-        ),
+        functools.partial(combine_kernel, lay, which, lead, scaled, edge, first is not None),
         args,
         [jax.ShapeDtypeStruct(shape, BF16)],
         [stage_shape(lay), pltpu.VMEM((spare, lay.width), F32)],
         2 * lay.slots * lay.tokens * lay.width,
-        smem_first=True,
+        8,
+        after,
     )[0]
 
 
 def gradient_kernel(passes, *refs):
-    wide = refs[: 2 * passes]
-    narrow = refs[2 * passes : 5 * passes]
-    grad_gate, grad_up, grad_down = refs[5 * passes :]
-
-    def total(left, right):
-        terms = [
-            lax.dot_general(a[...], b[...], TN, preferred_element_type=F32)
-            for a, b in zip(left, right)
-        ]
-        return functools.reduce(jnp.add, terms).astype(BF16)
-
-    rows, cots = wide[:passes], wide[passes:]
-    d_gate, d_up, hidden = narrow[:passes], narrow[passes : 2 * passes], narrow[2 * passes :]
-    grad_gate[...] = total(rows, d_gate)
-    grad_up[...] = total(rows, d_up)
-    grad_down[...] = total(hidden, cots)
+    rows, cots, both, hidden = (
+        jnp.concatenate([r[...] for r in refs[i * passes : (i + 1) * passes]], axis=0)
+        for i in range(4)
+    )
+    grad_gate, grad_up, grad_down = refs[4 * passes :]
+    half = hidden.shape[1]
+    total = lax.dot_general(rows, both, TN, preferred_element_type=F32)
+    grad_gate[...] = total[:, :half].astype(BF16)
+    grad_up[...] = total[:, half:].astype(BF16)
+    grad_down[...] = lax.dot_general(hidden, cots, TN, preferred_element_type=F32).astype(BF16)
 
 
 def gradients(kept, half):
     passes = len(kept)
     held, width = kept[0][0].shape
     tile = 2 * LANES if width % (2 * LANES) == 0 else width
-    args = [k[i] for i in range(5) for k in kept]
+    args = [k[i] for i in range(4) for k in kept]
     wide = pl.BlockSpec((held, tile), lambda i: (0, i))
+    both = pl.BlockSpec((held, 2 * half), lambda i: (0, 0))
     narrow = pl.BlockSpec((held, half), lambda i: (0, 0))
     tall = pl.BlockSpec((tile, half), lambda i: (i, 0))
     flat = pl.BlockSpec((half, tile), lambda i: (0, i))
@@ -361,9 +398,9 @@
         functools.partial(gradient_kernel, passes),
         grid=(width // tile,),
         out_shape=outs,
-        in_specs=[wide] * (2 * passes) + [narrow] * (3 * passes),
+        in_specs=[wide] * (2 * passes) + [both] * passes + [narrow] * passes,
         out_specs=[tall, tall, flat],
-        compiler_params=pltpu.CompilerParams(vmem_limit_bytes=VMEM_LIMIT),
+        compiler_params=pltpu.CompilerParams(vmem_limit_bytes=16 * MIB),
         cost_estimate=cost(2 * 3 * passes * held * width * half, args + outs),
     )(*args)
 
@@ -400,76 +437,90 @@
     lay = Layout(peers, tokens, width)
     weights = (w_gate[0, 0], w_up[0, 0], w_down[0, 0])
     half = w_gate.shape[-1]
-    section = lax.axis_index("section")
-    own_expert = lax.axis_index("expert") // 2
-    is_first = (section == 0).astype(jnp.int32)
-    is_last = (section == lax.axis_size("section") - 1).astype(jnp.int32)
-    left_scalars = jnp.stack([own_expert, is_first]).astype(jnp.int32)
-    right_scalars = jnp.stack([own_expert, is_last]).astype(jnp.int32)
-
-    def ids(slot, side):
-        return expert_ids[slot, side, 0]
-
-    def gates(slot, side):
-        return gate_values[slot, side, 0]
-
-    saved_zero = mirrored(right_saved[0, 0])
-    cot_zero = mirrored(right_cot[0])
-
-    sent = route(lay, left_scalars, [(left_in[0], ids(0, 0), None, None)])
-    rows_f0 = dispatch(lay, sent)
+    slots = expert_ids.shape[0]
+    tables = (
+        expert_ids.reshape(2 * slots, 1, tokens),
+        gate_values.reshape(2 * slots, 1, tokens),
+    )
+    f0, b0, f1, b1, f2, b2 = range(2 * slots)
+
+    mirror_zero = mirrored(stacked(lay, (right_saved, right_cot), ((0, 0), (0,))))
+
+    rows_f0 = dispatch(lay, route(lay, tables, [(left_in[0], None, f0, False, None, None)]))
     sent = route(
         lay,
-        left_scalars,
+        tables,
         [
-            (left_saved[0], ids(1, 1), None, None),
-            (left_cot[0], ids(1, 1), gates(1, 1), None),
+            (left_saved[0], None, b1, False, None, None),
+            (left_cot[0], None, b1, True, None, None),
         ],
     )
     rows_b1 = dispatch(lay, sent)
     parts_f0 = exchange(lay, forward(lay, rows_f0, 0, weights))
-    left_zero = combine(lay, left_scalars, left_in[0], ids(0, 0), gates(0, 0), parts_f0)
+    parts, kept_b1 = backward(lay, rows_b1, 0, rows_b1, 1, weights)
+    parts_b1 = exchange(lay, parts)
+    left_zero = combine(lay, tables, f0, True, left_in[0], parts_f0)
     arriving = passed_along(left_zero, 1)
-
-    right_first = mirrored(right_in[0])
-    saved_two = mirrored(right_saved[1, 0])
 
     sent = route(
         lay,
-        right_scalars,
-        [(saved_zero, ids(0, 1), None, None), (cot_zero, ids(0, 1), gates(0, 1), None)],
+        tables,
+        [(mirror_zero, 0, b0, False, None, None), (mirror_zero, 1, b0, True, None, None)],
+        after=(left_zero,),
     )
     rows_b0 = dispatch(lay, sent)
-    parts, kept_b1 = backward(lay, rows_b1, 0, rows_b1, 1, weights)
-    parts_b1 = exchange(lay, parts)
-    back_one = combine(lay, right_scalars, left_cot[0], ids(1, 1), None, parts_b1)
+    mirror_one = mirrored(
+        stacked(lay, (right_in, right_saved), ((0,), (1, 0)), after=(sent[0],))
+    )
+    back_one = combine(lay, tables, b1, False, left_cot[0], parts_b1, after=(sent[0],))
+
+    sent = route(
+        lay, tables, [(arriving, None, f2, False, "first", left_new)], after=(rows_b0[1],)
+    )
+    rows_f2 = dispatch(lay, sent)
     parts, kept_b0 = backward(lay, rows_b0, 0, rows_b0, 1, weights)
     parts_b0 = exchange(lay, parts)
-    back_zero = combine(lay, right_scalars, cot_zero, ids(0, 1), None, parts_b0)
+    parts_f2 = exchange(lay, forward(lay, rows_f2, 0, weights, after=(parts[0],)))
+    back_zero = combine(lay, tables, b0, False, mirror_zero, parts_b0, lead=1)
     returning = passed_along(back_zero, -1)
 
     sent = route(
         lay,
-        right_scalars,
-        [(right_first, ids(1, 0), None, None), (saved_two, ids(2, 1), None, None)],
+        tables,
+        [(mirror_one, 0, f1, False, None, None), (mirror_one, 1, b2, False, None, None)],
+        after=(back_zero,),
     )
     rows_f1 = dispatch(lay, sent)
-    sent = route(lay, left_scalars, [(arriving, ids(2, 0), None, left_new)])
-    rows_f2 = dispatch(lay, sent)
-    parts_f2 = exchange(lay, forward(lay, rows_f2, 0, weights))
     left_out = combine(
-        lay, left_scalars, arriving, ids(2, 0), gates(2, 0), parts_f2, left_new, left_zero
-    )
-    parts_f1 = exchange(lay, forward(lay, rows_f1, 0, weights))
-    right_out = combine(lay, right_scalars, right_first, ids(1, 0), gates(1, 0), parts_f1)
-
-    sent = route(lay, right_scalars, [(returning, ids(2, 1), gates(2, 1), right_cot_new)])
+        lay,
+        tables,
+        f2,
+        True,
+        arriving,
+        parts_f2,
+        edge="first",
+        fresh=left_new,
+        first=left_zero,
+        after=(sent[0],),
+    )
+
+    sent = route(lay, tables, [(returning, None, b2, True, "last", right_cot_new)])
     cots_b2 = dispatch(lay, sent)
+    parts_f1 = exchange(lay, forward(lay, rows_f1, 0, weights, after=(sent[0],)))
     parts, kept_b2 = backward(lay, rows_f1, 1, cots_b2, 0, weights)
     parts_b2 = exchange(lay, parts)
+    right_out = combine(lay, tables, f1, True, mirror_one, parts_f1, lead=0, after=(parts[0],))
     grad_gate, grad_up, grad_down = gradients((kept_b0, kept_b1, kept_b2), half)
     right_back = combine(
-        lay, right_scalars, returning, ids(2, 1), None, parts_b2, right_cot_new, back_zero
+        lay,
+        tables,
+        b2,
+        False,
+        returning,
+        parts_b2,
+        edge="last",
+        fresh=right_cot_new,
+        first=back_zero,
     )
     return (
         left_out[:, None],

time: 176 us -> 136 us (0.77)
  the two profiles are of different devices: /device:TPU:10 before, /device:TPU:18 now
where the time goes in v2:
time: 136 us
  waiting for transfers between devices  57.9 us (43%)
  starting transfers between devices  44.5 us (33%)
  Pallas kernels  25.2 us (19%)
  local copies, waits for them, and re-layouts  7.28 us (5%)
    ppermute x36, waiting for transfers between devices, exchange(): got.append(lax.ppermute(by_distance[d], 'expert', pairs))  44.8 us
    ppermute x36, starting transfers between devices, exchange(): got.append(lax.ppermute(by_distance[d], 'expert', pairs))  38.7 us
    pallas_call x18, Pallas kernels, call(): pl.pallas_call(body, out_shape=outs, in_specs=specs, out_specs=[VMEM_SPEC...  19.2 us
    ppermute x2, waiting for transfers between devices, passed_along(): return lax.ppermute(value, 'section', pairs)  13.1 us
    unnamed x38, local copies, waits for them, and re-layouts  7.28 us
    pallas_call x1, Pallas kernels, gradients(): pl.pallas_call(functools.partial(gradient_kernel, passes), grid=(width //...  5.91 us
    ppermute x2, starting transfers between devices, passed_along(): return lax.ppermute(value, 'section', pairs)  5.68 us
  transfers between devices with their start and end apart: 40, of which 13 were waited for; matrix products, arithmetic and copies ran while one was open for 0% of the time, Pallas kernels for 18%

profile of v2, /device:TPU:18, one launch (start us, length us, event | category | flops | bytes accessed | tf_op | source)
XLA Modules:
  0.0 135.8 jit_solution(8940515346759770840)
XLA Ops:
  6.2 2.4 %collective-permute-start.2 = (bf16[1,32,2176]{2,1,0:T(8,128)(2,1)S(1)}, bf16[1,32,2176]{2,1,0:T(8,128)(2,1)S(1)}, u32[]{:S(2)}, u32[]{:S(2)}) collective-permute-start(bf16[1,32,2176]{2,1,0:T(8,128)(2,1)S(1)} %get-tuple-element.59), channel_id=1, source_target_pairs={{0,3},{1,2},{2,1},{3,0},{4,7},{5,6},{6,5},{7,4},{8,11},{9,10},{10,... | collective-permute-start | bytes 417800 | tf_op jit(solution)/shard_map/ppermute | solution.py:208
  9.1 3.0 %collective-permute-done.refs_1_ = bf16[1,32,2176]{2,1,0:T(8,128)(2,1)S(1)} collective-permute-done((bf16[1,32,2176]{2,1,0:T(8,128)(2,1)S(1)}, bf16[1,32,2176]{2,1,0:T(8,128)(2,1)S(1)}, u32[]{:S(2)}, u32[]{:S(2)}) %collective-permute-start) | collective-permute-done | bytes 139296 | tf_op jit(solution)/shard_map/ppermute | solution.py:208
  12.1 3.7 %collective-permute-done.2.refs_3_ = bf16[1,32,2176]{2,1,0:T(8,128)(2,1)S(1)} collective-permute-done((bf16[1,32,2176]{2,1,0:T(8,128)(2,1)S(1)}, bf16[1,32,2176]{2,1,0:T(8,128)(2,1)S(1)}, u32[]{:S(2)}, u32[]{:S(2)}) %collective-permute-start.2) | collective-permute-done | bytes 139296 | tf_op jit(solution)/shard_map/ppermute | solution.py:208
  22.8 1.6 %collective-permute-start.31 = (bf16[2,32,2176]{2,1,0:T(8,128)(2,1)S(1)}, bf16[2,32,2176]{2,1,0:T(8,128)(2,1)S(1)}, u32[]{:S(2)}, u32[]{:S(2)}) collective-permute-start(bf16[2,32,2176]{2,1,0:T(8,128)(2,1)S(1)} %get-tuple-element.85.refs_0_.refs_4_), channel_id=1, source_target_pairs={{0,1},{1,0},{2,3},{3,2},{4,5},{5,4},{6,7},{7,6},{8,9},{9,8},{10,11... | collective-permute-start | bytes 835592 | tf_op jit(solution)/shard_map/ppermute | solution.py:208
  25.9 2.1 %collective-permute-done.3.refs_4_ = bf16[1,32,2176]{2,1,0:T(8,128)(2,1)S(1)} collective-permute-done((bf16[1,32,2176]{2,1,0:T(8,128)(2,1)S(1)}, bf16[1,32,2176]{2,1,0:T(8,128)(2,1)S(1)}, u32[]{:S(2)}, u32[]{:S(2)}) %collective-permute-start.3) | collective-permute-done | bytes 139296 | tf_op jit(solution)/shard_map/ppermute | solution.py:208
  29.8 11.6 %collective-permute-done.5.refs_6_ = bf16[1,32,2176]{2,1,0:T(8,128)(2,1)S(1)} collective-permute-done((bf16[1,32,2176]{2,1,0:T(8,128)(2,1)S(1)}, bf16[1,32,2176]{2,1,0:T(8,128)(2,1)S(1)}, u32[]{:S(2)}, u32[]{:S(2)}) %collective-permute-start.5) | collective-permute-done | bytes 139296 | tf_op jit(solution)/shard_map/ppermute | solution.py:208
  42.2 1.6 %collective-permute-start.13 = (bf16[2,32,2176]{2,1,0:T(8,128)(2,1)S(1)}, bf16[2,32,2176]{2,1,0:T(8,128)(2,1)S(1)}, u32[]{:S(2)}, u32[]{:S(2)}) collective-permute-start(bf16[2,32,2176]{2,1,0:T(8,128)(2,1)S(1)} %get-tuple-element.67), channel_id=1, source_target_pairs={{0,3},{1,2},{2,1},{3,0},{4,7},{5,6},{6,5},{7,4},{8,11},{9,10},{10,... | collective-permute-start | bytes 835592 | tf_op jit(solution)/shard_map/ppermute | solution.py:208
  46.0 3.6 %collective-permute-start.6 = (bf16[64,2048]{1,0:T(8,128)(2,1)S(1)}, bf16[64,2048]{1,0:T(8,128)(2,1)S(1)}, u32[]{:S(2)}, u32[]{:S(2)}) collective-permute-start(bf16[64,2048]{1,0:T(8,128)(2,1)S(1)} %shard_map.182.refs_4_), channel_id=1, source_target_pairs={{0,4},{4,8},{8,12},{12,16},{16,20},{20,24},{24,28},{1,5},{5,9},{9,... | collective-permute-start | bytes 786440 | tf_op jit(solution)/shard_map/ppermute | solution.py:416
  49.6 2.6 %shard_map.197 = (bf16[1,32,2176]{2,1,0:T(8,128)(2,1)S(1)}, bf16[1,32,2176]{2,1,0:T(8,128)(2,1)S(1)}, bf16[1,32,2176]{2,1,0:T(8,128)(2,1)S(1)}, bf16[1,32,2176]{...) custom-call(bf16[2,32,2176]{2,1,0:T(8,128)(2,1)S(1)} %get-tuple-elem, ...), custom_call_target="tpu_custom_call" | custom-call | flops 1069547520 | bytes 9015296 | tf_op jit(solution)/shard_map/pallas_call | solution.py:140
  53.3 3.2 %collective-permute-done.12.refs_2_.refs_6_ = bf16[2,32,2176]{2,1,0:T(8,128)(2,1)S(1)} collective-permute-done((bf16[2,32,2176]{2,1,0:T(8,128)(2,1)S(1)}, bf16[2,32,2176]{2,1,0:T(8,128)(2,1)S(1)}, u32[]{:S(2)}, u32[]{:S(2)}) %collective-permute-start.12) | collective-permute-done | bytes 278560 | tf_op jit(solution)/shard_map/ppermute | solution.py:208
  56.4 2.6 %shard_map.186 = (bf16[1,32,2176]{2,1,0:T(8,128)(2,1)S(1)}, bf16[1,32,2176]{2,1,0:T(8,128)(2,1)S(1)}, bf16[1,32,2176]{2,1,0:T(8,128)(2,1)S(1)}, bf16[1,32,2176]{...) custom-call(bf16[2,32,2176]{2,1,0:T(8,128)(2,1)S(1)} %get-tuple-elem, ...), custom_call_target="tpu_custom_call" | custom-call | flops 1069547520 | bytes 9015296 | tf_op jit(solution)/shard_map/pallas_call | solution.py:140
  61.1 13.1 %collective-permute-done.6.refs_2_ = bf16[64,2048]{1,0:T(8,128)(2,1)S(1)} collective-permute-done((bf16[64,2048]{1,0:T(8,128)(2,1)S(1)}, bf16[64,2048]{1,0:T(8,128)(2,1)S(1)}, u32[]{:S(2)}, u32[]{:S(2)}) %collective-permute-start.6) | collective-permute-done | bytes 262176 | tf_op jit(solution)/shard_map/ppermute | solution.py:416
  79.6 2.2 %collective-permute-done.20.refs_6_ = bf16[1,32,2176]{2,1,0:T(8,128)(2,1)S(1)} collective-permute-done((bf16[1,32,2176]{2,1,0:T(8,128)(2,1)S(1)}, bf16[1,32,2176]{2,1,0:T(8,128)(2,1)S(1)}, u32[]{:S(2)}, u32[]{:S(2)}) %collective-permute-start.20) | collective-permute-done | bytes 139296 | tf_op jit(solution)/shard_map/ppermute | solution.py:208
  84.8 2.0 %collective-permute-start.23 = (bf16[2,32,2176]{2,1,0:T(8,128)(2,1)S(1)}, bf16[2,32,2176]{2,1,0:T(8,128)(2,1)S(1)}, u32[]{:S(2)}, u32[]{:S(2)}) collective-permute-start(bf16[2,32,2176]{2,1,0:T(8,128)(2,1)S(1)} %get-tuple-element.77), channel_id=1, source_target_pairs={{0,3},{1,2},{2,1},{3,0},{4,7},{5,6},{6,5},{7,4},{8,11},{9,10},{10,... | collective-permute-start | bytes 835592 | tf_op jit(solution)/shard_map/ppermute | solution.py:208
  86.8 1.8 %collective-permute-start.22 = (bf16[2,32,2176]{2,1,0:T(8,128)(2,1)S(1)}, bf16[2,32,2176]{2,1,0:T(8,128)(2,1)S(1)}, u32[]{:S(2)}, u32[]{:S(2)}) collective-permute-start(bf16[2,32,2176]{2,1,0:T(8,128)(2,1)S(1)} %get-tuple-element.77), channel_id=1, source_target_pairs={{0,2},{1,3},{2,0},{3,1},{4,6},{5,7},{6,4},{7,5},{8,10},{9,11},{10,... | collective-permute-start | bytes 835592 | tf_op jit(solution)/shard_map/ppermute | solution.py:208
  88.5 5.1 %collective-permute-done.10.refs_2_ = bf16[1,32,2176]{2,1,0:T(8,128)(2,1)S(1)} collective-permute-done((bf16[1,32,2176]{2,1,0:T(8,128)(2,1)S(1)}, bf16[1,32,2176]{2,1,0:T(8,128)(2,1)S(1)}, u32[]{:S(2)}, u32[]{:S(2)}) %collective-permute-start.10) | collective-permute-done | bytes 139296 | tf_op jit(solution)/shard_map/ppermute | solution.py:208
  93.6 2.1 %collective-permute-start.24 = (bf16[64,2048]{1,0:T(8,128)(2,1)S(1)}, bf16[64,2048]{1,0:T(8,128)(2,1)S(1)}, u32[]{:S(2)}, u32[]{:S(2)}) collective-permute-start(bf16[64,2048]{1,0:T(8,128)(2,1)S(1)} %shard_map.189.refs_4_), channel_id=1, source_target_pairs={{4,0},{8,4},{12,8},{16,12},{20,16},{24,20},{28,24},{5,1},{9,5},{13... | collective-permute-start | bytes 786440 | tf_op jit(solution)/shard_map/ppermute | solution.py:416
  97.1 6.0 %collective-permute-done.14.refs_6_ = bf16[1,32,2176]{2,1,0:T(8,128)(2,1)S(1)} collective-permute-done((bf16[1,32,2176]{2,1,0:T(8,128)(2,1)S(1)}, bf16[1,32,2176]{2,1,0:T(8,128)(2,1)S(1)}, u32[]{:S(2)}, u32[]{:S(2)}) %collective-permute-start.14) | collective-permute-done | bytes 139296 | tf_op jit(solution)/shard_map/ppermute | solution.py:208
  105.3 2.0 %collective-permute-start.30 = (bf16[1,32,2176]{2,1,0:T(8,128)(2,1)S(1)}, bf16[1,32,2176]{2,1,0:T(8,128)(2,1)S(1)}, u32[]{:S(2)}, u32[]{:S(2)}) collective-permute-start(bf16[1,32,2176]{2,1,0:T(8,128)(2,1)S(1)} %get-tuple-element.83), channel_id=1, source_target_pairs={{0,3},{1,2},{2,1},{3,0},{4,7},{5,6},{6,5},{7,4},{8,11},{9,10},{10,... | collective-permute-start | bytes 417800 | tf_op jit(solution)/shard_map/ppermute | solution.py:208
  110.1 5.6 %collective-permute-done.15.refs_7_ = bf16[1,32,2176]{2,1,0:T(8,128)(2,1)S(1)} collective-permute-done((bf16[1,32,2176]{2,1,0:T(8,128)(2,1)S(1)}, bf16[1,32,2176]{2,1,0:T(8,128)(2,1)S(1)}, u32[]{:S(2)}, u32[]{:S(2)}) %collective-permute-start.15) | collective-permute-done | bytes 139296 | tf_op jit(solution)/shard_map/ppermute | solution.py:208
  117.9 2.0 %collective-permute-start.26 = (bf16[1,32,2176]{2,1,0:T(8,128)(2,1)S(1)}, bf16[1,32,2176]{2,1,0:T(8,128)(2,1)S(1)}, u32[]{:S(2)}, u32[]{:S(2)}) collective-permute-start(bf16[1,32,2176]{2,1,0:T(8,128)(2,1)S(1)} %get-tuple-element.81), channel_id=1, source_target_pairs={{0,2},{1,3},{2,0},{3,1},{4,6},{5,7},{6,4},{7,5},{8,10},{9,11},{10,... | collective-permute-start | bytes 417800 | tf_op jit(solution)/shard_map/ppermute | solution.py:208
  121.4 2.6 %shard_map.194 = (bf16[1,32,2176]{2,1,0:T(8,128)(2,1)S(1)}, bf16[1,32,2176]{2,1,0:T(8,128)(2,1)S(1)}, bf16[1,32,2176]{2,1,0:T(8,128)(2,1)S(1)}, bf16[1,32,2176]{...) custom-call(bf16[2,32,2176]{2,1,0:T(8,128)(2,1)S(1)} %get-tuple-elem, ...), custom_call_target="tpu_custom_call" | custom-call | flops 1069547520 | bytes 8458240 | tf_op jit(solution)/shard_map/pallas_call | solution.py:140
  124.1 2.0 %collective-permute-start.38 = (bf16[1,32,2176]{2,1,0:T(8,128)(2,1)S(1)}, bf16[1,32,2176]{2,1,0:T(8,128)(2,1)S(1)}, u32[]{:S(2)}, u32[]{:S(2)}) collective-permute-start(bf16[1,32,2176]{2,1,0:T(8,128)(2,1)S(1)} %get-tuple-element.92), channel_id=1, source_target_pairs={{0,2},{1,3},{2,0},{3,1},{4,6},{5,7},{6,4},{7,5},{8,10},{9,11},{10,... | collective-permute-start | bytes 417800 | tf_op jit(solution)/shard_map/ppermute | solution.py:208
  127.6 5.9 %shard_map.200 = (bf16[2048,384]{1,0:T(8,128)(2,1)}, bf16[2048,384]{1,0:T(8,128)(2,1)}, bf16[384,2048]{1,0:T(8,128)(2,1)}) custom-call(bf16[144,2048]{1,0:T(8,128)(2,1)S(1)} %get-tuple-element.94.refs_0_, bf16[144,2048]{1,0:T(8,128)(2,1)S(1)} %get-tuple-element.95.refs_1_, bf16[144,2048]{1,0:T(8,128)(2,1)S(1)} %get-tuple-element.96.refs_2_, ...), custom_call_target="tpu_custom_call" | custom-call | flops 2038431744 | bytes 9252864 | tf_op jit(solution)/shard_map/pallas_call | solution.py:397
  (115 shorter events, 44.7 us)
Async XLA Ops:
  2.8 39.0 %collective-permute-start.7 = (bf16[2,64,2048]{2,1,0:T(8,128)(2,1)S(1)}, bf16[2,64,2048]{2,1,0:T(8,128)(2,1)S(1)}, u32[]{:S(2)}, u32[]{:S(2)}) collective-permute-start(bf16[2,64,2048]{2,1,0:T(8,128)(2,1)S(1)} %shard_map.183), channel_id=1, source_target_pairs={{0,28},{4,24},{8,20},{12,16},{16,12},{20,8},{24,4},{28,0},{1,29},{... | collective-permute-start | bytes 1572872 | tf_op jit(solution)/shard_map/ppermute | solution.py:410
  22.8 21.4 %collective-permute-start.31 = (bf16[2,32,2176]{2,1,0:T(8,128)(2,1)S(1)}, bf16[2,32,2176]{2,1,0:T(8,128)(2,1)S(1)}, u32[]{:S(2)}, u32[]{:S(2)}) collective-permute-start(bf16[2,32,2176]{2,1,0:T(8,128)(2,1)S(1)} %get-tuple-element.85.refs_0_.refs_4_), channel_id=1, source_target_pairs={{0,1},{1,0},{2,3},{3,2},{4,5},{5,4},{6,7},{7,6},{8,9},{9,8},{10,11... | collective-permute-start | bytes 835592 | tf_op jit(solution)/shard_map/ppermute | solution.py:208
  24.4 21.4 %collective-permute-start.33 = (bf16[2,32,2176]{2,1,0:T(8,128)(2,1)S(1)}, bf16[2,32,2176]{2,1,0:T(8,128)(2,1)S(1)}, u32[]{:S(2)}, u32[]{:S(2)}) collective-permute-start(bf16[2,32,2176]{2,1,0:T(8,128)(2,1)S(1)} %get-tuple-element.86), channel_id=1, source_target_pairs={{0,3},{1,2},{2,1},{3,0},{4,7},{5,6},{6,5},{7,4},{8,11},{9,10},{10,... | collective-permute-start | bytes 835592 | tf_op jit(solution)/shard_map/ppermute | solution.py:208
  28.0 18.0 %collective-permute-start.32 = (bf16[2,32,2176]{2,1,0:T(8,128)(2,1)S(1)}, bf16[2,32,2176]{2,1,0:T(8,128)(2,1)S(1)}, u32[]{:S(2)}, u32[]{:S(2)}) collective-permute-start(bf16[2,32,2176]{2,1,0:T(8,128)(2,1)S(1)} %get-tuple-element.86), channel_id=1, source_target_pairs={{0,2},{1,3},{2,0},{3,1},{4,6},{5,7},{6,4},{7,5},{8,10},{9,11},{10,... | collective-permute-start | bytes 835592 | tf_op jit(solution)/shard_map/ppermute | solution.py:208
  28.2 13.1 %collective-permute-start.5 = (bf16[1,32,2176]{2,1,0:T(8,128)(2,1)S(1)}, bf16[1,32,2176]{2,1,0:T(8,128)(2,1)S(1)}, u32[]{:S(2)}, u32[]{:S(2)}) collective-permute-start(bf16[1,32,2176]{2,1,0:T(8,128)(2,1)S(1)} %get-tuple-element.63), channel_id=1, source_target_pairs={{0,3},{1,2},{2,1},{3,0},{4,7},{5,6},{6,5},{7,4},{8,11},{9,10},{10,... | collective-permute-start | bytes 417800 | tf_op jit(solution)/shard_map/ppermute | solution.py:208
  43.8 12.7 %collective-permute-start.12 = (bf16[2,32,2176]{2,1,0:T(8,128)(2,1)S(1)}, bf16[2,32,2176]{2,1,0:T(8,128)(2,1)S(1)}, u32[]{:S(2)}, u32[]{:S(2)}) collective-permute-start(bf16[2,32,2176]{2,1,0:T(8,128)(2,1)S(1)} %get-tuple-element.67), channel_id=1, source_target_pairs={{0,2},{1,3},{2,0},{3,1},{4,6},{5,7},{6,4},{7,5},{8,10},{9,11},{10,... | collective-permute-start | bytes 835592 | tf_op jit(solution)/shard_map/ppermute | solution.py:208
  44.3 12.2 %collective-permute-start.8 = (bf16[2,32,2176]{2,1,0:T(8,128)(2,1)S(1)}, bf16[2,32,2176]{2,1,0:T(8,128)(2,1)S(1)}, u32[]{:S(2)}, u32[]{:S(2)}) collective-permute-start(bf16[2,32,2176]{2,1,0:T(8,128)(2,1)S(1)} %get-tuple-element.64.refs_0_.refs_4_.refs_2_.refs_7_), channel_id=1, source_target_pairs={{0,1},{1,0},{2,3},{3,2},{4,5},{5,4},{6,7},{7,6},{8,9},{9,8},{10,11... | collective-permute-start | bytes 835592 | tf_op jit(solution)/shard_map/ppermute | solution.py:208
  45.9 37.1 %collective-permute-start.17 = (bf16[2,64,2048]{2,1,0:T(8,128)(2,1)S(1)}, bf16[2,64,2048]{2,1,0:T(8,128)(2,1)S(1)}, u32[]{:S(2)}, u32[]{:S(2)}) collective-permute-start(bf16[2,64,2048]{2,1,0:T(8,128)(2,1)S(1)} %shard_map.188), channel_id=1, source_target_pairs={{0,28},{4,24},{8,20},{12,16},{16,12},{20,8},{24,4},{28,0},{1,29},{... | collective-permute-start | bytes 1572872 | tf_op jit(solution)/shard_map/ppermute | solution.py:410
  46.0 28.2 %collective-permute-start.6 = (bf16[64,2048]{1,0:T(8,128)(2,1)S(1)}, bf16[64,2048]{1,0:T(8,128)(2,1)S(1)}, u32[]{:S(2)}, u32[]{:S(2)}) collective-permute-start(bf16[64,2048]{1,0:T(8,128)(2,1)S(1)} %shard_map.182.refs_4_), channel_id=1, source_target_pairs={{0,4},{4,8},{8,12},{12,16},{16,20},{20,24},{24,28},{1,5},{5,9},{9,... | collective-permute-start | bytes 786440 | tf_op jit(solution)/shard_map/ppermute | solution.py:416
  52.8 23.2 %collective-permute-start.34 = (bf16[1,32,2176]{2,1,0:T(8,128)(2,1)S(1)}, bf16[1,32,2176]{2,1,0:T(8,128)(2,1)S(1)}, u32[]{:S(2)}, u32[]{:S(2)}) collective-permute-start(bf16[1,32,2176]{2,1,0:T(8,128)(2,1)S(1)} %get-tuple-element.88), channel_id=1, source_target_pairs={{0,1},{1,0},{2,3},{3,2},{4,5},{5,4},{6,7},{7,6},{8,9},{9,8},{10,11... | collective-permute-start | bytes 417800 | tf_op jit(solution)/shard_map/ppermute | solution.py:208
  59.0 17.6 %collective-permute-start.18 = (bf16[1,32,2176]{2,1,0:T(8,128)(2,1)S(1)}, bf16[1,32,2176]{2,1,0:T(8,128)(2,1)S(1)}, u32[]{:S(2)}, u32[]{:S(2)}) collective-permute-start(bf16[1,32,2176]{2,1,0:T(8,128)(2,1)S(1)} %get-tuple-element.73), channel_id=1, source_target_pairs={{0,1},{1,0},{2,3},{3,2},{4,5},{5,4},{6,7},{7,6},{8,9},{9,8},{10,11... | collective-permute-start | bytes 417800 | tf_op jit(solution)/shard_map/ppermute | solution.py:208
  60.6 17.5 %collective-permute-start.19 = (bf16[1,32,2176]{2,1,0:T(8,128)(2,1)S(1)}, bf16[1,32,2176]{2,1,0:T(8,128)(2,1)S(1)}, u32[]{:S(2)}, u32[]{:S(2)}) collective-permute-start(bf16[1,32,2176]{2,1,0:T(8,128)(2,1)S(1)} %get-tuple-element.74), channel_id=1, source_target_pairs={{0,2},{1,3},{2,0},{3,1},{4,6},{5,7},{6,4},{7,5},{8,10},{9,11},{10,... | collective-permute-start | bytes 417800 | tf_op jit(solution)/shard_map/ppermute | solution.py:208
  81.8 11.8 %collective-permute-start.10 = (bf16[1,32,2176]{2,1,0:T(8,128)(2,1)S(1)}, bf16[1,32,2176]{2,1,0:T(8,128)(2,1)S(1)}, u32[]{:S(2)}, u32[]{:S(2)}) collective-permute-start(bf16[1,32,2176]{2,1,0:T(8,128)(2,1)S(1)} %get-tuple-element.66), channel_id=1, source_target_pairs={{0,2},{1,3},{2,0},{3,1},{4,6},{5,7},{6,4},{7,5},{8,10},{9,11},{10,... | collective-permute-start | bytes 417800 | tf_op jit(solution)/shard_map/ppermute | solution.py:208
  82.9 14.1 %collective-permute-start.36 = (bf16[1,32,2176]{2,1,0:T(8,128)(2,1)S(1)}, bf16[1,32,2176]{2,1,0:T(8,128)(2,1)S(1)}, u32[]{:S(2)}, u32[]{:S(2)}) collective-permute-start(bf16[1,32,2176]{2,1,0:T(8,128)(2,1)S(1)} %get-tuple-element.90), channel_id=1, source_target_pairs={{0,3},{1,2},{2,1},{3,0},{4,7},{5,6},{6,5},{7,4},{8,11},{9,10},{10,... | collective-permute-start | bytes 417800 | tf_op jit(solution)/shard_map/ppermute | solution.py:208
  84.8 20.5 %collective-permute-start.23 = (bf16[2,32,2176]{2,1,0:T(8,128)(2,1)S(1)}, bf16[2,32,2176]{2,1,0:T(8,128)(2,1)S(1)}, u32[]{:S(2)}, u32[]{:S(2)}) collective-permute-start(bf16[2,32,2176]{2,1,0:T(8,128)(2,1)S(1)} %get-tuple-element.77), channel_id=1, source_target_pairs={{0,3},{1,2},{2,1},{3,0},{4,7},{5,6},{6,5},{7,4},{8,11},{9,10},{10,... | collective-permute-start | bytes 835592 | tf_op jit(solution)/shard_map/ppermute | solution.py:208
  86.8 20.5 %collective-permute-start.22 = (bf16[2,32,2176]{2,1,0:T(8,128)(2,1)S(1)}, bf16[2,32,2176]{2,1,0:T(8,128)(2,1)S(1)}, u32[]{:S(2)}, u32[]{:S(2)}) collective-permute-start(bf16[2,32,2176]{2,1,0:T(8,128)(2,1)S(1)} %get-tuple-element.77), channel_id=1, source_target_pairs={{0,2},{1,3},{2,0},{3,1},{4,6},{5,7},{6,4},{7,5},{8,10},{9,11},{10,... | collective-permute-start | bytes 835592 | tf_op jit(solution)/shard_map/ppermute | solution.py:208
  88.5 20.0 %collective-permute-start.21 = (bf16[2,32,2176]{2,1,0:T(8,128)(2,1)S(1)}, bf16[2,32,2176]{2,1,0:T(8,128)(2,1)S(1)}, u32[]{:S(2)}, u32[]{:S(2)}) collective-permute-start(bf16[2,32,2176]{2,1,0:T(8,128)(2,1)S(1)} %get-tuple-element.76.refs_9_.refs_0_), channel_id=1, source_target_pairs={{0,1},{1,0},{2,3},{3,2},{4,5},{5,4},{6,7},{7,6},{8,9},{9,8},{10,11... | collective-permute-start | bytes 835592 | tf_op jit(solution)/shard_map/ppermute | solution.py:208
  103.1 12.5 %collective-permute-start.15 = (bf16[1,32,2176]{2,1,0:T(8,128)(2,1)S(1)}, bf16[1,32,2176]{2,1,0:T(8,128)(2,1)S(1)}, u32[]{:S(2)}, u32[]{:S(2)}) collective-permute-start(bf16[1,32,2176]{2,1,0:T(8,128)(2,1)S(1)} %get-tuple-element.71), channel_id=1, source_target_pairs={{0,2},{1,3},{2,0},{3,1},{4,6},{5,7},{6,4},{7,5},{8,10},{9,11},{10,... | collective-permute-start | bytes 417800 | tf_op jit(solution)/shard_map/ppermute | solution.py:208
  103.9 12.8 %collective-permute-start.16 = (bf16[1,32,2176]{2,1,0:T(8,128)(2,1)S(1)}, bf16[1,32,2176]{2,1,0:T(8,128)(2,1)S(1)}, u32[]{:S(2)}, u32[]{:S(2)}) collective-permute-start(bf16[1,32,2176]{2,1,0:T(8,128)(2,1)S(1)} %get-tuple-element.72), channel_id=1, source_target_pairs={{0,3},{1,2},{2,1},{3,0},{4,7},{5,6},{6,5},{7,4},{8,11},{9,10},{10,... | collective-permute-start | bytes 417800 | tf_op jit(solution)/shard_map/ppermute | solution.py:208
  105.3 14.7 %collective-permute-start.30 = (bf16[1,32,2176]{2,1,0:T(8,128)(2,1)S(1)}, bf16[1,32,2176]{2,1,0:T(8,128)(2,1)S(1)}, u32[]{:S(2)}, u32[]{:S(2)}) collective-permute-start(bf16[1,32,2176]{2,1,0:T(8,128)(2,1)S(1)} %get-tuple-element.83), channel_id=1, source_target_pairs={{0,3},{1,2},{2,1},{3,0},{4,7},{5,6},{6,5},{7,4},{8,11},{9,10},{10,... | collective-permute-start | bytes 417800 | tf_op jit(solution)/shard_map/ppermute | solution.py:208
  107.3 14.1 %collective-permute-start.29 = (bf16[1,32,2176]{2,1,0:T(8,128)(2,1)S(1)}, bf16[1,32,2176]{2,1,0:T(8,128)(2,1)S(1)}, u32[]{:S(2)}, u32[]{:S(2)}) collective-permute-start(bf16[1,32,2176]{2,1,0:T(8,128)(2,1)S(1)} %get-tuple-element.83), channel_id=1, source_target_pairs={{0,2},{1,3},{2,0},{3,1},{4,6},{5,7},{6,4},{7,5},{8,10},{9,11},{10,... | collective-permute-start | bytes 417800 | tf_op jit(solution)/shard_map/ppermute | solution.py:208
  108.5 12.9 %collective-permute-start.28 = (bf16[1,32,2176]{2,1,0:T(8,128)(2,1)S(1)}, bf16[1,32,2176]{2,1,0:T(8,128)(2,1)S(1)}, u32[]{:S(2)}, u32[]{:S(2)}) collective-permute-start(bf16[1,32,2176]{2,1,0:T(8,128)(2,1)S(1)} %get-tuple-element.78.refs_7_.refs_4_), channel_id=1, source_target_pairs={{0,1},{1,0},{2,3},{3,2},{4,5},{5,4},{6,7},{7,6},{8,9},{9,8},{10,11... | collective-permute-start | bytes 417800 | tf_op jit(solution)/shard_map/ppermute | solution.py:208
  117.9 15.5 %collective-permute-start.26 = (bf16[1,32,2176]{2,1,0:T(8,128)(2,1)S(1)}, bf16[1,32,2176]{2,1,0:T(8,128)(2,1)S(1)}, u32[]{:S(2)}, u32[]{:S(2)}) collective-permute-start(bf16[1,32,2176]{2,1,0:T(8,128)(2,1)S(1)} %get-tuple-element.81), channel_id=1, source_target_pairs={{0,2},{1,3},{2,0},{3,1},{4,6},{5,7},{6,4},{7,5},{8,10},{9,11},{10,... | collective-permute-start | bytes 417800 | tf_op jit(solution)/shard_map/ppermute | solution.py:208
  119.9 13.6 %collective-permute-start.27 = (bf16[1,32,2176]{2,1,0:T(8,128)(2,1)S(1)}, bf16[1,32,2176]{2,1,0:T(8,128)(2,1)S(1)}, u32[]{:S(2)}, u32[]{:S(2)}) collective-permute-start(bf16[1,32,2176]{2,1,0:T(8,128)(2,1)S(1)} %get-tuple-element.82), channel_id=1, source_target_pairs={{0,3},{1,2},{2,1},{3,0},{4,7},{5,6},{6,5},{7,4},{8,11},{9,10},{10,... | collective-permute-start | bytes 417800 | tf_op jit(solution)/shard_map/ppermute | solution.py:208
  (35 other events, 300.7 us)

commit v3 on v2

v3 whole, which is shorter than its diff:
```python
import functools

import jax
import jax.numpy as jnp
from jax import lax
from jax.experimental import pallas as pl
from jax.experimental.pallas import tpu as pltpu
from jax.sharding import PartitionSpec as P

LANES = 128
F32 = jnp.float32
BF16 = jnp.bfloat16
MIB = 1024 * 1024


class Layout:
    def __init__(self, peers, tokens, width):
        self.peers = peers
        self.experts = peers // 2
        self.tokens = tokens
        self.width = width
        self.cap = min(tokens, 2 * ((tokens // self.experts + 1) // 2) + 2)
        self.main = self.cap // 8 * 8
        self.extra = self.cap - self.main
        self.slabs = width // LANES
        self.per_group = self.main // self.extra if self.extra else 1
        self.groups = -(-self.slabs // self.per_group) if self.extra else 0
        self.packed = width + self.groups * LANES
        self.slots = -(-(self.experts * self.cap) // 16) * 16
        self.rows = peers * self.cap
        self.rows_held = -(-self.rows // 16) * 16


def slab_place(lay, slab):
    group, at = divmod(slab, lay.per_group)
    return at * lay.extra, lay.width + group * LANES


def pack_extra(lay, rows, start, out_ref, lead, stage):
    if not lay.extra:
        return
    if lay.slabs % lay.per_group:
        stage[...] = jnp.zeros_like(stage)
    part = rows[start : start + lay.extra, :]
    for slab in range(lay.slabs):
        row, col = slab_place(lay, slab)
        stage[row : row + lay.extra, col - lay.width : col - lay.width + LANES] = part[
            :, slab * LANES : (slab + 1) * LANES
        ]
    out_ref[lead, :, lay.width :] = stage[...].astype(BF16)


def unpack_extra(lay, packed, stage, into, row_at):
    stage[...] = packed
    for slab in range(lay.slabs):
        row, col = slab_place(lay, slab)
        into[row_at : row_at + lay.extra, slab * LANES : (slab + 1) * LANES] = stage[
            row : row + lay.extra, col - lay.width : col - lay.width + LANES
        ]


def stacked_main(lay, blocks):
    if lay.main % 16:
        return jnp.concatenate([b.astype(F32) for b in blocks], axis=0).astype(BF16)
    return jnp.concatenate(blocks, axis=0)


def as_column(row):
    square = (row.shape[1], row.shape[1])
    down = lax.broadcasted_iota(jnp.int32, square, 0)
    across = lax.broadcasted_iota(jnp.int32, square, 1)
    return jnp.sum(jnp.where(down == across, row, jnp.zeros_like(row)), axis=1, keepdims=True)


def slot_onehot(lay, ids_row):
    tokens = lay.tokens
    own_expert = lax.axis_index("expert") // 2
    down = lax.broadcasted_iota(jnp.int32, (tokens, tokens), 0)
    across = lax.broadcasted_iota(jnp.int32, (tokens, tokens), 1)
    earlier = jnp.logical_and(as_column(ids_row) == ids_row, down < across)
    rank = jnp.sum(earlier.astype(jnp.int32), axis=0, keepdims=True)
    near = ids_row ^ own_expert
    slot = jnp.where(
        rank < lay.main,
        near * lay.main + rank,
        lay.experts * lay.main + near * lay.extra + rank - lay.main,
    )
    place = lax.broadcasted_iota(jnp.int32, (lay.slots, tokens), 0)
    return (place == slot).astype(F32).astype(BF16)


def stage_shape(lay):
    return pltpu.VMEM((lay.main, max(1, lay.groups) * LANES), F32)


def at_edge(edge):
    last = lax.axis_size("section") - 1
    return lax.axis_index("section") == (0 if edge == "first" else last)


def route_kernel(lay, plan, groups, loads, *refs):
    inputs = sum(1 if edge is None else 2 for *_, edge in plan)
    ids, gates = refs[inputs : inputs + 2]
    outs = refs[inputs + 2 : inputs + 2 + len(groups) * lay.experts]
    scratch = refs[inputs + 2 + len(outs) :]
    stage = scratch[0]
    copies = []
    for i in range(loads):
        copies.append(pltpu.make_async_copy(refs[i], scratch[1].at[i], scratch[2].at[i]))
        copies[-1].start()
    onehots = {which: slot_onehot(lay, ids[which]) for which, *_ in plan}

    def read(at, lead):
        if loads:
            copies[at].wait()
            return scratch[1][at]
        return refs[at][...] if lead is None else refs[at][lead]

    at = 0
    places = [(g, lead) for g, size in enumerate(groups) for lead in range(size)]
    for (group, place), (which, lead, scaled, edge) in zip(places, plan):
        tokens = read(at, lead)
        at += 1
        if edge is not None:
            tokens = jnp.where(at_edge(edge), read(at, None), tokens)
            at += 1
        if scaled:
            tokens = (as_column(gates[which]) * tokens.astype(F32)).astype(BF16)
        rows = jnp.dot(onehots[which], tokens, preferred_element_type=F32)
        for j in range(lay.experts):
            out = outs[group * lay.experts + j]
            out[place, :, : lay.width] = rows[j * lay.main : (j + 1) * lay.main].astype(BF16)
            pack_extra(lay, rows, lay.experts * lay.main + j * lay.extra, out, place, stage)


VMEM_SPEC = pl.BlockSpec(memory_space=pltpu.VMEM)
ANY_SPEC = pl.BlockSpec(memory_space=pl.ANY)
HBM_SPEC = pl.BlockSpec(memory_space=pltpu.HBM)


def cost(flops, arrays):
    moved = sum(a.size * a.dtype.itemsize for a in arrays)
    return pl.CostEstimate(flops=int(flops), bytes_accessed=int(moved), transcendentals=0)


class Chain:
    def __init__(self):
        self.last = ()


def call(chain, kernel, args, outs, scratch, flops, limit, in_hbm=0):
    after = chain.last
    specs = [HBM_SPEC] * in_hbm + [VMEM_SPEC] * (len(args) - in_hbm) + [ANY_SPEC] * len(after)

    def body(*refs):
        kernel(*refs[: len(args)], *refs[len(args) + len(after) :])

    got = pl.pallas_call(
        body,
        out_shape=outs,
        in_specs=specs,
        out_specs=[VMEM_SPEC] * len(outs),
        scratch_shapes=scratch,
        compiler_params=pltpu.CompilerParams(vmem_limit_bytes=limit * MIB),
        cost_estimate=cost(flops, list(args) + list(outs)),
    )(*args, *after)
    chain.last = (got[0],)
    return got


def route(lay, chain, tables, items, groups, in_hbm=False, limit=10):
    args = []
    plan = []
    for tokens, lead, which, scaled, edge, fresh in items:
        args.append(tokens)
        if fresh is not None:
            args.append(fresh)
        plan.append((which, lead, scaled, edge))
    loads = len(args) if in_hbm else 0
    outs = [
        jax.ShapeDtypeStruct((size, lay.main, lay.packed), BF16)
        for size in groups
        for _ in range(lay.experts)
    ]
    scratch = [stage_shape(lay)]
    if loads:
        scratch += [
            pltpu.VMEM((loads, lay.tokens, lay.width), BF16),
            pltpu.SemaphoreType.DMA((loads,)),
        ]
    got = call(
        chain,
        functools.partial(route_kernel, lay, tuple(plan), tuple(groups), loads),
        args + list(tables),
        outs,
        scratch,
        2 * lay.slots * lay.tokens * lay.width * len(items),
        limit,
        loads,
    )
    return [got[g * lay.experts : (g + 1) * lay.experts] for g in range(len(groups))]


def stack_kernel(picks, *refs):
    count = len(picks)
    out, sems = refs[count], refs[count + 1]
    copies = []
    for at, pick in enumerate(picks):
        source = refs[at]
        for i in pick:
            source = source.at[i]
        copies.append(pltpu.make_async_copy(source, out.at[at], sems.at[at]))
    for copy in copies:
        copy.start()
    for copy in copies:
        copy.wait()


def stacked(lay, chain, arrays, picks, limit=4):
    count = len(arrays)
    out = jax.ShapeDtypeStruct((count, lay.tokens, lay.width), BF16)
    scratch = [pltpu.SemaphoreType.DMA((count,))]
    kernel = functools.partial(stack_kernel, tuple(picks))
    return call(chain, kernel, arrays, [out], scratch, 0, limit, count)[0]


def swapped(lay, value, bits):
    return lax.ppermute(value, "expert", [(i, i ^ bits) for i in range(lay.peers)])


def dispatch(lay, payloads, direct=False):
    got = []
    for j, payload in enumerate(payloads):
        here = payload if j == 0 else swapped(lay, payload, 2 * j)
        over = swapped(lay, payload, 2 * j + 1) if direct else swapped(lay, here, 1)
        got += [here, over]
    return got


def add_kernel(left, right, out):
    out[...] = (left[...].astype(F32) + right[...].astype(F32)).astype(BF16)


def handed_over(lay, parts, direct=False):
    if direct:
        return [parts[0]] + [swapped(lay, parts[d], d) for d in range(1, lay.peers)]
    return [swapped(lay, parts[2 * j + 1], 1) for j in range(lay.experts)]


def summed(lay, chain, parts, others):
    if len(others) == lay.peers:
        return others
    totals = []
    for j in range(1, lay.experts):
        other = others[j]
        out = jax.ShapeDtypeStruct(other.shape, BF16)
        total = call(chain, add_kernel, [parts[2 * j], other], [out], [], 2 * other.size, 4)[0]
        totals.append(swapped(lay, total, 2 * j))
    return [parts[0], others[0]] + totals


def load_rows(lay, refs, lead, stage, extra_rows):
    main = stacked_main(lay, [r[lead, :, : lay.width] for r in refs])
    if not lay.extra:
        return main
    extra_rows[...] = jnp.zeros_like(extra_rows)
    for d, ref in enumerate(refs):
        unpack_extra(lay, ref[lead, :, lay.width :].astype(F32), stage, extra_rows, d * lay.extra)
    return jnp.concatenate([main, extra_rows[...].astype(BF16)], axis=0)


def store_parts(lay, rows, refs, lead, stage):
    for d, ref in enumerate(refs):
        ref[lead, :, : lay.width] = rows[d * lay.main : (d + 1) * lay.main].astype(BF16)
        pack_extra(lay, rows, lay.peers * lay.main + d * lay.extra, ref, lead, stage)


def extra_shape(lay):
    return pltpu.VMEM((lay.rows_held - lay.peers * lay.main, lay.width), F32)


NT = (((1,), (1,)), ((), ()))
TN = (((0,), (0,)), ((), ()))


def expert_kernel(lay, tasks, groups, *refs):
    n = lay.peers
    blocks = [refs[g * n : (g + 1) * n] for g in range(groups)]
    at = groups * n
    w_gate, w_up, w_down = refs[at : at + 3]
    outs = refs[at + 3 : at + 3 + n]
    kept = refs[at + 3 + n : len(refs) - 2]
    stage, extra_rows = refs[len(refs) - 2 :]
    for task, (kind, *sources) in enumerate(tasks):
        held = [load_rows(lay, blocks[g], lead, stage, extra_rows) for g, lead in sources]
        rows = held[0]
        gate = jnp.dot(rows, w_gate[...], preferred_element_type=F32)
        up = jnp.dot(rows, w_up[...], preferred_element_type=F32)
        logistic = jax.nn.sigmoid(gate)
        swish = gate * logistic
        hidden = (swish * up).astype(BF16)
        if kind == "forward":
            part = jnp.dot(hidden, w_down[...], preferred_element_type=F32)
            store_parts(lay, part, outs, task, stage)
            continue
        row_cot = held[1]
        d_hidden = lax.dot_general(row_cot, w_down[...], NT, preferred_element_type=F32)
        d_gate = (d_hidden * up * logistic * (1.0 + gate * (1.0 - logistic))).astype(BF16)
        d_up = (d_hidden * swish).astype(BF16)
        back = lax.dot_general(d_gate, w_gate[...], NT, preferred_element_type=F32)
        back = back + lax.dot_general(d_up, w_up[...], NT, preferred_element_type=F32)
        store_parts(lay, back, outs, task, stage)
        rows_out, cot_out, both_out, hidden_out = kept[:4]
        kept = kept[4:]
        half = d_gate.shape[1]
        rows_out[...] = rows
        cot_out[...] = row_cot
        both_out[:, :half] = d_gate
        both_out[:, half:] = d_up
        hidden_out[...] = hidden


def run_experts(lay, chain, tasks, groups, weights):
    half = weights[0].shape[1]
    out = jax.ShapeDtypeStruct((len(tasks), lay.main, lay.packed), BF16)
    wide = jax.ShapeDtypeStruct((lay.rows_held, lay.width), BF16)
    both = jax.ShapeDtypeStruct((lay.rows_held, 2 * half), BF16)
    narrow = jax.ShapeDtypeStruct((lay.rows_held, half), BF16)
    backs = sum(task[0] == "backward" for task in tasks)
    products = 3 * (len(tasks) - backs) + 5 * backs
    got = call(
        chain,
        functools.partial(expert_kernel, lay, tuple(tasks), len(groups)),
        [block for group in groups for block in group] + list(weights),
        [out] * lay.peers + [wide, wide, both, narrow] * backs,
        [stage_shape(lay), extra_shape(lay)],
        2 * products * lay.rows * lay.width * half,
        20,
    )
    kept = got[lay.peers :]
    return got[: lay.peers], [tuple(kept[4 * i : 4 * i + 4]) for i in range(backs)]


def mixed_tokens(lay, tokens, parts, task, ids_row, gates_row, stage, extra_rows):
    pairs = [[parts[0], parts[1]]]
    if len(parts) == lay.peers:
        pairs += [[parts[2 * j], parts[2 * j + 1]] for j in range(1, lay.experts)]
    else:
        pairs += [[part] for part in parts[2:]]
    mains = []
    if lay.extra:
        extra_rows[...] = jnp.zeros_like(extra_rows)
    for j in range(lay.experts):
        total = functools.reduce(jnp.add, [part[task].astype(F32) for part in pairs[j]])
        mains.append(total[:, : lay.width].astype(BF16))
        if lay.extra:
            unpack_extra(lay, total[:, lay.width :], stage, extra_rows, j * lay.extra)
    outputs = stacked_main(lay, mains)
    if lay.slots > lay.experts * lay.main:
        outputs = jnp.concatenate([outputs, extra_rows[...].astype(BF16)], axis=0)
    onehot = slot_onehot(lay, ids_row)
    picked = lax.dot_general(onehot, outputs, TN, preferred_element_type=F32)
    if gates_row is not None:
        picked = picked * as_column(gates_row)
    return (tokens.astype(F32) + picked).astype(BF16)


def combine_kernel(lay, which, lead, scaled, edge, has_first, task, ids, gates, tokens_ref, *refs):
    at = 0
    tokens = tokens_ref[...] if lead is None else tokens_ref[lead]
    if edge is not None:
        tokens = jnp.where(at_edge(edge), refs[at][...], tokens)
        at += 1
    if has_first:
        first = refs[at]
        at += 1
    parts = refs[at : len(refs) - 3]
    out, stage, extra_rows = refs[len(refs) - 3 :]
    gates_row = gates[which] if scaled else None
    mixed = mixed_tokens(lay, tokens, parts, task, ids[which], gates_row, stage, extra_rows)
    if has_first:
        out[0] = first[...]
        out[1] = mixed
    else:
        out[...] = mixed


def combine(
    lay,
    chain,
    tables,
    which,
    scaled,
    tokens,
    parts,
    task,
    lead=None,
    edge=None,
    fresh=None,
    first=None,
):
    args = list(tables) + [tokens]
    if fresh is not None:
        args.append(fresh)
    if first is not None:
        args.append(first)
    args += list(parts)
    shape = (lay.tokens, lay.width)
    if first is not None:
        shape = (2,) + shape
    spare = max(8, lay.slots - lay.experts * lay.main)
    return call(
        chain,
        functools.partial(
            combine_kernel, lay, which, lead, scaled, edge, first is not None, task
        ),
        args,
        [jax.ShapeDtypeStruct(shape, BF16)],
        [stage_shape(lay), pltpu.VMEM((spare, lay.width), F32)],
        2 * lay.slots * lay.tokens * lay.width,
        8,
    )[0]


def all_gradients_kernel(passes, *refs):
    rows, cots, both, hidden = (
        jnp.concatenate([r[...] for r in refs[i * passes : (i + 1) * passes]], axis=0)
        for i in range(4)
    )
    grad_gate, grad_up, grad_down = refs[4 * passes :]
    half = hidden.shape[1]

    total = lax.dot_general(rows, both, TN, preferred_element_type=F32)
    grad_gate[...] = total[:, :half].astype(BF16)
    grad_up[...] = total[:, half:].astype(BF16)
    grad_down[...] = lax.dot_general(hidden, cots, TN, preferred_element_type=F32).astype(BF16)


def all_gradients(chain, kept):
    after = chain.last
    passes = len(kept)
    held, width = kept[0][0].shape
    half = kept[0][3].shape[1]
    tile = 4 * LANES if width % (4 * LANES) == 0 else width
    args = [k[i] for i in range(4) for k in kept]
    wide = pl.BlockSpec((held, tile), lambda i: (0, i))
    both = pl.BlockSpec((held, 2 * half), lambda i: (0, 0))
    narrow = pl.BlockSpec((held, half), lambda i: (0, 0))
    tall = pl.BlockSpec((tile, half), lambda i: (i, 0))
    flat = pl.BlockSpec((half, tile), lambda i: (0, i))
    outs = [
        jax.ShapeDtypeStruct((width, half), BF16),
        jax.ShapeDtypeStruct((width, half), BF16),
        jax.ShapeDtypeStruct((half, width), BF16),
    ]

    def body(*refs):
        all_gradients_kernel(passes, *refs[: len(args)], *refs[len(args) + len(after) :])

    return pl.pallas_call(
        body,
        grid=(width // tile,),
        out_shape=outs,
        in_specs=[wide] * (2 * passes) + [both] * passes + [narrow] * passes
        + [ANY_SPEC] * len(after),
        out_specs=[tall, tall, flat],
        compiler_params=pltpu.CompilerParams(vmem_limit_bytes=20 * MIB),
        cost_estimate=cost(2 * 3 * passes * held * width * half, args + outs),
    )(*args, *after)


def opening_kernel(lay, plan, groups, picks, *refs):
    loads, stacks = len(plan), len(picks)
    tokens_in, ids_in, gates_in = refs[:loads], refs[loads], refs[loads + 1]
    stacked_in = refs[loads + 2 : loads + 2 + stacks]
    stack_out = refs[loads + 2 + stacks]
    outs = refs[loads + 3 + stacks : loads + 3 + stacks + len(groups) * lay.experts]
    stage, held, ids, gates, sems = refs[loads + 3 + stacks + len(outs) :]
    places = [(g, lead) for g, size in enumerate(groups) for lead in range(size)]
    sources = []
    for at, pick in enumerate(picks):
        source = stacked_in[at]
        for i in pick:
            source = source.at[i]
        sources.append(source)
    copies = [
        pltpu.make_async_copy(ids_in, ids, sems.at[0]),
        pltpu.make_async_copy(gates_in, gates, sems.at[1]),
    ]
    copies += [
        pltpu.make_async_copy(tokens_in[i], held.at[i], sems.at[2 + i]) for i in range(loads)
    ]
    copies += [
        pltpu.make_async_copy(source, stack_out.at[at], sems.at[2 + loads + at])
        for at, source in enumerate(sources)
    ]
    for copy in copies:
        copy.start()
    copies[0].wait()
    copies[1].wait()
    onehots = {which: slot_onehot(lay, ids[which]) for which, _ in plan}
    for at, ((group, place), (which, scaled)) in enumerate(zip(places, plan)):
        copies[2 + at].wait()
        tokens = held[at]
        if scaled:
            tokens = (as_column(gates[which]) * tokens.astype(F32)).astype(BF16)
        rows = jnp.dot(onehots[which], tokens, preferred_element_type=F32)
        for j, out in enumerate(outs[group * lay.experts : (group + 1) * lay.experts]):
            out[place, :, : lay.width] = rows[j * lay.main : (j + 1) * lay.main].astype(BF16)
            pack_extra(lay, rows, lay.experts * lay.main + j * lay.extra, out, place, stage)
    for copy in copies[2 + loads :]:
        copy.wait()


def opening(lay, chain, tables, items, groups, arrays, picks, limit):
    stack = jax.ShapeDtypeStruct((len(arrays), lay.tokens, lay.width), BF16)
    payloads = [
        jax.ShapeDtypeStruct((size, lay.main, lay.packed), BF16)
        for size in groups
        for _ in range(lay.experts)
    ]
    plan = tuple((which, scaled) for _, which, scaled in items)
    args = [tokens for tokens, _, _ in items] + list(tables) + list(arrays)
    outs = [stack] + payloads
    got = pl.pallas_call(
        functools.partial(opening_kernel, lay, plan, tuple(groups), tuple(picks)),
        out_shape=outs,
        in_specs=[HBM_SPEC] * len(args),
        out_specs=[VMEM_SPEC] * len(outs),
        scratch_shapes=[
            stage_shape(lay),
            pltpu.VMEM((len(items), lay.tokens, lay.width), BF16),
            pltpu.VMEM(tables[0].shape, jnp.int32),
            pltpu.VMEM(tables[1].shape, F32),
            pltpu.SemaphoreType.DMA((2 + len(items) + len(arrays),)),
        ],
        compiler_params=pltpu.CompilerParams(vmem_limit_bytes=limit * MIB),
        cost_estimate=cost(2 * lay.slots * lay.tokens * lay.width * len(items), args + outs),
    )(*args)
    chain.last = (got[1],)
    each = [got[1 + g * lay.experts : 1 + (g + 1) * lay.experts] for g in range(len(groups))]
    return got[0], each


def mirrored(value):
    count = lax.axis_size("section")
    return lax.ppermute(value, "section", [(i, count - 1 - i) for i in range(count)])


def passed_along(value, by):
    count = lax.axis_size("section")
    pairs = [(i, i + by) for i in range(count) if 0 <= i + by < count]
    return lax.ppermute(value, "section", pairs)


def per_device(
    left_in,
    left_new,
    left_saved,
    left_cot,
    right_in,
    right_saved,
    right_cot,
    right_cot_new,
    expert_ids,
    gate_values,
    w_gate,
    w_up,
    w_down,
):
    peers = lax.axis_size("expert")
    tokens, width = left_in.shape[1:]
    assert expert_ids.shape[-1] == 1
    lay = Layout(peers, tokens, width)
    slots = expert_ids.shape[0]
    tables = (
        expert_ids.reshape(2 * slots, 1, tokens),
        gate_values.reshape(2 * slots, 1, tokens),
    )
    f0, b0, f1, b1, f2, b2 = range(2 * slots)

    chain = Chain()
    weights = (w_gate[0, 0], w_up[0, 0], w_down[0, 0])
    left_first, cot_first, left_fresh, cot_fresh = left_in[0], left_cot[0], left_new, right_cot_new
    stack_zero, (sent_f0, sent_b1) = opening(
        lay,
        chain,
        tables,
        [(left_in[0], f0, False), (left_saved[0], b1, False), (left_cot[0], b1, True)],
        (1, 2),
        [right_saved, right_cot],
        [(0, 0), (0,)],
        56,
    )
    mirror_zero = mirrored(stack_zero)
    rows_f0 = dispatch(lay, sent_f0, True)
    rows_b1 = dispatch(lay, sent_b1, True)
    parts_f0, _ = run_experts(lay, chain, [("forward", (0, 0))], [rows_f0], weights)
    over_f0 = handed_over(lay, parts_f0, False)
    (sent_b0,) = route(
        lay,
        chain,
        tables,
        [(mirror_zero, 0, b0, False, None, None), (mirror_zero, 1, b0, True, None, None)],
        (2,),
    )
    rows_b0 = dispatch(lay, sent_b0, True)
    saved_two = mirrored(stacked(lay, chain, [right_saved], [(1, 0)]))
    back_f0 = summed(lay, chain, parts_f0, over_f0)
    parts_b1, (kept_b1,) = run_experts(
        lay, chain, [("backward", (0, 0), (0, 1))], [rows_b1], weights
    )
    over_b1 = handed_over(lay, parts_b1, True)
    left_zero = combine(lay, chain, tables, f0, True, left_first, back_f0, 0)
    arriving = passed_along(left_zero, 1)
    parts_b0, (kept_b0,) = run_experts(
        lay, chain, [("backward", (0, 0), (0, 1))], [rows_b0], weights
    )
    over_b0 = handed_over(lay, parts_b0, True)
    back_b0 = summed(lay, chain, parts_b0, over_b0)
    back_b1 = summed(lay, chain, parts_b1, over_b1)
    right_first = mirrored(stacked(lay, chain, [right_in], [(0,)]))
    (sent_f2,) = route(
        lay,
        chain,
        tables,
        [(saved_two, 0, b2, False, None, None), (arriving, None, f2, False, "first", left_fresh)],
        (2,),
    )
    rows_f2 = dispatch(lay, sent_f2, True)
    rows_s1, lead_f2 = rows_f2, 1
    back_zero = combine(lay, chain, tables, b0, False, mirror_zero, back_b0, 0, lead=1)
    returning = passed_along(back_zero, -1)
    back_one = combine(lay, chain, tables, b1, False, cot_first, back_b1, 0)
    (sent_f1,) = route(
        lay, chain, tables, [(right_first, 0, f1, False, None, None)], (1,)
    )
    rows_f1 = dispatch(lay, sent_f1, True)
    parts_f2, _ = run_experts(lay, chain, [("forward", (0, lead_f2))], [rows_f2], weights)
    over_f2 = handed_over(lay, parts_f2, True)
    (sent_c2,) = route(
        lay, chain, tables, [(returning, None, b2, True, "last", cot_fresh)], (1,)
    )
    cots_b2 = dispatch(lay, sent_c2, True)
    back_f2 = summed(lay, chain, parts_f2, over_f2)
    parts_f1, _ = run_experts(lay, chain, [("forward", (0, 0))], [rows_f1], weights)
    over_f1 = handed_over(lay, parts_f1, True)
    parts_b2, (kept_b2,) = run_experts(
        lay, chain, [("backward", (0, 0), (1, 0))], [rows_s1, cots_b2], weights
    )
    over_b2 = handed_over(lay, parts_b2, True)
    back_f1 = summed(lay, chain, parts_f1, over_f1)
    left_out = combine(
        lay,
        chain,
        tables,
        f2,
        True,
        arriving,
        back_f2,
        0,
        edge="first",
        fresh=left_fresh,
        first=left_zero,
    )
    grad_gate, grad_up, grad_down = all_gradients(chain, (kept_b0, kept_b1, kept_b2))
    back_b2 = summed(lay, chain, parts_b2, over_b2)
    right_out = combine(lay, chain, tables, f1, True, right_first, back_f1, 0, lead=0)
    right_back = combine(
        lay,
        chain,
        tables,
        b2,
        False,
        returning,
        back_b2,
        0,
        edge="last",
        fresh=cot_fresh,
        first=back_zero,
    )
    return (
        left_out[:, None],
        right_out[None],
        back_one[None],
        right_back[:, None],
        grad_gate[None, None],
        grad_up[None, None],
        grad_down[None, None],
    )


def solution(mesh):
    in_specs = (
        P("section", "expert", None),
        P("expert", None),
        P("section", "expert", None),
        P("section", "expert", None),
        P("section", "expert", None),
        P(None, "section", "expert", None),
        P("section", "expert", None),
        P("expert", None),
        P(None, None, "section", "expert", None),
        P(None, None, "section", "expert", None),
        P("section", "expert", None, None),
        P("section", "expert", None, None),
        P("section", "expert", None, None),
    )
    out_specs = (
        P(None, "section", "expert", None),
        P("section", "expert", None),
        P("section", "expert", None),
        P(None, "section", "expert", None),
        P("section", "expert", None, None),
        P("section", "expert", None, None),
        P("section", "expert", None, None),
    )
    return jax.shard_map(
        per_device, mesh=mesh, in_specs=in_specs, out_specs=out_specs, check_vma=False
    )
```

time: 136 us -> 115 us (0.85)
  the two profiles are of different devices: /device:TPU:18 before, /device:TPU:10 now
where the time goes in v3:
time: 115 us; the launch traced here: 114 us
  starting transfers between devices  46.5 us (40%)
  waiting for transfers between devices  35.4 us (31%)
  Pallas kernels  25.8 us (22%)
  local copies, waits for them, and re-layouts  5.76 us (5%)
    ppermute x36, starting transfers between devices, swapped(): lax.ppermute(value, 'expert', [(i, i ^ bits) for i in range(lay.peers)])  41.4 us
    ppermute x36, waiting for transfers between devices, swapped(): lax.ppermute(value, 'expert', [(i, i ^ bits) for i in range(lay.peers)])  28.4 us
    pallas_call x19, Pallas kernels, call(): pl.pallas_call(body, out_shape=outs, in_specs=specs, out_specs=[VMEM_SPEC...  18.2 us
    ppermute x3, waiting for transfers between devices, mirrored(): lax.ppermute(value, 'section', [(i, count - 1 - i) for i in range(count)])  7.03 us
    unnamed x34, local copies, waits for them, and re-layouts  5.76 us
    pallas_call x1, Pallas kernels, all_gradients(): pl.pallas_call(body, grid=(width // tile,), out_shape=outs, in_specs=[wid...  4.58 us
    ppermute x2, starting transfers between devices, passed_along(): return lax.ppermute(value, 'section', pairs)  4.02 us
    pallas_call x1, Pallas kernels, opening(): pl.pallas_call(functools.partial(opening_kernel, lay, plan, tuple(groups)...  3.02 us
  transfers between devices with their start and end apart: 41, of which 15 were waited for; matrix products, arithmetic and copies ran while one was open for 0% of the time, Pallas kernels for 19%

profile of v3, /device:TPU:10, one launch (start us, length us, event | category | flops | bytes accessed | tf_op | source)
XLA Modules:
  0.0 114.4 jit_solution(16424838634569180018)
XLA Ops:
  0.6 3.0 %shard_map.180 = (bf16[2,64,2048]{2,1,0:T(8,128)(2,1)}, bf16[1,32,2176]{2,1,0:T(8,128)(2,1)}, bf16[1,32,2176]{2,1,0:T(8,128)(2,1)}, bf16[2,32,2176]{2,1,0:T(8,128)(2,1)}, bf16[2,32,2176]{2,1,0:T(8,128)(2,1)}) custom-call(bf16[64,2048]{1,0:T(8,128)(2,1)} %bitcast.40, bf16[64,2048]{1,0:T(8,128)(2,1)} %bitcast.67, bf16[64,2048]{1,0:T(8,128)(2,1)} %bitcast.42, ...), custom_call_target="tpu_custom_call" | custom-call | flops 62914560 | bytes 2935808 | tf_op jit(solution)/shard_map/pallas_call | solution.py:525
  5.3 2.5 %collective-permute-start.2 = (bf16[1,32,2176]{2,1,0:T(8,128)(2,1)}, bf16[1,32,2176]{2,1,0:T(8,128)(2,1)S(1)}, u32[]{:S(2)}, u32[]{:S(2)}) collective-permute-start(bf16[1,32,2176]{2,1,0:T(8,128)(2,1)} %get-tuple-element.60), channel_id=1, source_target_pairs={{0,3},{1,2},{2,1},{3,0},{4,7},{5,6},{6,5},{7,4},{8,11},{9,10},{10,... | collective-permute-start | bytes 417800 | tf_op jit(solution)/shard_map/ppermute | solution.py:228
  8.8 2.7 %collective-permute-done.refs_1_ = bf16[1,32,2176]{2,1,0:T(8,128)(2,1)S(1)} collective-permute-done((bf16[1,32,2176]{2,1,0:T(8,128)(2,1)}, bf16[1,32,2176]{2,1,0:T(8,128)(2,1)S(1)}, u32[]{:S(2)}, u32[]{:S(2)}) %collective-permute-start) | collective-permute-done | bytes 139296 | tf_op jit(solution)/shard_map/ppermute | solution.py:228
  11.5 1.5 %collective-permute-start.9 = (bf16[2,32,2176]{2,1,0:T(8,128)(2,1)}, bf16[2,32,2176]{2,1,0:T(8,128)(2,1)S(1)}, u32[]{:S(2)}, u32[]{:S(2)}) collective-permute-start(bf16[2,32,2176]{2,1,0:T(8,128)(2,1)} %get-tuple-element.68), channel_id=1, source_target_pairs={{0,3},{1,2},{2,1},{3,0},{4,7},{5,6},{6,5},{7,4},{8,11},{9,10},{10,... | collective-permute-start | bytes 835592 | tf_op jit(solution)/shard_map/ppermute | solution.py:228
  13.0 2.5 %collective-permute-done.2.refs_3_ = bf16[1,32,2176]{2,1,0:T(8,128)(2,1)S(1)} collective-permute-done((bf16[1,32,2176]{2,1,0:T(8,128)(2,1)}, bf16[1,32,2176]{2,1,0:T(8,128)(2,1)S(1)}, u32[]{:S(2)}, u32[]{:S(2)}) %collective-permute-start.2) | collective-permute-done | bytes 139296 | tf_op jit(solution)/shard_map/ppermute | solution.py:228
  22.2 7.0 %collective-permute-done.5.refs_0_.refs_1_.refs_2_ = bf16[2,64,2048]{2,1,0:T(8,128)(2,1)S(1)} collective-permute-done((bf16[2,64,2048]{2,1,0:T(8,128)(2,1)}, bf16[2,64,2048]{2,1,0:T(8,128)(2,1)S(1)}, u32[]{:S(2)}, u32[]{:S(2)}) %collective-permute-start.5) | collective-permute-done | bytes 524320 | tf_op jit(solution)/shard_map/ppermute | solution.py:547
  30.4 1.6 %collective-permute-start.6 = (bf16[1,32,2176]{2,1,0:T(8,128)(2,1)S(1)}, bf16[1,32,2176]{2,1,0:T(8,128)(2,1)S(1)}, u32[]{:S(2)}, u32[]{:S(2)}) collective-permute-start(bf16[1,32,2176]{2,1,0:T(8,128)(2,1)S(1)} %shard_map.184.refs_7_), channel_id=1, source_target_pairs={{0,2},{1,3},{2,0},{3,1},{4,6},{5,7},{6,4},{7,5},{8,10},{9,11},{10,... | collective-permute-start | bytes 417800 | tf_op jit(solution)/shard_map/ppermute | solution.py:228
  33.4 1.5 %collective-permute-start.13 = (bf16[2,32,2176]{2,1,0:T(8,128)(2,1)S(1)}, bf16[2,32,2176]{2,1,0:T(8,128)(2,1)S(1)}, u32[]{:S(2)}, u32[]{:S(2)}) collective-permute-start(bf16[2,32,2176]{2,1,0:T(8,128)(2,1)S(1)} %get-tuple-element.70), channel_id=1, source_target_pairs={{0,2},{1,3},{2,0},{3,1},{4,6},{5,7},{6,4},{7,5},{8,10},{9,11},{10,... | collective-permute-start | bytes 835592 | tf_op jit(solution)/shard_map/ppermute | solution.py:228
  35.5 2.5 %shard_map.185 = (bf16[1,32,2176]{2,1,0:T(8,128)(2,1)S(1)}, bf16[1,32,2176]{2,1,0:T(8,128)(2,1)S(1)}, bf16[1,32,2176]{2,1,0:T(8,128)(2,1)S(1)}, bf16[1,32,2176]{...) custom-call(bf16[2,32,2176]{2,1,0:T(8,128)(2,1)S(1)} %copy-done.15, ...), custom_call_target="tpu_custom_call" | custom-call | flops 1069547520 | bytes 7901184 | tf_op jit(solution)/shard_map/pallas_call | solution.py:158
  38.0 4.4 %collective-permute-done.6.refs_5_ = bf16[1,32,2176]{2,1,0:T(8,128)(2,1)S(1)} collective-permute-done((bf16[1,32,2176]{2,1,0:T(8,128)(2,1)S(1)}, bf16[1,32,2176]{2,1,0:T(8,128)(2,1)S(1)}, u32[]{:S(2)}, u32[]{:S(2)}) %collective-permute-start.6) | collective-permute-done | bytes 139296 | tf_op jit(solution)/shard_map/ppermute | solution.py:228
  42.8 1.9 %collective-permute-start.10 = (bf16[64,2048]{1,0:T(8,128)(2,1)S(1)}, bf16[64,2048]{1,0:T(8,128)(2,1)S(1)}, u32[]{:S(2)}, u32[]{:S(2)}) collective-permute-start(bf16[64,2048]{1,0:T(8,128)(2,1)S(1)} %shard_map.186.refs_7_.refs_4_), channel_id=1, source_target_pairs={{0,4},{4,8},{8,12},{12,16},{16,20},{20,24},{24,28},{1,5},{5,9},{9,... | collective-permute-start | bytes 786440 | tf_op jit(solution)/shard_map/ppermute | solution.py:553
  44.8 2.0 %collective-permute-start.19 = (bf16[1,32,2176]{2,1,0:T(8,128)(2,1)S(1)}, bf16[1,32,2176]{2,1,0:T(8,128)(2,1)S(1)}, u32[]{:S(2)}, u32[]{:S(2)}) collective-permute-start(bf16[1,32,2176]{2,1,0:T(8,128)(2,1)S(1)} %get-tuple-element.74), channel_id=1, source_target_pairs={{0,1},{1,0},{2,3},{3,2},{4,5},{5,4},{6,7},{7,6},{8,9},{9,8},{10,11... | collective-permute-start | bytes 417800 | tf_op jit(solution)/shard_map/ppermute | solution.py:228
  49.3 2.5 %shard_map.187 = (bf16[1,32,2176]{2,1,0:T(8,128)(2,1)S(1)}, bf16[1,32,2176]{2,1,0:T(8,128)(2,1)S(1)}, bf16[1,32,2176]{2,1,0:T(8,128)(2,1)S(1)}, bf16[1,32,2176]{...) custom-call(bf16[2,32,2176]{2,1,0:T(8,128)(2,1)S(1)} %get-tuple-elem, ...), custom_call_target="tpu_custom_call" | custom-call | flops 1069547520 | bytes 7901184 | tf_op jit(solution)/shard_map/pallas_call | solution.py:158
  51.8 1.5 %collective-permute-start.22 = (bf16[1,32,2176]{2,1,0:T(8,128)(2,1)S(1)}, bf16[1,32,2176]{2,1,0:T(8,128)(2,1)S(1)}, u32[]{:S(2)}, u32[]{:S(2)}) collective-permute-start(bf16[1,32,2176]{2,1,0:T(8,128)(2,1)S(1)} %get-tuple-element.77), channel_id=1, source_target_pairs={{0,1},{1,0},{2,3},{3,2},{4,5},{5,4},{6,7},{7,6},{8,9},{9,8},{10,11... | collective-permute-start | bytes 417800 | tf_op jit(solution)/shard_map/ppermute | solution.py:228
  55.9 1.6 %collective-permute-start.17 = (bf16[2,32,2176]{2,1,0:T(8,128)(2,1)S(1)}, bf16[2,32,2176]{2,1,0:T(8,128)(2,1)S(1)}, u32[]{:S(2)}, u32[]{:S(2)}) collective-permute-start(bf16[2,32,2176]{2,1,0:T(8,128)(2,1)S(1)} %get-tuple-element.73), channel_id=1, source_target_pairs={{0,3},{1,2},{2,1},{3,0},{4,7},{5,6},{6,5},{7,4},{8,11},{9,10},{10,... | collective-permute-start | bytes 835592 | tf_op jit(solution)/shard_map/ppermute | solution.py:228
  58.9 12.0 %collective-permute-done.23.refs_5_ = bf16[1,32,2176]{2,1,0:T(8,128)(2,1)S(1)} collective-permute-done((bf16[1,32,2176]{2,1,0:T(8,128)(2,1)S(1)}, bf16[1,32,2176]{2,1,0:T(8,128)(2,1)S(1)}, u32[]{:S(2)}, u32[]{:S(2)}) %collective-permute-start.23) | collective-permute-done | bytes 139296 | tf_op jit(solution)/shard_map/ppermute | solution.py:228
  72.7 2.1 %collective-permute-start.28 = (bf16[64,2048]{1,0:T(8,128)(2,1)S(1)}, bf16[64,2048]{1,0:T(8,128)(2,1)S(1)}, u32[]{:S(2)}, u32[]{:S(2)}) collective-permute-start(bf16[64,2048]{1,0:T(8,128)(2,1)S(1)} %shard_map.190.refs_7_.refs_4_), channel_id=1, source_target_pairs={{4,0},{8,4},{12,8},{16,12},{20,16},{24,20},{28,24},{5,1},{9,5},{13... | collective-permute-start | bytes 786440 | tf_op jit(solution)/shard_map/ppermute | solution.py:553
  77.2 2.2 %collective-permute-start.34 = (bf16[1,32,2176]{2,1,0:T(8,128)(2,1)S(1)}, bf16[1,32,2176]{2,1,0:T(8,128)(2,1)S(1)}, u32[]{:S(2)}, u32[]{:S(2)}) collective-permute-start(bf16[1,32,2176]{2,1,0:T(8,128)(2,1)S(1)} %get-tuple-element.87), channel_id=1, source_target_pairs={{0,3},{1,2},{2,1},{3,0},{4,7},{5,6},{6,5},{7,4},{8,11},{9,10},{10,... | collective-permute-start | bytes 417800 | tf_op jit(solution)/shard_map/ppermute | solution.py:228
  79.3 1.4 %collective-permute-start.32 = (bf16[1,32,2176]{2,1,0:T(8,128)(2,1)S(1)}, bf16[1,32,2176]{2,1,0:T(8,128)(2,1)S(1)}, u32[]{:S(2)}, u32[]{:S(2)}) collective-permute-start(bf16[1,32,2176]{2,1,0:T(8,128)(2,1)S(1)} %get-tuple-element.80.refs_7_.refs_0_), channel_id=1, source_target_pairs={{0,1},{1,0},{2,3},{3,2},{4,5},{5,4},{6,7},{7,6},{8,9},{9,8},{10,11... | collective-permute-start | bytes 417800 | tf_op jit(solution)/shard_map/ppermute | solution.py:228
  83.1 2.8 %collective-permute-start.31 = (bf16[1,32,2176]{2,1,0:T(8,128)(2,1)S(1)}, bf16[1,32,2176]{2,1,0:T(8,128)(2,1)S(1)}, u32[]{:S(2)}, u32[]{:S(2)}) collective-permute-start(bf16[1,32,2176]{2,1,0:T(8,128)(2,1)S(1)} %get-tuple-element.86), channel_id=1, source_target_pairs={{0,3},{1,2},{2,1},{3,0},{4,7},{5,6},{6,5},{7,4},{8,11},{9,10},{10,... | collective-permute-start | bytes 417800 | tf_op jit(solution)/shard_map/ppermute | solution.py:228
  88.2 1.8 %collective-permute-start.26 = (bf16[1,32,2176]{2,1,0:T(8,128)(2,1)S(1)}, bf16[1,32,2176]{2,1,0:T(8,128)(2,1)S(1)}, u32[]{:S(2)}, u32[]{:S(2)}) collective-permute-start(bf16[1,32,2176]{2,1,0:T(8,128)(2,1)S(1)} %get-tuple-element.83), channel_id=1, source_target_pairs={{0,2},{1,3},{2,0},{3,1},{4,6},{5,7},{6,4},{7,5},{8,10},{9,11},{10,... | collective-permute-start | bytes 417800 | tf_op jit(solution)/shard_map/ppermute | solution.py:228
  97.8 2.5 %shard_map.196 = (bf16[1,32,2176]{2,1,0:T(8,128)(2,1)S(1)}, bf16[1,32,2176]{2,1,0:T(8,128)(2,1)S(1)}, bf16[1,32,2176]{2,1,0:T(8,128)(2,1)S(1)}, bf16[1,32,2176]{...) custom-call(bf16[2,32,2176]{2,1,0:T(8,128)(2,1)S(1)} %get-tuple-elem, ...), custom_call_target="tpu_custom_call" | custom-call | flops 1069547520 | bytes 8458240 | tf_op jit(solution)/shard_map/pallas_call | solution.py:158
  101.3 2.0 %collective-permute-start.39 = (bf16[1,32,2176]{2,1,0:T(8,128)(2,1)S(1)}, bf16[1,32,2176]{2,1,0:T(8,128)(2,1)S(1)}, u32[]{:S(2)}, u32[]{:S(2)}) collective-permute-start(bf16[1,32,2176]{2,1,0:T(8,128)(2,1)S(1)} %get-tuple-element.94), channel_id=1, source_target_pairs={{0,2},{1,3},{2,0},{3,1},{4,6},{5,7},{6,4},{7,5},{8,10},{9,11},{10,... | collective-permute-start | bytes 417800 | tf_op jit(solution)/shard_map/ppermute | solution.py:228
  108.6 4.6 %shard_map.200 = (bf16[2048,384]{1,0:T(8,128)(2,1)}, bf16[2048,384]{1,0:T(8,128)(2,1)}, bf16[384,2048]{1,0:T(8,128)(2,1)}) custom-call(bf16[144,2048]{1,0:T(8,128)(2,1)S(1)} %get-tuple-element.96.refs_0_, bf16[144,2048]{1,0:T(8,128)(2,1)S(1)} %get-tuple-element.97.refs_1_, bf16[144,2048]{1,0:T(8,128)(2,1)S(1)} %get-tuple-element.98.refs_2_, ...), custom_call_target="tpu_custom_call" | custom-call | flops 2038431744 | bytes 9252864 | tf_op jit(solution)/shard_map/pallas_call | solution.py:460
  (113 shorter events, 43.3 us)
Async XLA Ops:
  3.7 25.6 %collective-permute-start.5 = (bf16[2,64,2048]{2,1,0:T(8,128)(2,1)}, bf16[2,64,2048]{2,1,0:T(8,128)(2,1)S(1)}, u32[]{:S(2)}, u32[]{:S(2)}) collective-permute-start(bf16[2,64,2048]{2,1,0:T(8,128)(2,1)} %get-tuple-element.65), channel_id=1, source_target_pairs={{0,28},{4,24},{8,20},{12,16},{16,12},{20,8},{24,4},{28,0},{1,29},{... | collective-permute-start | bytes 1572872 | tf_op jit(solution)/shard_map/ppermute | solution.py:547
  5.3 10.2 %collective-permute-start.2 = (bf16[1,32,2176]{2,1,0:T(8,128)(2,1)}, bf16[1,32,2176]{2,1,0:T(8,128)(2,1)S(1)}, u32[]{:S(2)}, u32[]{:S(2)}) collective-permute-start(bf16[1,32,2176]{2,1,0:T(8,128)(2,1)} %get-tuple-element.60), channel_id=1, source_target_pairs={{0,3},{1,2},{2,1},{3,0},{4,7},{5,6},{6,5},{7,4},{8,11},{9,10},{10,... | collective-permute-start | bytes 417800 | tf_op jit(solution)/shard_map/ppermute | solution.py:228
  8.2 23.7 %collective-permute-start.7 = (bf16[2,32,2176]{2,1,0:T(8,128)(2,1)}, bf16[2,32,2176]{2,1,0:T(8,128)(2,1)S(1)}, u32[]{:S(2)}, u32[]{:S(2)}) collective-permute-start(bf16[2,32,2176]{2,1,0:T(8,128)(2,1)} %get-tuple-element.67.refs_0_), channel_id=1, source_target_pairs={{0,1},{1,0},{2,3},{3,2},{4,5},{5,4},{6,7},{7,6},{8,9},{9,8},{10,11... | collective-permute-start | bytes 835592 | tf_op jit(solution)/shard_map/ppermute | solution.py:228
  11.5 21.9 %collective-permute-start.9 = (bf16[2,32,2176]{2,1,0:T(8,128)(2,1)}, bf16[2,32,2176]{2,1,0:T(8,128)(2,1)S(1)}, u32[]{:S(2)}, u32[]{:S(2)}) collective-permute-start(bf16[2,32,2176]{2,1,0:T(8,128)(2,1)} %get-tuple-element.68), channel_id=1, source_target_pairs={{0,3},{1,2},{2,1},{3,0},{4,7},{5,6},{6,5},{7,4},{8,11},{9,10},{10,... | collective-permute-start | bytes 835592 | tf_op jit(solution)/shard_map/ppermute | solution.py:228
  15.5 19.4 %collective-permute-start.8 = (bf16[2,32,2176]{2,1,0:T(8,128)(2,1)}, bf16[2,32,2176]{2,1,0:T(8,128)(2,1)S(1)}, u32[]{:S(2)}, u32[]{:S(2)}) collective-permute-start(bf16[2,32,2176]{2,1,0:T(8,128)(2,1)} %get-tuple-element.68), channel_id=1, source_target_pairs={{0,2},{1,3},{2,0},{3,1},{4,6},{5,7},{6,4},{7,5},{8,10},{9,11},{10,... | collective-permute-start | bytes 835592 | tf_op jit(solution)/shard_map/ppermute | solution.py:228
  30.4 12.1 %collective-permute-start.6 = (bf16[1,32,2176]{2,1,0:T(8,128)(2,1)S(1)}, bf16[1,32,2176]{2,1,0:T(8,128)(2,1)S(1)}, u32[]{:S(2)}, u32[]{:S(2)}) collective-permute-start(bf16[1,32,2176]{2,1,0:T(8,128)(2,1)S(1)} %shard_map.184.refs_7_), channel_id=1, source_target_pairs={{0,2},{1,3},{2,0},{3,1},{4,6},{5,7},{6,4},{7,5},{8,10},{9,11},{10,... | collective-permute-start | bytes 417800 | tf_op jit(solution)/shard_map/ppermute | solution.py:228
  32.0 12.8 %collective-permute-start.14 = (bf16[2,32,2176]{2,1,0:T(8,128)(2,1)S(1)}, bf16[2,32,2176]{2,1,0:T(8,128)(2,1)S(1)}, u32[]{:S(2)}, u32[]{:S(2)}) collective-permute-start(bf16[2,32,2176]{2,1,0:T(8,128)(2,1)S(1)} %get-tuple-element.70), channel_id=1, source_target_pairs={{0,3},{1,2},{2,1},{3,0},{4,7},{5,6},{6,5},{7,4},{8,11},{9,10},{10,... | collective-permute-start | bytes 835592 | tf_op jit(solution)/shard_map/ppermute | solution.py:228
  33.4 14.5 %collective-permute-start.13 = (bf16[2,32,2176]{2,1,0:T(8,128)(2,1)S(1)}, bf16[2,32,2176]{2,1,0:T(8,128)(2,1)S(1)}, u32[]{:S(2)}, u32[]{:S(2)}) collective-permute-start(bf16[2,32,2176]{2,1,0:T(8,128)(2,1)S(1)} %get-tuple-element.70), channel_id=1, source_target_pairs={{0,2},{1,3},{2,0},{3,1},{4,6},{5,7},{6,4},{7,5},{8,10},{9,11},{10,... | collective-permute-start | bytes 835592 | tf_op jit(solution)/shard_map/ppermute | solution.py:228
  34.9 14.4 %collective-permute-start.12 = (bf16[2,32,2176]{2,1,0:T(8,128)(2,1)S(1)}, bf16[2,32,2176]{2,1,0:T(8,128)(2,1)S(1)}, u32[]{:S(2)}, u32[]{:S(2)}) collective-permute-start(bf16[2,32,2176]{2,1,0:T(8,128)(2,1)S(1)} %get-tuple-element.66.refs_1_.refs_0_), channel_id=1, source_target_pairs={{0,1},{1,0},{2,3},{3,2},{4,5},{5,4},{6,7},{7,6},{8,9},{9,8},{10,11... | collective-permute-start | bytes 835592 | tf_op jit(solution)/shard_map/ppermute | solution.py:228
  38.0 15.4 %collective-permute-start.11 = (bf16[1,64,2048]{2,1,0:T(8,128)(2,1)S(1)}, bf16[1,64,2048]{2,1,0:T(8,128)(2,1)S(1)}, u32[]{:S(2)}, u32[]{:S(2)}) collective-permute-start(bf16[1,64,2048]{2,1,0:T(8,128)(2,1)S(1)} %shard_map.183.refs_2_), channel_id=1, source_target_pairs={{0,28},{4,24},{8,20},{12,16},{16,12},{20,8},{24,4},{28,0},{1,29},{... | collective-permute-start | bytes 786440 | tf_op jit(solution)/shard_map/ppermute | solution.py:547
  42.8 11.2 %collective-permute-start.10 = (bf16[64,2048]{1,0:T(8,128)(2,1)S(1)}, bf16[64,2048]{1,0:T(8,128)(2,1)S(1)}, u32[]{:S(2)}, u32[]{:S(2)}) collective-permute-start(bf16[64,2048]{1,0:T(8,128)(2,1)S(1)} %shard_map.186.refs_7_.refs_4_), channel_id=1, source_target_pairs={{0,4},{4,8},{8,12},{12,16},{16,20},{20,24},{24,28},{1,5},{5,9},{9,... | collective-permute-start | bytes 786440 | tf_op jit(solution)/shard_map/ppermute | solution.py:553
  44.8 11.1 %collective-permute-start.19 = (bf16[1,32,2176]{2,1,0:T(8,128)(2,1)S(1)}, bf16[1,32,2176]{2,1,0:T(8,128)(2,1)S(1)}, u32[]{:S(2)}, u32[]{:S(2)}) collective-permute-start(bf16[1,32,2176]{2,1,0:T(8,128)(2,1)S(1)} %get-tuple-element.74), channel_id=1, source_target_pairs={{0,1},{1,0},{2,3},{3,2},{4,5},{5,4},{6,7},{7,6},{8,9},{9,8},{10,11... | collective-permute-start | bytes 417800 | tf_op jit(solution)/shard_map/ppermute | solution.py:228
  53.4 17.5 %collective-permute-start.23 = (bf16[1,32,2176]{2,1,0:T(8,128)(2,1)S(1)}, bf16[1,32,2176]{2,1,0:T(8,128)(2,1)S(1)}, u32[]{:S(2)}, u32[]{:S(2)}) collective-permute-start(bf16[1,32,2176]{2,1,0:T(8,128)(2,1)S(1)} %get-tuple-element.78), channel_id=1, source_target_pairs={{0,2},{1,3},{2,0},{3,1},{4,6},{5,7},{6,4},{7,5},{8,10},{9,11},{10,... | collective-permute-start | bytes 417800 | tf_op jit(solution)/shard_map/ppermute | solution.py:228
  54.0 16.9 %collective-permute-start.24 = (bf16[1,32,2176]{2,1,0:T(8,128)(2,1)S(1)}, bf16[1,32,2176]{2,1,0:T(8,128)(2,1)S(1)}, u32[]{:S(2)}, u32[]{:S(2)}) collective-permute-start(bf16[1,32,2176]{2,1,0:T(8,128)(2,1)S(1)} %get-tuple-element.79), channel_id=1, source_target_pairs={{0,3},{1,2},{2,1},{3,0},{4,7},{5,6},{6,5},{7,4},{8,11},{9,10},{10,... | collective-permute-start | bytes 417800 | tf_op jit(solution)/shard_map/ppermute | solution.py:228
  55.9 23.4 %collective-permute-start.17 = (bf16[2,32,2176]{2,1,0:T(8,128)(2,1)S(1)}, bf16[2,32,2176]{2,1,0:T(8,128)(2,1)S(1)}, u32[]{:S(2)}, u32[]{:S(2)}) collective-permute-start(bf16[2,32,2176]{2,1,0:T(8,128)(2,1)S(1)} %get-tuple-element.73), channel_id=1, source_target_pairs={{0,3},{1,2},{2,1},{3,0},{4,7},{5,6},{6,5},{7,4},{8,11},{9,10},{10,... | collective-permute-start | bytes 835592 | tf_op jit(solution)/shard_map/ppermute | solution.py:228
  57.5 15.2 %collective-permute-start.21 = (bf16[1,32,2176]{2,1,0:T(8,128)(2,1)S(1)}, bf16[1,32,2176]{2,1,0:T(8,128)(2,1)S(1)}, u32[]{:S(2)}, u32[]{:S(2)}) collective-permute-start(bf16[1,32,2176]{2,1,0:T(8,128)(2,1)S(1)} %get-tuple-element.76), channel_id=1, source_target_pairs={{0,3},{1,2},{2,1},{3,0},{4,7},{5,6},{6,5},{7,4},{8,11},{9,10},{10,... | collective-permute-start | bytes 417800 | tf_op jit(solution)/shard_map/ppermute | solution.py:228
  58.9 17.0 %collective-permute-start.18 = (bf16[1,64,2048]{2,1,0:T(8,128)(2,1)S(1)}, bf16[1,64,2048]{2,1,0:T(8,128)(2,1)S(1)}, u32[]{:S(2)}, u32[]{:S(2)}) collective-permute-start(bf16[1,64,2048]{2,1,0:T(8,128)(2,1)S(1)} %shard_map.188.refs_5_), channel_id=1, source_target_pairs={{0,28},{4,24},{8,20},{12,16},{16,12},{20,8},{24,4},{28,0},{1,29},{... | collective-permute-start | bytes 786440 | tf_op jit(solution)/shard_map/ppermute | solution.py:547
  83.1 10.5 %collective-permute-start.31 = (bf16[1,32,2176]{2,1,0:T(8,128)(2,1)S(1)}, bf16[1,32,2176]{2,1,0:T(8,128)(2,1)S(1)}, u32[]{:S(2)}, u32[]{:S(2)}) collective-permute-start(bf16[1,32,2176]{2,1,0:T(8,128)(2,1)S(1)} %get-tuple-element.86), channel_id=1, source_target_pairs={{0,3},{1,2},{2,1},{3,0},{4,7},{5,6},{6,5},{7,4},{8,11},{9,10},{10,... | collective-permute-start | bytes 417800 | tf_op jit(solution)/shard_map/ppermute | solution.py:228
  88.2 12.7 %collective-permute-start.26 = (bf16[1,32,2176]{2,1,0:T(8,128)(2,1)S(1)}, bf16[1,32,2176]{2,1,0:T(8,128)(2,1)S(1)}, u32[]{:S(2)}, u32[]{:S(2)}) collective-permute-start(bf16[1,32,2176]{2,1,0:T(8,128)(2,1)S(1)} %get-tuple-element.83), channel_id=1, source_target_pairs={{0,2},{1,3},{2,0},{3,1},{4,6},{5,7},{6,4},{7,5},{8,10},{9,11},{10,... | collective-permute-start | bytes 417800 | tf_op jit(solution)/shard_map/ppermute | solution.py:228
  91.2 10.1 %collective-permute-start.27 = (bf16[1,32,2176]{2,1,0:T(8,128)(2,1)S(1)}, bf16[1,32,2176]{2,1,0:T(8,128)(2,1)S(1)}, u32[]{:S(2)}, u32[]{:S(2)}) collective-permute-start(bf16[1,32,2176]{2,1,0:T(8,128)(2,1)S(1)} %get-tuple-element.84), channel_id=1, source_target_pairs={{0,3},{1,2},{2,1},{3,0},{4,7},{5,6},{6,5},{7,4},{8,11},{9,10},{10,... | collective-permute-start | bytes 417800 | tf_op jit(solution)/shard_map/ppermute | solution.py:228
  93.6 10.8 %collective-permute-start.35 = (bf16[1,32,2176]{2,1,0:T(8,128)(2,1)S(1)}, bf16[1,32,2176]{2,1,0:T(8,128)(2,1)S(1)}, u32[]{:S(2)}, u32[]{:S(2)}) collective-permute-start(bf16[1,32,2176]{2,1,0:T(8,128)(2,1)S(1)} %get-tuple-element.90), channel_id=1, source_target_pairs={{0,1},{1,0},{2,3},{3,2},{4,5},{5,4},{6,7},{7,6},{8,9},{9,8},{10,11... | collective-permute-start | bytes 417800 | tf_op jit(solution)/shard_map/ppermute | solution.py:228
  94.9 11.6 %collective-permute-start.36 = (bf16[1,32,2176]{2,1,0:T(8,128)(2,1)S(1)}, bf16[1,32,2176]{2,1,0:T(8,128)(2,1)S(1)}, u32[]{:S(2)}, u32[]{:S(2)}) collective-permute-start(bf16[1,32,2176]{2,1,0:T(8,128)(2,1)S(1)} %get-tuple-element.91), channel_id=1, source_target_pairs={{0,2},{1,3},{2,0},{3,1},{4,6},{5,7},{6,4},{7,5},{8,10},{9,11},{10,... | collective-permute-start | bytes 417800 | tf_op jit(solution)/shard_map/ppermute | solution.py:228
  100.9 12.3 %collective-permute-start.38 = (bf16[1,32,2176]{2,1,0:T(8,128)(2,1)S(1)}, bf16[1,32,2176]{2,1,0:T(8,128)(2,1)S(1)}, u32[]{:S(2)}, u32[]{:S(2)}) collective-permute-start(bf16[1,32,2176]{2,1,0:T(8,128)(2,1)S(1)} %get-tuple-element.93), channel_id=1, source_target_pairs={{0,1},{1,0},{2,3},{3,2},{4,5},{5,4},{6,7},{7,6},{8,9},{9,8},{10,11... | collective-permute-start | bytes 417800 | tf_op jit(solution)/shard_map/ppermute | solution.py:228
  101.3 11.9 %collective-permute-start.39 = (bf16[1,32,2176]{2,1,0:T(8,128)(2,1)S(1)}, bf16[1,32,2176]{2,1,0:T(8,128)(2,1)S(1)}, u32[]{:S(2)}, u32[]{:S(2)}) collective-permute-start(bf16[1,32,2176]{2,1,0:T(8,128)(2,1)S(1)} %get-tuple-element.94), channel_id=1, source_target_pairs={{0,2},{1,3},{2,0},{3,1},{4,6},{5,7},{6,4},{7,5},{8,10},{9,11},{10,... | collective-permute-start | bytes 417800 | tf_op jit(solution)/shard_map/ppermute | solution.py:228
  (34 other events, 268.1 us)

commit v4 on v3

--- a/solution.py
+++ b/solution.py
@@ -102,7 +102,8 @@
     inputs = sum(1 if edge is None else 2 for *_, edge in plan)
     ids, gates = refs[inputs : inputs + 2]
     outs = refs[inputs + 2 : inputs + 2 + len(groups) * lay.experts]
-    scratch = refs[inputs + 2 + len(outs) :]
+    chosen = list(refs[inputs + 2 + len(outs) : inputs + 2 + len(outs) + inputs - len(plan)])
+    scratch = refs[inputs + 2 + len(outs) + len(chosen) :]
     stage = scratch[0]
     copies = []
     for i in range(loads):
@@ -124,6 +125,7 @@
         if edge is not None:
             tokens = jnp.where(at_edge(edge), read(at, None), tokens)
             at += 1
+            chosen.pop(0)[...] = tokens
         if scaled:
             tokens = (as_column(gates[which]) * tokens.astype(F32)).astype(BF16)
         rows = jnp.dot(onehots[which], tokens, preferred_element_type=F32)
@@ -182,6 +184,8 @@
         for size in groups
         for _ in range(lay.experts)
     ]
+    taken = jax.ShapeDtypeStruct((lay.tokens, lay.width), BF16)
+    outs += [taken] * sum(edge is not None for *_, edge in plan)
     scratch = [stage_shape(lay)]
     if loads:
         scratch += [
@@ -198,7 +202,8 @@
         limit,
         loads,
     )
-    return [got[g * lay.experts : (g + 1) * lay.experts] for g in range(len(groups))]
+    sent = [got[g * lay.experts : (g + 1) * lay.experts] for g in range(len(groups))]
+    return sent + list(got[len(groups) * lay.experts :])
 
 
 def stack_kernel(picks, *refs):
@@ -441,7 +446,7 @@
     passes = len(kept)
     held, width = kept[0][0].shape
     half = kept[0][3].shape[1]
-    tile = 4 * LANES if width % (4 * LANES) == 0 else width
+    tile = 8 * LANES if width % (8 * LANES) == 0 else width
     args = [k[i] for i in range(4) for k in kept]
     wide = pl.BlockSpec((held, tile), lambda i: (0, i))
     both = pl.BlockSpec((held, 2 * half), lambda i: (0, 0))
@@ -464,7 +469,7 @@
         in_specs=[wide] * (2 * passes) + [both] * passes + [narrow] * passes
         + [ANY_SPEC] * len(after),
         out_specs=[tall, tall, flat],
-        compiler_params=pltpu.CompilerParams(vmem_limit_bytes=20 * MIB),
+        compiler_params=pltpu.CompilerParams(vmem_limit_bytes=28 * MIB),
         cost_estimate=cost(2 * 3 * passes * held * width * half, args + outs),
     )(*args, *after)
 
@@ -614,13 +619,13 @@
     left_zero = combine(lay, chain, tables, f0, True, left_first, back_f0, 0)
     arriving = passed_along(left_zero, 1)
     parts_b0, (kept_b0,) = run_experts(
-        lay, chain, [("backward", (0, 0), (0, 1))], [rows_b0], weights
+        lay, Chain(), [("backward", (0, 0), (0, 1))], [rows_b0], weights
     )
     over_b0 = handed_over(lay, parts_b0, True)
     back_b0 = summed(lay, chain, parts_b0, over_b0)
     back_b1 = summed(lay, chain, parts_b1, over_b1)
     right_first = mirrored(stacked(lay, chain, [right_in], [(0,)]))
-    (sent_f2,) = route(
+    sent_f2, tokens_f2 = route(
         lay,
         chain,
         tables,
@@ -629,7 +634,7 @@
     )
     rows_f2 = dispatch(lay, sent_f2, True)
     rows_s1, lead_f2 = rows_f2, 1
-    back_zero = combine(lay, chain, tables, b0, False, mirror_zero, back_b0, 0, lead=1)
+    back_zero = combine(lay, Chain(), tables, b0, False, mirror_zero, back_b0, 0, lead=1)
     returning = passed_along(back_zero, -1)
     back_one = combine(lay, chain, tables, b1, False, cot_first, back_b1, 0)
     (sent_f1,) = route(
@@ -638,7 +643,7 @@
     rows_f1 = dispatch(lay, sent_f1, True)
     parts_f2, _ = run_experts(lay, chain, [("forward", (0, lead_f2))], [rows_f2], weights)
     over_f2 = handed_over(lay, parts_f2, True)
-    (sent_c2,) = route(
+    sent_c2, tokens_c2 = route(
         lay, chain, tables, [(returning, None, b2, True, "last", cot_fresh)], (1,)
     )
     cots_b2 = dispatch(lay, sent_c2, True)
@@ -652,15 +657,13 @@
     back_f1 = summed(lay, chain, parts_f1, over_f1)
     left_out = combine(
         lay,
-        chain,
+        Chain(),
         tables,
         f2,
         True,
-        arriving,
+        tokens_f2,
         back_f2,
         0,
-        edge="first",
-        fresh=left_fresh,
         first=left_zero,
     )
     grad_gate, grad_up, grad_down = all_gradients(chain, (kept_b0, kept_b1, kept_b2))
@@ -672,11 +675,9 @@
         tables,
         b2,
         False,
-        returning,
+        tokens_c2,
         back_b2,
         0,
-        edge="last",
-        fresh=cot_fresh,
         first=back_zero,
     )
     return (

time: 115 us -> 114 us (level)
    unnamed x34 -> x30, local copies, waits for them, and re-layouts: 5.76 us -> 4.72 us
where the time goes in v4:
time: 114 us; the launch traced here: 113 us
  starting transfers between devices  46.5 us (41%)
  waiting for transfers between devices  35.4 us (31%)
  Pallas kernels  25.6 us (22%)
  local copies, waits for them, and re-layouts  4.72 us (4%)
    ppermute x36, starting transfers between devices, swapped(): lax.ppermute(value, 'expert', [(i, i ^ bits) for i in range(lay.peers)])  41.3 us
    ppermute x36, waiting for transfers between devices, swapped(): lax.ppermute(value, 'expert', [(i, i ^ bits) for i in range(lay.peers)])  28.4 us
    pallas_call x19, Pallas kernels, call(): pl.pallas_call(body, out_shape=outs, in_specs=specs, out_specs=[VMEM_SPEC...  18.3 us
    ppermute x3, waiting for transfers between devices, mirrored(): lax.ppermute(value, 'section', [(i, count - 1 - i) for i in range(count)])  7.02 us
    unnamed x30, local copies, waits for them, and re-layouts  4.72 us
    pallas_call x1, Pallas kernels, all_gradients(): pl.pallas_call(body, grid=(width // tile,), out_shape=outs, in_specs=[wid...  4.33 us
    ppermute x2, starting transfers between devices, passed_along(): return lax.ppermute(value, 'section', pairs)  4.02 us
    pallas_call x1, Pallas kernels, opening(): pl.pallas_call(functools.partial(opening_kernel, lay, plan, tuple(groups)...  3.02 us
  transfers between devices with their start and end apart: 41, of which 15 were waited for; matrix products, arithmetic and copies ran while one was open for 0% of the time, Pallas kernels for 19%

profile of v4, /device:TPU:10, one launch (start us, length us, event | category | flops | bytes accessed | tf_op | source)
XLA Modules:
  0.0 113.1 jit_solution(12852012198565159968)
XLA Ops:
  0.6 3.0 %shard_map.180 = (bf16[2,64,2048]{2,1,0:T(8,128)(2,1)}, bf16[1,32,2176]{2,1,0:T(8,128)(2,1)}, bf16[1,32,2176]{2,1,0:T(8,128)(2,1)}, bf16[2,32,2176]{2,1,0:T(8,128)(2,1)}, bf16[2,32,2176]{2,1,0:T(8,128)(2,1)}) custom-call(bf16[64,2048]{1,0:T(8,128)(2,1)} %bitcast.39, bf16[64,2048]{1,0:T(8,128)(2,1)} %bitcast.67, bf16[64,2048]{1,0:T(8,128)(2,1)} %bitcast.41, ...), custom_call_target="tpu_custom_call" | custom-call | flops 62914560 | bytes 2935808 | tf_op jit(solution)/shard_map/pallas_call | solution.py:530
  5.3 2.5 %collective-permute-start.3 = (bf16[1,32,2176]{2,1,0:T(8,128)(2,1)}, bf16[1,32,2176]{2,1,0:T(8,128)(2,1)S(1)}, u32[]{:S(2)}, u32[]{:S(2)}) collective-permute-start(bf16[1,32,2176]{2,1,0:T(8,128)(2,1)} %get-tuple-element.63), channel_id=1, source_target_pairs={{0,3},{1,2},{2,1},{3,0},{4,7},{5,6},{6,5},{7,4},{8,11},{9,10},{10,... | collective-permute-start | bytes 417800 | tf_op jit(solution)/shard_map/ppermute | solution.py:233
  8.8 2.7 %collective-permute-done.1.refs_1_ = bf16[1,32,2176]{2,1,0:T(8,128)(2,1)S(1)} collective-permute-done((bf16[1,32,2176]{2,1,0:T(8,128)(2,1)}, bf16[1,32,2176]{2,1,0:T(8,128)(2,1)S(1)}, u32[]{:S(2)}, u32[]{:S(2)}) %collective-permute-start.1) | collective-permute-done | bytes 139296 | tf_op jit(solution)/shard_map/ppermute | solution.py:233
  11.5 1.5 %collective-permute-start.10 = (bf16[2,32,2176]{2,1,0:T(8,128)(2,1)}, bf16[2,32,2176]{2,1,0:T(8,128)(2,1)S(1)}, u32[]{:S(2)}, u32[]{:S(2)}) collective-permute-start(bf16[2,32,2176]{2,1,0:T(8,128)(2,1)} %get-tuple-element.70), channel_id=1, source_target_pairs={{0,3},{1,2},{2,1},{3,0},{4,7},{5,6},{6,5},{7,4},{8,11},{9,10},{10,... | collective-permute-start | bytes 835592 | tf_op jit(solution)/shard_map/ppermute | solution.py:233
  13.0 2.5 %collective-permute-done.3.refs_3_ = bf16[1,32,2176]{2,1,0:T(8,128)(2,1)S(1)} collective-permute-done((bf16[1,32,2176]{2,1,0:T(8,128)(2,1)}, bf16[1,32,2176]{2,1,0:T(8,128)(2,1)S(1)}, u32[]{:S(2)}, u32[]{:S(2)}) %collective-permute-start.3) | collective-permute-done | bytes 139296 | tf_op jit(solution)/shard_map/ppermute | solution.py:233
  22.2 7.0 %collective-permute-done.refs_0_.refs_1_.refs_2_ = bf16[2,64,2048]{2,1,0:T(8,128)(2,1)S(1)} collective-permute-done((bf16[2,64,2048]{2,1,0:T(8,128)(2,1)}, bf16[2,64,2048]{2,1,0:T(8,128)(2,1)S(1)}, u32[]{:S(2)}, u32[]{:S(2)}) %collective-permute-start) | collective-permute-done | bytes 524320 | tf_op jit(solution)/shard_map/ppermute | solution.py:552
  30.4 1.6 %collective-permute-start.7 = (bf16[1,32,2176]{2,1,0:T(8,128)(2,1)S(1)}, bf16[1,32,2176]{2,1,0:T(8,128)(2,1)S(1)}, u32[]{:S(2)}, u32[]{:S(2)}) collective-permute-start(bf16[1,32,2176]{2,1,0:T(8,128)(2,1)S(1)} %shard_map.184.refs_7_), channel_id=1, source_target_pairs={{0,2},{1,3},{2,0},{3,1},{4,6},{5,7},{6,4},{7,5},{8,10},{9,11},{10,... | collective-permute-start | bytes 417800 | tf_op jit(solution)/shard_map/ppermute | solution.py:233
  33.4 1.5 %collective-permute-start.26 = (bf16[2,32,2176]{2,1,0:T(8,128)(2,1)S(1)}, bf16[2,32,2176]{2,1,0:T(8,128)(2,1)S(1)}, u32[]{:S(2)}, u32[]{:S(2)}) collective-permute-start(bf16[2,32,2176]{2,1,0:T(8,128)(2,1)S(1)} %get-tuple-element.84), channel_id=1, source_target_pairs={{0,2},{1,3},{2,0},{3,1},{4,6},{5,7},{6,4},{7,5},{8,10},{9,11},{10,... | collective-permute-start | bytes 835592 | tf_op jit(solution)/shard_map/ppermute | solution.py:233
  35.5 2.5 %shard_map.185 = (bf16[1,32,2176]{2,1,0:T(8,128)(2,1)S(1)}, bf16[1,32,2176]{2,1,0:T(8,128)(2,1)S(1)}, bf16[1,32,2176]{2,1,0:T(8,128)(2,1)S(1)}, bf16[1,32,2176]{...) custom-call(bf16[2,32,2176]{2,1,0:T(8,128)(2,1)S(1)} %copy-done.11, ...), custom_call_target="tpu_custom_call" | custom-call | flops 1069547520 | bytes 7901184 | tf_op jit(solution)/shard_map/pallas_call | solution.py:160
  38.1 4.4 %collective-permute-done.7.refs_5_ = bf16[1,32,2176]{2,1,0:T(8,128)(2,1)S(1)} collective-permute-done((bf16[1,32,2176]{2,1,0:T(8,128)(2,1)S(1)}, bf16[1,32,2176]{2,1,0:T(8,128)(2,1)S(1)}, u32[]{:S(2)}, u32[]{:S(2)}) %collective-permute-start.7) | collective-permute-done | bytes 139296 | tf_op jit(solution)/shard_map/ppermute | solution.py:233
  42.8 1.9 %collective-permute-start.11 = (bf16[64,2048]{1,0:T(8,128)(2,1)S(1)}, bf16[64,2048]{1,0:T(8,128)(2,1)S(1)}, u32[]{:S(2)}, u32[]{:S(2)}) collective-permute-start(bf16[64,2048]{1,0:T(8,128)(2,1)S(1)} %shard_map.186.refs_1_.refs_3_), channel_id=1, source_target_pairs={{0,4},{4,8},{8,12},{12,16},{16,20},{20,24},{24,28},{1,5},{5,9},{9,... | collective-permute-start | bytes 786440 | tf_op jit(solution)/shard_map/ppermute | solution.py:558
  44.8 2.0 %collective-permute-start.16 = (bf16[1,32,2176]{2,1,0:T(8,128)(2,1)S(1)}, bf16[1,32,2176]{2,1,0:T(8,128)(2,1)S(1)}, u32[]{:S(2)}, u32[]{:S(2)}) collective-permute-start(bf16[1,32,2176]{2,1,0:T(8,128)(2,1)S(1)} %get-tuple-element.75), channel_id=1, source_target_pairs={{0,1},{1,0},{2,3},{3,2},{4,5},{5,4},{6,7},{7,6},{8,9},{9,8},{10,11... | collective-permute-start | bytes 417800 | tf_op jit(solution)/shard_map/ppermute | solution.py:233
  49.3 2.5 %shard_map.193 = (bf16[1,32,2176]{2,1,0:T(8,128)(2,1)S(1)}, bf16[1,32,2176]{2,1,0:T(8,128)(2,1)S(1)}, bf16[1,32,2176]{2,1,0:T(8,128)(2,1)S(1)}, bf16[1,32,2176]{...) custom-call(bf16[2,32,2176]{2,1,0:T(8,128)(2,1)S(1)} %get-tuple-elem, ...), custom_call_target="tpu_custom_call" | custom-call | flops 1069547520 | bytes 7901184 | tf_op jit(solution)/shard_map/pallas_call | solution.py:160
  51.8 1.5 %collective-permute-start.28 = (bf16[1,32,2176]{2,1,0:T(8,128)(2,1)S(1)}, bf16[1,32,2176]{2,1,0:T(8,128)(2,1)S(1)}, u32[]{:S(2)}, u32[]{:S(2)}) collective-permute-start(bf16[1,32,2176]{2,1,0:T(8,128)(2,1)S(1)} %get-tuple-element.86), channel_id=1, source_target_pairs={{0,1},{1,0},{2,3},{3,2},{4,5},{5,4},{6,7},{7,6},{8,9},{9,8},{10,11... | collective-permute-start | bytes 417800 | tf_op jit(solution)/shard_map/ppermute | solution.py:233
  55.9 1.6 %collective-permute-start.14 = (bf16[2,32,2176]{2,1,0:T(8,128)(2,1)S(1)}, bf16[2,32,2176]{2,1,0:T(8,128)(2,1)S(1)}, u32[]{:S(2)}, u32[]{:S(2)}) collective-permute-start(bf16[2,32,2176]{2,1,0:T(8,128)(2,1)S(1)} %get-tuple-element.74), channel_id=1, source_target_pairs={{0,3},{1,2},{2,1},{3,0},{4,7},{5,6},{6,5},{7,4},{8,11},{9,10},{10,... | collective-permute-start | bytes 835592 | tf_op jit(solution)/shard_map/ppermute | solution.py:233
  58.9 12.0 %collective-permute-done.29.refs_5_ = bf16[1,32,2176]{2,1,0:T(8,128)(2,1)S(1)} collective-permute-done((bf16[1,32,2176]{2,1,0:T(8,128)(2,1)S(1)}, bf16[1,32,2176]{2,1,0:T(8,128)(2,1)S(1)}, u32[]{:S(2)}, u32[]{:S(2)}) %collective-permute-start.29) | collective-permute-done | bytes 139296 | tf_op jit(solution)/shard_map/ppermute | solution.py:233
  72.7 2.1 %collective-permute-start.31 = (bf16[64,2048]{1,0:T(8,128)(2,1)S(1)}, bf16[64,2048]{1,0:T(8,128)(2,1)S(1)}, u32[]{:S(2)}, u32[]{:S(2)}) collective-permute-start(bf16[64,2048]{1,0:T(8,128)(2,1)S(1)} %shard_map.194.refs_3_), channel_id=1, source_target_pairs={{4,0},{8,4},{12,8},{16,12},{20,16},{24,20},{28,24},{5,1},{9,5},{13... | collective-permute-start | bytes 786440 | tf_op jit(solution)/shard_map/ppermute | solution.py:558
  77.2 2.2 %collective-permute-start.24 = (bf16[1,32,2176]{2,1,0:T(8,128)(2,1)S(1)}, bf16[1,32,2176]{2,1,0:T(8,128)(2,1)S(1)}, u32[]{:S(2)}, u32[]{:S(2)}) collective-permute-start(bf16[1,32,2176]{2,1,0:T(8,128)(2,1)S(1)} %get-tuple-element.83), channel_id=1, source_target_pairs={{0,3},{1,2},{2,1},{3,0},{4,7},{5,6},{6,5},{7,4},{8,11},{9,10},{10,... | collective-permute-start | bytes 417800 | tf_op jit(solution)/shard_map/ppermute | solution.py:233
  79.4 1.4 %collective-permute-start.22 = (bf16[1,32,2176]{2,1,0:T(8,128)(2,1)S(1)}, bf16[1,32,2176]{2,1,0:T(8,128)(2,1)S(1)}, u32[]{:S(2)}, u32[]{:S(2)}) collective-permute-start(bf16[1,32,2176]{2,1,0:T(8,128)(2,1)S(1)} %get-tuple-element.78.refs_7_.refs_0_), channel_id=1, source_target_pairs={{0,1},{1,0},{2,3},{3,2},{4,5},{5,4},{6,7},{7,6},{8,9},{9,8},{10,11... | collective-permute-start | bytes 417800 | tf_op jit(solution)/shard_map/ppermute | solution.py:233
  83.1 2.8 %collective-permute-start.37 = (bf16[1,32,2176]{2,1,0:T(8,128)(2,1)S(1)}, bf16[1,32,2176]{2,1,0:T(8,128)(2,1)S(1)}, u32[]{:S(2)}, u32[]{:S(2)}) collective-permute-start(bf16[1,32,2176]{2,1,0:T(8,128)(2,1)S(1)} %get-tuple-element.94), channel_id=1, source_target_pairs={{0,3},{1,2},{2,1},{3,0},{4,7},{5,6},{6,5},{7,4},{8,11},{9,10},{10,... | collective-permute-start | bytes 417800 | tf_op jit(solution)/shard_map/ppermute | solution.py:233
  88.2 1.8 %collective-permute-start.20 = (bf16[1,32,2176]{2,1,0:T(8,128)(2,1)S(1)}, bf16[1,32,2176]{2,1,0:T(8,128)(2,1)S(1)}, u32[]{:S(2)}, u32[]{:S(2)}) collective-permute-start(bf16[1,32,2176]{2,1,0:T(8,128)(2,1)S(1)} %get-tuple-element.81), channel_id=1, source_target_pairs={{0,2},{1,3},{2,0},{3,1},{4,6},{5,7},{6,4},{7,5},{8,10},{9,11},{10,... | collective-permute-start | bytes 417800 | tf_op jit(solution)/shard_map/ppermute | solution.py:233
  97.8 2.5 %shard_map.197 = (bf16[1,32,2176]{2,1,0:T(8,128)(2,1)S(1)}, bf16[1,32,2176]{2,1,0:T(8,128)(2,1)S(1)}, bf16[1,32,2176]{2,1,0:T(8,128)(2,1)S(1)}, bf16[1,32,2176]{...) custom-call(bf16[2,32,2176]{2,1,0:T(8,128)(2,1)S(1)} %get-tuple-elem, ...), custom_call_target="tpu_custom_call" | custom-call | flops 1069547520 | bytes 8458240 | tf_op jit(solution)/shard_map/pallas_call | solution.py:160
  101.3 1.9 %collective-permute-start.39 = (bf16[1,32,2176]{2,1,0:T(8,128)(2,1)S(1)}, bf16[1,32,2176]{2,1,0:T(8,128)(2,1)S(1)}, u32[]{:S(2)}, u32[]{:S(2)}) collective-permute-start(bf16[1,32,2176]{2,1,0:T(8,128)(2,1)S(1)} %get-tuple-element.98), channel_id=1, source_target_pairs={{0,2},{1,3},{2,0},{3,1},{4,6},{5,7},{6,4},{7,5},{8,10},{9,11},{10,... | collective-permute-start | bytes 417800 | tf_op jit(solution)/shard_map/ppermute | solution.py:233
  107.6 4.3 %shard_map.200 = (bf16[2048,384]{1,0:T(8,128)(2,1)}, bf16[2048,384]{1,0:T(8,128)(2,1)}, bf16[384,2048]{1,0:T(8,128)(2,1)}) custom-call(bf16[144,2048]{1,0:T(8,128)(2,1)S(1)} %get-tuple-element.100.refs_0_, bf16[144,2048]{1,0:T(8,128)(2,1)S(1)} %get-tuple-element.101.refs_1_, bf16[144,2048]{1,0:T(8,128)(2,1)S(1)} %get-tuple-element.102.refs_2_, ...), custom_call_target="tpu_custom_call" | custom-call | flops 2038431744 | bytes 9252864 | tf_op jit(solution)/shard_map/pallas_call | solution.py:465
  (109 shorter events, 42.3 us)
Async XLA Ops:
  3.7 25.6 %collective-permute-start = (bf16[2,64,2048]{2,1,0:T(8,128)(2,1)}, bf16[2,64,2048]{2,1,0:T(8,128)(2,1)S(1)}, u32[]{:S(2)}, u32[]{:S(2)}) collective-permute-start(bf16[2,64,2048]{2,1,0:T(8,128)(2,1)} %get-tuple-element.61), channel_id=1, source_target_pairs={{0,28},{4,24},{8,20},{12,16},{16,12},{20,8},{24,4},{28,0},{1,29},{... | collective-permute-start | bytes 1572872 | tf_op jit(solution)/shard_map/ppermute | solution.py:552
  5.3 10.2 %collective-permute-start.3 = (bf16[1,32,2176]{2,1,0:T(8,128)(2,1)}, bf16[1,32,2176]{2,1,0:T(8,128)(2,1)S(1)}, u32[]{:S(2)}, u32[]{:S(2)}) collective-permute-start(bf16[1,32,2176]{2,1,0:T(8,128)(2,1)} %get-tuple-element.63), channel_id=1, source_target_pairs={{0,3},{1,2},{2,1},{3,0},{4,7},{5,6},{6,5},{7,4},{8,11},{9,10},{10,... | collective-permute-start | bytes 417800 | tf_op jit(solution)/shard_map/ppermute | solution.py:233
  8.2 23.7 %collective-permute-start.8 = (bf16[2,32,2176]{2,1,0:T(8,128)(2,1)}, bf16[2,32,2176]{2,1,0:T(8,128)(2,1)S(1)}, u32[]{:S(2)}, u32[]{:S(2)}) collective-permute-start(bf16[2,32,2176]{2,1,0:T(8,128)(2,1)} %get-tuple-element.69.refs_0_), channel_id=1, source_target_pairs={{0,1},{1,0},{2,3},{3,2},{4,5},{5,4},{6,7},{7,6},{8,9},{9,8},{10,11... | collective-permute-start | bytes 835592 | tf_op jit(solution)/shard_map/ppermute | solution.py:233
  11.5 21.9 %collective-permute-start.10 = (bf16[2,32,2176]{2,1,0:T(8,128)(2,1)}, bf16[2,32,2176]{2,1,0:T(8,128)(2,1)S(1)}, u32[]{:S(2)}, u32[]{:S(2)}) collective-permute-start(bf16[2,32,2176]{2,1,0:T(8,128)(2,1)} %get-tuple-element.70), channel_id=1, source_target_pairs={{0,3},{1,2},{2,1},{3,0},{4,7},{5,6},{6,5},{7,4},{8,11},{9,10},{10,... | collective-permute-start | bytes 835592 | tf_op jit(solution)/shard_map/ppermute | solution.py:233
  15.5 19.4 %collective-permute-start.9 = (bf16[2,32,2176]{2,1,0:T(8,128)(2,1)}, bf16[2,32,2176]{2,1,0:T(8,128)(2,1)S(1)}, u32[]{:S(2)}, u32[]{:S(2)}) collective-permute-start(bf16[2,32,2176]{2,1,0:T(8,128)(2,1)} %get-tuple-element.70), channel_id=1, source_target_pairs={{0,2},{1,3},{2,0},{3,1},{4,6},{5,7},{6,4},{7,5},{8,10},{9,11},{10,... | collective-permute-start | bytes 835592 | tf_op jit(solution)/shard_map/ppermute | solution.py:233
  30.4 12.1 %collective-permute-start.7 = (bf16[1,32,2176]{2,1,0:T(8,128)(2,1)S(1)}, bf16[1,32,2176]{2,1,0:T(8,128)(2,1)S(1)}, u32[]{:S(2)}, u32[]{:S(2)}) collective-permute-start(bf16[1,32,2176]{2,1,0:T(8,128)(2,1)S(1)} %shard_map.184.refs_7_), channel_id=1, source_target_pairs={{0,2},{1,3},{2,0},{3,1},{4,6},{5,7},{6,4},{7,5},{8,10},{9,11},{10,... | collective-permute-start | bytes 417800 | tf_op jit(solution)/shard_map/ppermute | solution.py:233
  32.0 12.8 %collective-permute-start.27 = (bf16[2,32,2176]{2,1,0:T(8,128)(2,1)S(1)}, bf16[2,32,2176]{2,1,0:T(8,128)(2,1)S(1)}, u32[]{:S(2)}, u32[]{:S(2)}) collective-permute-start(bf16[2,32,2176]{2,1,0:T(8,128)(2,1)S(1)} %get-tuple-element.84), channel_id=1, source_target_pairs={{0,3},{1,2},{2,1},{3,0},{4,7},{5,6},{6,5},{7,4},{8,11},{9,10},{10,... | collective-permute-start | bytes 835592 | tf_op jit(solution)/shard_map/ppermute | solution.py:233
  33.4 14.5 %collective-permute-start.26 = (bf16[2,32,2176]{2,1,0:T(8,128)(2,1)S(1)}, bf16[2,32,2176]{2,1,0:T(8,128)(2,1)S(1)}, u32[]{:S(2)}, u32[]{:S(2)}) collective-permute-start(bf16[2,32,2176]{2,1,0:T(8,128)(2,1)S(1)} %get-tuple-element.84), channel_id=1, source_target_pairs={{0,2},{1,3},{2,0},{3,1},{4,6},{5,7},{6,4},{7,5},{8,10},{9,11},{10,... | collective-permute-start | bytes 835592 | tf_op jit(solution)/shard_map/ppermute | solution.py:233
  34.9 14.4 %collective-permute-start.25 = (bf16[2,32,2176]{2,1,0:T(8,128)(2,1)S(1)}, bf16[2,32,2176]{2,1,0:T(8,128)(2,1)S(1)}, u32[]{:S(2)}, u32[]{:S(2)}) collective-permute-start(bf16[2,32,2176]{2,1,0:T(8,128)(2,1)S(1)} %get-tuple-element.65.refs_1_.refs_0_), channel_id=1, source_target_pairs={{0,1},{1,0},{2,3},{3,2},{4,5},{5,4},{6,7},{7,6},{8,9},{9,8},{10,11... | collective-permute-start | bytes 835592 | tf_op jit(solution)/shard_map/ppermute | solution.py:233
  38.0 15.4 %collective-permute-start.4 = (bf16[1,64,2048]{2,1,0:T(8,128)(2,1)S(1)}, bf16[1,64,2048]{2,1,0:T(8,128)(2,1)S(1)}, u32[]{:S(2)}, u32[]{:S(2)}) collective-permute-start(bf16[1,64,2048]{2,1,0:T(8,128)(2,1)S(1)} %shard_map.183.refs_2_), channel_id=1, source_target_pairs={{0,28},{4,24},{8,20},{12,16},{16,12},{20,8},{24,4},{28,0},{1,29},{... | collective-permute-start | bytes 786440 | tf_op jit(solution)/shard_map/ppermute | solution.py:552
  42.8 11.2 %collective-permute-start.11 = (bf16[64,2048]{1,0:T(8,128)(2,1)S(1)}, bf16[64,2048]{1,0:T(8,128)(2,1)S(1)}, u32[]{:S(2)}, u32[]{:S(2)}) collective-permute-start(bf16[64,2048]{1,0:T(8,128)(2,1)S(1)} %shard_map.186.refs_1_.refs_3_), channel_id=1, source_target_pairs={{0,4},{4,8},{8,12},{12,16},{16,20},{20,24},{24,28},{1,5},{5,9},{9,... | collective-permute-start | bytes 786440 | tf_op jit(solution)/shard_map/ppermute | solution.py:558
  44.8 11.1 %collective-permute-start.16 = (bf16[1,32,2176]{2,1,0:T(8,128)(2,1)S(1)}, bf16[1,32,2176]{2,1,0:T(8,128)(2,1)S(1)}, u32[]{:S(2)}, u32[]{:S(2)}) collective-permute-start(bf16[1,32,2176]{2,1,0:T(8,128)(2,1)S(1)} %get-tuple-element.75), channel_id=1, source_target_pairs={{0,1},{1,0},{2,3},{3,2},{4,5},{5,4},{6,7},{7,6},{8,9},{9,8},{10,11... | collective-permute-start | bytes 417800 | tf_op jit(solution)/shard_map/ppermute | solution.py:233
  53.4 17.5 %collective-permute-start.29 = (bf16[1,32,2176]{2,1,0:T(8,128)(2,1)S(1)}, bf16[1,32,2176]{2,1,0:T(8,128)(2,1)S(1)}, u32[]{:S(2)}, u32[]{:S(2)}) collective-permute-start(bf16[1,32,2176]{2,1,0:T(8,128)(2,1)S(1)} %get-tuple-element.87), channel_id=1, source_target_pairs={{0,2},{1,3},{2,0},{3,1},{4,6},{5,7},{6,4},{7,5},{8,10},{9,11},{10,... | collective-permute-start | bytes 417800 | tf_op jit(solution)/shard_map/ppermute | solution.py:233
  54.0 16.9 %collective-permute-start.30 = (bf16[1,32,2176]{2,1,0:T(8,128)(2,1)S(1)}, bf16[1,32,2176]{2,1,0:T(8,128)(2,1)S(1)}, u32[]{:S(2)}, u32[]{:S(2)}) collective-permute-start(bf16[1,32,2176]{2,1,0:T(8,128)(2,1)S(1)} %get-tuple-element.88), channel_id=1, source_target_pairs={{0,3},{1,2},{2,1},{3,0},{4,7},{5,6},{6,5},{7,4},{8,11},{9,10},{10,... | collective-permute-start | bytes 417800 | tf_op jit(solution)/shard_map/ppermute | solution.py:233
  55.9 23.5 %collective-permute-start.14 = (bf16[2,32,2176]{2,1,0:T(8,128)(2,1)S(1)}, bf16[2,32,2176]{2,1,0:T(8,128)(2,1)S(1)}, u32[]{:S(2)}, u32[]{:S(2)}) collective-permute-start(bf16[2,32,2176]{2,1,0:T(8,128)(2,1)S(1)} %get-tuple-element.74), channel_id=1, source_target_pairs={{0,3},{1,2},{2,1},{3,0},{4,7},{5,6},{6,5},{7,4},{8,11},{9,10},{10,... | collective-permute-start | bytes 835592 | tf_op jit(solution)/shard_map/ppermute | solution.py:233
  57.5 15.1 %collective-permute-start.18 = (bf16[1,32,2176]{2,1,0:T(8,128)(2,1)S(1)}, bf16[1,32,2176]{2,1,0:T(8,128)(2,1)S(1)}, u32[]{:S(2)}, u32[]{:S(2)}) collective-permute-start(bf16[1,32,2176]{2,1,0:T(8,128)(2,1)S(1)} %get-tuple-element.77), channel_id=1, source_target_pairs={{0,3},{1,2},{2,1},{3,0},{4,7},{5,6},{6,5},{7,4},{8,11},{9,10},{10,... | collective-permute-start | bytes 417800 | tf_op jit(solution)/shard_map/ppermute | solution.py:233
  58.9 17.0 %collective-permute-start.15 = (bf16[1,64,2048]{2,1,0:T(8,128)(2,1)S(1)}, bf16[1,64,2048]{2,1,0:T(8,128)(2,1)S(1)}, u32[]{:S(2)}, u32[]{:S(2)}) collective-permute-start(bf16[1,64,2048]{2,1,0:T(8,128)(2,1)S(1)} %shard_map.187.refs_5_), channel_id=1, source_target_pairs={{0,28},{4,24},{8,20},{12,16},{16,12},{20,8},{24,4},{28,0},{1,29},{... | collective-permute-start | bytes 786440 | tf_op jit(solution)/shard_map/ppermute | solution.py:552
  83.1 10.5 %collective-permute-start.37 = (bf16[1,32,2176]{2,1,0:T(8,128)(2,1)S(1)}, bf16[1,32,2176]{2,1,0:T(8,128)(2,1)S(1)}, u32[]{:S(2)}, u32[]{:S(2)}) collective-permute-start(bf16[1,32,2176]{2,1,0:T(8,128)(2,1)S(1)} %get-tuple-element.94), channel_id=1, source_target_pairs={{0,3},{1,2},{2,1},{3,0},{4,7},{5,6},{6,5},{7,4},{8,11},{9,10},{10,... | collective-permute-start | bytes 417800 | tf_op jit(solution)/shard_map/ppermute | solution.py:233
  88.2 12.8 %collective-permute-start.20 = (bf16[1,32,2176]{2,1,0:T(8,128)(2,1)S(1)}, bf16[1,32,2176]{2,1,0:T(8,128)(2,1)S(1)}, u32[]{:S(2)}, u32[]{:S(2)}) collective-permute-start(bf16[1,32,2176]{2,1,0:T(8,128)(2,1)S(1)} %get-tuple-element.81), channel_id=1, source_target_pairs={{0,2},{1,3},{2,0},{3,1},{4,6},{5,7},{6,4},{7,5},{8,10},{9,11},{10,... | collective-permute-start | bytes 417800 | tf_op jit(solution)/shard_map/ppermute | solution.py:233
  91.2 10.2 %collective-permute-start.21 = (bf16[1,32,2176]{2,1,0:T(8,128)(2,1)S(1)}, bf16[1,32,2176]{2,1,0:T(8,128)(2,1)S(1)}, u32[]{:S(2)}, u32[]{:S(2)}) collective-permute-start(bf16[1,32,2176]{2,1,0:T(8,128)(2,1)S(1)} %get-tuple-element.82), channel_id=1, source_target_pairs={{0,3},{1,2},{2,1},{3,0},{4,7},{5,6},{6,5},{7,4},{8,11},{9,10},{10,... | collective-permute-start | bytes 417800 | tf_op jit(solution)/shard_map/ppermute | solution.py:233
  93.6 10.8 %collective-permute-start.32 = (bf16[1,32,2176]{2,1,0:T(8,128)(2,1)S(1)}, bf16[1,32,2176]{2,1,0:T(8,128)(2,1)S(1)}, u32[]{:S(2)}, u32[]{:S(2)}) collective-permute-start(bf16[1,32,2176]{2,1,0:T(8,128)(2,1)S(1)} %get-tuple-element.91), channel_id=1, source_target_pairs={{0,1},{1,0},{2,3},{3,2},{4,5},{5,4},{6,7},{7,6},{8,9},{9,8},{10,11... | collective-permute-start | bytes 417800 | tf_op jit(solution)/shard_map/ppermute | solution.py:233
  95.0 11.6 %collective-permute-start.33 = (bf16[1,32,2176]{2,1,0:T(8,128)(2,1)S(1)}, bf16[1,32,2176]{2,1,0:T(8,128)(2,1)S(1)}, u32[]{:S(2)}, u32[]{:S(2)}) collective-permute-start(bf16[1,32,2176]{2,1,0:T(8,128)(2,1)S(1)} %get-tuple-element.92), channel_id=1, source_target_pairs={{0,2},{1,3},{2,0},{3,1},{4,6},{5,7},{6,4},{7,5},{8,10},{9,11},{10,... | collective-permute-start | bytes 417800 | tf_op jit(solution)/shard_map/ppermute | solution.py:233
  100.9 11.0 %collective-permute-start.38 = (bf16[1,32,2176]{2,1,0:T(8,128)(2,1)S(1)}, bf16[1,32,2176]{2,1,0:T(8,128)(2,1)S(1)}, u32[]{:S(2)}, u32[]{:S(2)}) collective-permute-start(bf16[1,32,2176]{2,1,0:T(8,128)(2,1)S(1)} %get-tuple-element.97), channel_id=1, source_target_pairs={{0,1},{1,0},{2,3},{3,2},{4,5},{5,4},{6,7},{7,6},{8,9},{9,8},{10,11... | collective-permute-start | bytes 417800 | tf_op jit(solution)/shard_map/ppermute | solution.py:233
  101.3 10.6 %collective-permute-start.39 = (bf16[1,32,2176]{2,1,0:T(8,128)(2,1)S(1)}, bf16[1,32,2176]{2,1,0:T(8,128)(2,1)S(1)}, u32[]{:S(2)}, u32[]{:S(2)}) collective-permute-start(bf16[1,32,2176]{2,1,0:T(8,128)(2,1)S(1)} %get-tuple-element.98), channel_id=1, source_target_pairs={{0,2},{1,3},{2,0},{3,1},{4,6},{5,7},{6,4},{7,5},{8,10},{9,11},{10,... | collective-permute-start | bytes 417800 | tf_op jit(solution)/shard_map/ppermute | solution.py:233
  (32 other events, 265.9 us)
